TPU v7x, 32 devices: a whole 2x2x4 slice. The times are simulated.
32 devices in a mesh: dp: 2 (over core), fsdp: 16 (over z, y, x).
Axes of the slice: x: 2, y: 2, z: 4, core: 2. Of those that a mesh axis runs over, the one named last changes fastest.
Arguments:
- tokens: bfloat16 [65536, 768], P(('dp', 'fsdp')), may hold values from -6 to 6
- sensor_tag: int32 [64], P(('dp', 'fsdp')), may hold values from 0 to 1
- owner_order: int32 [32, 2048], P(('dp', 'fsdp')), may hold values from 0 to 2047, each once within a row
- ln1_gain: bfloat16 [768], P('fsdp'), may hold values from 0.25 to 1.75
- ln1_bias: bfloat16 [768], P('fsdp'), may hold values from -3 to 3
- w_qkv: bfloat16 [768, 2304], P('fsdp'), may hold values from -0.21875 to 0.21875
- b_query: bfloat16 [768], P('fsdp'), may hold values from -4 to 4
- b_value: bfloat16 [768], P('fsdp'), may hold values from -4 to 4
- w_out: bfloat16 [768, 768], P('fsdp'), may hold values from -0.625 to 0.625
- b_out: bfloat16 [768], P('fsdp'), may hold values from -3 to 3
- ln2_gain: bfloat16 [768], P('fsdp'), may hold values from 0.25 to 1.75
- ln2_bias: bfloat16 [768], P('fsdp'), may hold values from -3 to 3
- w_up: bfloat16 [768, 3072], P('fsdp'), may hold values from -0.21875 to 0.21875
- b_up: bfloat16 [3072], P('fsdp'), may hold values from -4 to 4
- w_down: bfloat16 [3072, 768], P('fsdp'), may hold values from -0.109375 to 0.109375
- b_down: bfloat16 [768], P('fsdp'), may hold values from -3 to 3
- out_grad: float32 [65536, 768], P(('dp', 'fsdp')), may hold values from -6 to 6
Outputs:
- encoded: float32 [65536, 768], P(('dp', 'fsdp'))
- tokens_grad: float32 [65536, 768], P(('dp', 'fsdp'))
- grad_ln1_gain: float32 [768], P('fsdp')
- grad_ln1_bias: float32 [768], P('fsdp')
- grad_w_qkv: float32 [768, 2304], P('fsdp')
- grad_b_query: float32 [768], P('fsdp')
- grad_b_value: float32 [768], P('fsdp')
- grad_w_out: float32 [768, 768], P('fsdp')
- grad_b_out: float32 [768], P('fsdp')
- grad_ln2_gain: float32 [768], P('fsdp')
- grad_ln2_bias: float32 [768], P('fsdp')
- grad_w_up: float32 [768, 3072], P('fsdp')
- grad_b_up: float32 [3072], P('fsdp')
- grad_w_down: float32 [3072, 768], P('fsdp')
- grad_b_down: float32 [768], P('fsdp')
Inputs may be any that keep to these rules, and one draw needn't show every extreme that they name: `sensor_tag`: 0 marks a row holding one chip of 1024 tokens, 1 a row of four chips of 256 tokens. `owner_order`: each row is a permutation of 0 to 2047.
All inputs are finite; a program needn't handle non-finite values.
Results may differ from a plain program's by a relative error of at most 0.025.
Values may be sent and summed in bfloat16 or wider, within the bound.
No kernel may reach another device: no remote copies, remote signals or barrier semaphores. Data moves between devices by JAX's collectives and lax.ppermute only.
A program may use at most 320 MiB of HBM per device.

v0:
```python
import functools
import math

import jax
import jax.numpy as jnp
from jax import lax
from jax.experimental import pallas as pl
from jax.experimental.pallas import tpu as pltpu
from jax.sharding import PartitionSpec as P

F32 = jnp.float32
BF = jnp.bfloat16
EPS = 1e-6
LOG2E = math.log2(math.e)
LN2 = math.log(2.0)
NT = (((1,), (1,)), ((), ()))
TN = (((0,), (0,)), ((), ()))
NN = (((1,), (0,)), ((), ()))
ANY = pl.BlockSpec(memory_space=pl.ANY)
VECS = 16
SDS = jax.ShapeDtypeStruct


def dg(a, b, dims):
    return lax.dot_general(a, b, dims, preferred_element_type=F32)


def params(axes=1):
    return pltpu.CompilerParams(
        vmem_limit_bytes=58 * 2**20, dimension_semantics=("arbitrary",) * axes
    )


def cost(flops, nbytes, trans=0):
    return pl.CostEstimate(flops=int(flops) >> 10, bytes_accessed=int(nbytes) >> 10, transcendentals=int(trans) >> 10)


def rows_of(height, width):
    return pl.BlockSpec((height, width), lambda i, *_: (i, 0))


def whole(shape):
    zeros = (0,) * len(shape)
    return pl.BlockSpec(shape, lambda *_: zeros, pipeline_mode=pl.Buffered(1))


def fixed(shape):
    zeros = (0,) * len(shape)
    return pl.BlockSpec(shape, lambda *_: zeros)


def norm_stats(x):
    n = x.shape[-1]
    c = x - jnp.sum(x, axis=-1, keepdims=True) * (1.0 / n)
    var = jnp.sum(c * c, axis=-1, keepdims=True) * (1.0 / n)
    return c, lax.rsqrt(var + EPS)


def after(x, *deps):
    return lax.optimization_barrier((x,) + deps)[0]


def xor_pp(x, b, n):
    return lax.ppermute(x, "fsdp", [(i, i ^ b) for i in range(n)])


def core_swap(x, m):
    return lax.ppermute(x, "dp", [(i, i ^ 1) for i in range(m)])


def gather_near(x, n):
    q = n // 4
    return jnp.stack([x] + [xor_pp(x, d * q, n) for d in (1, 2, 3)])


def tops(n):
    q = n // 4
    return [[low + z * q for z in range(4)] for low in range(q)]


def gather_far(s, n):
    return [s] + [xor_pp(s, e, n) for e in range(1, n // 4)]


def fits(rows, n):
    return rows % 16 == 0 and n == 16


def settle(pieces, order, c, n, wide=None):
    q = n // 4
    rows, width = pieces[0].shape[1:]
    if fits(rows, n):
        return pieces
    height = n * rows // 16
    halves = []
    for side in (pieces[:q], pieces[q:]):
        rel = jnp.stack(side, axis=1).reshape((n, rows, width))
        whole_side = jnp.take(rel, order, axis=0)
        flat = whole_side.reshape(16, height, width)
        if wide is not None:
            cut = width * (wide + 1) // (2 * wide + 1)
            low = whole_side[..., cut:].reshape(n, rows, wide, -1).transpose(0, 2, 1, 3)
            low = low.reshape(16, wide, height, -1).transpose(0, 2, 1, 3).reshape(16, height, -1)
            flat = jnp.concatenate([flat[..., :cut], low], axis=2)
        halves.append(flat.reshape(4, 4, height, width))
    left, right = jnp.where(c == 0, halves[0], halves[1]), jnp.where(c == 0, halves[1], halves[0])
    return [side[:, e] for side in (left, right) for e in range(4)]


def load_pieces(idx_ref, plan, sem):
    c = idx_ref[1]
    started = []
    for find, shard, start, skip, width, dst, height, first in plan:
        for e in range(4):
            for d in range(4):
                for block, h in zip(find(e, d), (c, 1 - c), strict=False):
                    rows = block.shape[0]
                    at = pl.ds(pl.multiple_of(shard(e, d) * height + first, 16), rows)
                    cols = pl.ds(pl.multiple_of(h * width, 128), width) if dst.shape[1] > width else slice(None)
                    src = block.at[:, pl.ds(start if e else start + skip, width)]
                    started.append(pltpu.make_async_copy(src, dst.at[at, cols], sem))
    for cp in started:
        cp.start()
    return started


def relative(idx_ref):
    return lambda e, d: lax.bitwise_xor(idx_ref[0], jnp.int32(d * 4 + e))


def by_top(idx_ref):
    return lambda e, d: lax.bitwise_xor(idx_ref[0] % 4, jnp.int32(e)) + d * 4


def load_qkv(idx_ref, pieces, w_ref, sem, vec_ref=None):
    def find(e, d):
        if len(pieces) == 8:
            return pieces[e].at[d], pieces[4 + e].at[d]
        return pieces[e].at[d], pieces[5].at[e - 1, d] if e else pieces[4].at[d]

    where = relative(idx_ref)
    rows, half = pieces[0].shape[1], w_ref.shape[1] // 2
    if vec_ref is not None:
        return load_pieces(idx_ref, [(lambda e, d: find(e, d)[:1], where, half, 0, 128, vec_ref, rows, 0)], sem)
    return load_pieces(idx_ref, [(find, where, 0, 0, half, w_ref, rows, 0)], sem)


def load_mlp(idx_ref, pieces, w1_ref, w2_ref, sem):
    where = by_top(idx_ref)

    def find1(e, d):
        return pieces[2 * e].at[d], pieces[2 * e + 1].at[d]

    def find2(e, d):
        at = 6 + 2 * e if e else 0
        return pieces[at].at[d], pieces[at + 1].at[d]

    rows = pieces[0].shape[1]
    half = w1_ref.shape[1] // 2
    w = w2_ref.shape[1] // 2
    one = [(find1, where, 0, 0, half, w1_ref, rows, 0)]
    two = [(find2, where, j * w, half, w, w2_ref, 4 * rows, j * rows) for j in range(4)]
    return load_pieces(idx_ref, one, sem.at[0]), load_pieces(idx_ref, two, sem.at[1])


def wait_mlp(w_ref, sem):
    pltpu.make_async_copy(w_ref, w_ref, sem).wait()


def qkv_kernel(idx_ref, x_ref, *refs):
    pieces = refs[:-9]
    q_ref, k_ref, v_ref, h_ref, vt_ref, bu_ref, w_ref, vec_ref, sem = refs[-9:]
    d = x_ref.shape[1]

    @pl.when(pl.program_id(0) == 0)
    def _():
        rows = pieces[0].shape[1]
        vecs = load_qkv(idx_ref, pieces, w_ref, sem.at[1], vec_ref)
        going = load_qkv(idx_ref, pieces, w_ref, sem.at[0])
        for cp in vecs:
            cp.wait()
        table = vec_ref[...].astype(F32).T[:VECS]
        vt_ref[...] = table
        bu_ref[...] = jnp.concatenate(
            [table[8 + j : 9 + j, s * rows : (s + 1) * rows] for s in range(d // rows) for j in range(4)], axis=1
        )
        for cp in going:
            cp.wait()

    c, r = norm_stats(x_ref[...].astype(F32))
    h = (c * r * vt_ref[0:1, :] + vt_ref[1:2, :]).astype(BF)
    h_ref[...] = h
    q = dg(h, w_ref[:, :d], NN)
    q_ref[...] = ((q + vt_ref[2:3, :]) * (0.125 * LOG2E)).astype(BF)
    k_ref[...] = dg(h, w_ref[:, d : 2 * d], NN).astype(BF)
    v_ref[...] = (dg(h, w_ref[:, 2 * d :], NN) + vt_ref[3:4, :]).astype(BF)


def qkv(idx, x, pieces, tb=512):
    t, d = x.shape
    return pl.pallas_call(
        qkv_kernel,
        grid_spec=pltpu.PrefetchScalarGridSpec(
            num_scalar_prefetch=1,
            grid=(t // tb,),
            in_specs=[rows_of(tb, d)] + [ANY] * len(pieces),
            out_specs=[rows_of(tb, d)] * 4 + [fixed((VECS, d)), fixed((1, 4 * d))],
            scratch_shapes=[
                pltpu.VMEM((d, 3 * d), BF),
                pltpu.VMEM((d, 128), BF),
                pltpu.SemaphoreType.DMA((2,)),
            ],
        ),
        out_shape=[SDS((t, d), BF)] * 4 + [SDS((VECS, d), F32), SDS((1, 4 * d), F32)],
        compiler_params=params(),
        cost_estimate=cost(6 * t * d * d, t * d * 8 + d * d * 6),
        name="qkv",
    )(idx, x, *pieces)


def attend_kernel(tag_ref, q_ref, k_ref, v_ref, *refs, qb):
    o_ref, l_ref = refs[-2:]
    r = pl.program_id(0)
    length = q_ref.shape[0]
    low = lax.broadcasted_iota(jnp.int32, (1, 128), 1) < 64

    def block(qs, qn, ks, kn):
        q = q_ref[pl.ds(qs, qn), :]
        k = k_ref[pl.ds(ks, kn), :]
        v = v_ref[pl.ds(ks, kn), :]
        outs = []
        for h in range(2):
            sel = low if h == 0 else jnp.logical_not(low)
            qm = jnp.where(sel, q, jnp.asarray(0, BF))
            vm = jnp.where(sel, v, jnp.asarray(1, BF))
            s = dg(qm, k, NT)
            m = jnp.max(s, axis=1, keepdims=True)
            outs.append((dg(jnp.exp2(s - m).astype(BF), vm, NN), m))
        (a, ma), (b, mb) = outs
        acc = jnp.where(low, a, b)
        total = pltpu.roll(jnp.where(low, b, a), 64, 1)
        o_ref[pl.ds(qs, qn), :] = (acc / total).astype(o_ref.dtype)
        lse = (jnp.where(low, ma, mb) + jnp.log2(total)).T
        l_ref[0, 0, 0:1, pl.ds(qs, qn)] = lse[0:1]
        l_ref[0, 0, 1:2, pl.ds(qs, qn)] = lse[64:65]

    @pl.when(tag_ref[r] == 0)
    def _():
        for i in range(length // qb):
            block(i * qb, qb, 0, length)

    @pl.when(tag_ref[r] != 0)
    def _():
        c = length // 4
        for i in range(4):
            block(i * c, c, i * c, c)


def attend(tag, q, k, v, first, pairs, before=(), qb=512):
    t, d = q.shape
    rows = tag.shape[0]
    length = t // rows
    blk = pl.BlockSpec((length, 128), lambda r, p, _: (r, p + first))
    lse = pl.BlockSpec((1, 1, 2, length), lambda r, p, _: (r, p + first, 0, 0))
    return pl.pallas_call(
        functools.partial(attend_kernel, qb=qb),
        grid_spec=pltpu.PrefetchScalarGridSpec(
            num_scalar_prefetch=1,
            grid=(rows, pairs),
            in_specs=[blk] * 3 + [ANY] * len(before),
            out_specs=[blk, lse],
        ),
        out_shape=[SDS((t, d), BF), SDS((rows, d // 128, 2, length), F32)],
        input_output_aliases={4: 0, 5: 1} if before else {},
        compiler_params=params(2),
        cost_estimate=cost(2048 * t * length * pairs, t * d * 8, t * length * 12),
        name="attend",
    )(tag, q, k, v, *before)


ODDS = (2.3021649, 1.05007451e-1, -2.545477e-4, -1.0560537e-4, 4.093017e-6)


def gelu_both(u):
    z = u * u
    odds = ODDS[3] + z * ODDS[4]
    odds = ODDS[2] + z * odds
    odds = ODDS[1] + z * odds
    odds = ODDS[0] + z * odds
    phi = pltpu.reciprocal(1.0 + jnp.exp2(-u * odds), approx=True)
    density = jnp.exp2(z * (-0.5 * LOG2E) - 0.5 * math.log2(2.0 * math.pi))
    return u * phi, phi + u * density


def mlp_kernel(idx_ref, x_ref, o_ref, vt_ref, bu_ref, *refs, fc):
    pieces = refs[:14]
    x2_ref, gl_ref, gp_ref, y_ref, w1_ref, w2_ref, sem = refs[14:]
    d = x_ref.shape[1]
    ff = w2_ref.shape[0]

    @pl.when(pl.program_id(0) == 0)
    def _():
        going, _ = load_mlp(idx_ref, pieces, w1_ref, w2_ref, sem)
        for cp in going:
            cp.wait()

    x2 = x_ref[...].astype(F32) + dg(o_ref[...], w1_ref[:, :d], NN) + vt_ref[4:5, :]
    x2_ref[...] = x2
    c, r = norm_stats(x2)
    h = (c * r * vt_ref[5:6, :] + vt_ref[6:7, :]).astype(BF)
    y = x2 + vt_ref[7:8, :]

    @pl.when(pl.program_id(0) == 0)
    def _():
        wait_mlp(w2_ref, sem.at[1])

    for f in range(0, ff, fc):
        u = dg(h, w1_ref[:, d + f : d + f + fc], NN) + bu_ref[:, f : f + fc]
        g, gp = gelu_both(u)
        g = g.astype(BF)
        gl_ref[:, f : f + fc] = g
        gp_ref[:, f : f + fc] = gp.astype(BF)
        y = y + dg(g, w2_ref[f : f + fc, :], NN)
    y_ref[...] = y.astype(BF)


def mlp(idx, x, o, vt, bu, pieces, tb=256, fc=768):
    t, d = x.shape
    ff = bu.shape[1]
    return pl.pallas_call(
        functools.partial(mlp_kernel, fc=fc),
        grid_spec=pltpu.PrefetchScalarGridSpec(
            num_scalar_prefetch=1,
            grid=(t // tb,),
            in_specs=[rows_of(tb, d)] * 2 + [whole(vt.shape), whole(bu.shape)] + [ANY] * 14,
            out_specs=[rows_of(tb, d), rows_of(tb, ff), rows_of(tb, ff), rows_of(tb, d)],
            scratch_shapes=[
                pltpu.VMEM((d, d + ff), BF),
                pltpu.VMEM((ff, d), BF),
                pltpu.SemaphoreType.DMA((2,)),
            ],
        ),
        out_shape=[SDS((t, d), F32), SDS((t, ff), BF), SDS((t, ff), BF), SDS((t, d), BF)],
        compiler_params=params(),
        cost_estimate=cost(4 * t * d * (d + 2 * ff), t * (10 * d + 4 * ff) + 4 * d * ff, 2 * t * ff),
        name="mlp",
    )(idx, x, o, vt, bu, *pieces)


def permute_kernel(ord_ref, y_ref, o_ref):
    jb = o_ref.shape[0]
    t = y_ref.shape[0]
    order = jnp.broadcast_to(ord_ref[...].astype(F32), (8, jb)).T[:, 0:1]
    hot = jnp.where(order == lax.broadcasted_iota(jnp.int32, (jb, t), 1).astype(F32), 1.0, 0.0)
    o_ref[...] = dg(hot.astype(BF), y_ref[...], NN).astype(BF)


def permute(order, y, jb=512):
    t, d = y.shape
    return pl.pallas_call(
        permute_kernel,
        grid=(t // jb,),
        in_specs=[pl.BlockSpec((1, jb), lambda i: (0, i)), whole((t, d))],
        out_specs=rows_of(jb, d),
        out_shape=pltpu.HBM((t, d), BF),
        compiler_params=params(),
        cost_estimate=cost(2 * t * t * d, t * d * 4),
        name="permute",
    )(order, y)


def split_halves(c, r, mine_ref, theirs_ref):
    h = r.shape[1] // 2
    left, right = r[:, :h], r[:, h:]
    mine_ref[...] = jnp.where(c == 0, left, right)
    theirs_ref[...] = jnp.where(c == 0, right, left)


def mlp_back_kernel(idx_ref, ord_ref, ret_ref, gp_ref, x2_ref, o_ref, vt_ref, *refs, fc):
    pieces = refs[:14]
    (dm_ref, du_ref, dx2_ref, do_ref, h2_ref, sums_ref, gbu_ref, mine_ref, theirs_ref) = refs[14:23]
    w1_ref, w2_ref, acc_ref, sem = refs[23:]
    i = pl.program_id(0)
    tb, ff = gp_ref.shape
    t, d = ret_ref.shape

    @pl.when(i == 0)
    def _():
        load_mlp(idx_ref, pieces, w1_ref, w2_ref, sem)
        sums_ref[...] = jnp.zeros_like(sums_ref)
        gbu_ref[...] = jnp.zeros_like(gbu_ref)
        acc_ref[...] = jnp.zeros_like(acc_ref)
        wait_mlp(w2_ref, sem.at[1])
        wait_mlp(w1_ref, sem.at[0])

    at = lax.broadcasted_iota(jnp.int32, (tb, t), 0) + i * tb
    hot = jnp.where(ord_ref[...] == at, 1.0, 0.0).astype(BF)
    dy = dg(hot, ret_ref[...], NN)
    dm = dy.astype(BF)
    dm_ref[...] = dm
    sums_ref[0:1, :] += jnp.sum(dy, axis=0, keepdims=True)
    dh = jnp.zeros((tb, d), F32)
    ahead = dg(dm, w2_ref[:fc, :], NT)
    for f in range(0, ff, fc):
        du = ahead * gp_ref[:, f : f + fc].astype(F32)
        if f + fc < ff:
            ahead = dg(dm, w2_ref[f + fc : f + 2 * fc, :], NT)
        gbu_ref[:, f : f + fc] += jnp.sum(du, axis=0, keepdims=True)
        du = du.astype(BF)
        du_ref[:, f : f + fc] = du
        dh = dh + dg(du, w1_ref[:, d + f : d + f + fc], NT)
    c, r = norm_stats(x2_ref[...])
    xh = c * r
    gain = vt_ref[5:6, :]
    h2_ref[...] = (xh * gain + vt_ref[6:7, :]).astype(BF)
    sums_ref[1:2, :] += jnp.sum(dh * xh, axis=0, keepdims=True)
    sums_ref[2:3, :] += jnp.sum(dh, axis=0, keepdims=True)
    dz = dh * gain
    m1 = jnp.sum(dz, axis=-1, keepdims=True) * (1.0 / d)
    m2 = jnp.sum(dz * xh, axis=-1, keepdims=True) * (1.0 / d)
    dx2 = dy + r * (dz - m1 - xh * m2)
    dx2_ref[...] = dx2
    da = dx2.astype(BF)
    sums_ref[3:4, :] += jnp.sum(da.astype(F32), axis=0, keepdims=True)
    do_ref[...] = dg(da, w1_ref[:, :d], NT).astype(BF)
    acc_ref[...] += dg(o_ref[...], da, TN)

    @pl.when(i == pl.num_programs(0) - 1)
    def _():
        split_halves(idx_ref[1], acc_ref[...].astype(BF), mine_ref, theirs_ref)


def mlp_back(idx, order_row, ret, gp, x2, o, vt, pieces, tb=256, fc=768):
    t, d = x2.shape
    ff = gp.shape[1]
    return pl.pallas_call(
        functools.partial(mlp_back_kernel, fc=fc),
        grid_spec=pltpu.PrefetchScalarGridSpec(
            num_scalar_prefetch=1,
            grid=(t // tb,),
            in_specs=[whole((1, t)), whole((t, d)), rows_of(tb, ff), rows_of(tb, d), rows_of(tb, d), whole(vt.shape)]
            + [ANY] * 14,
            out_specs=[rows_of(tb, d), rows_of(tb, ff)]
            + [rows_of(tb, d)] * 3
            + [fixed((8, d)), fixed((1, ff))]
            + [fixed((d, d // 2))] * 2,
            scratch_shapes=[
                pltpu.VMEM((d, d + ff), BF),
                pltpu.VMEM((ff, d), BF),
                pltpu.VMEM((d, d), F32),
                pltpu.SemaphoreType.DMA((2,)),
            ],
        ),
        out_shape=[
            SDS((t, d), BF),
            SDS((t, ff), BF),
            SDS((t, d), F32),
            SDS((t, d), BF),
            SDS((t, d), BF),
            SDS((8, d), F32),
            SDS((1, ff), F32),
            pltpu.HBM((d, d // 2), BF),
            pltpu.HBM((d, d // 2), BF),
        ],
        compiler_params=params(),
        cost_estimate=cost(2 * t * d * (d + 2 * ff + t) * 1.5, t * (20 * d + 4 * ff)),
        name="mlp_back",
    )(idx, order_row, ret, gp, x2, o, vt, *pieces)


def grad_mlp_kernel(
    idx_ref, g_ref, dm_ref, h2_any, du_ref, down_own, down_other, up_own, up_other, h2_ref, sem
):
    i = pl.program_id(0)
    steps = pl.num_programs(0) // 2

    @pl.when(i == 0)
    def _():
        pltpu.make_async_copy(h2_any, h2_ref, sem).start()

    @pl.when(i == steps)
    def _():
        pltpu.make_async_copy(h2_any, h2_ref, sem).wait()

    @pl.when(i < steps)
    def _():
        split_halves(idx_ref[1], dg(g_ref[...], dm_ref[...], TN).astype(BF), down_own, down_other)

    @pl.when(i >= steps)
    def _():
        split_halves(idx_ref[1], dg(h2_ref[...], du_ref[...], TN).astype(BF), up_own, up_other)


def grad_mlp(idx, g, dm, h2, du):
    t, ff = g.shape
    d = dm.shape[1]
    steps = ff // d

    def down(i):
        return jnp.minimum(i, steps - 1)

    def up(i):
        return jnp.maximum(i - steps, 0)

    return pl.pallas_call(
        grad_mlp_kernel,
        grid_spec=pltpu.PrefetchScalarGridSpec(
            num_scalar_prefetch=1,
            grid=(2 * steps,),
            in_specs=[
                pl.BlockSpec((t, d), lambda i, _: (0, down(i))),
                whole((t, d)),
                ANY,
                pl.BlockSpec((t, d), lambda i, _: (0, up(i))),
            ],
            out_specs=[pl.BlockSpec((d, d // 2), lambda i, _: (down(i), 0))] * 2
            + [pl.BlockSpec((d, d // 2), lambda i, _: (0, up(i)))] * 2,
            scratch_shapes=[pltpu.VMEM((t, d), BF), pltpu.SemaphoreType.DMA],
        ),
        out_shape=[pltpu.HBM((ff, d // 2), BF)] * 2 + [pltpu.HBM((d, ff // 2), BF)] * 2,
        compiler_params=params(),
        cost_estimate=cost(6 * t * ff * d, 4 * t * (ff + d) + 4 * ff * d),
        name="grad_mlp",
    )(idx, g, dm, h2, du)


def attend_back_kernel(
    tag_ref, q_ref, k_ref, v_ref, do_ref, o_ref, l_ref, *refs, kb, qb
):
    dq_ref, dk_ref, dv_ref, dl_ref, dqt_ref = refs[-5:]
    r = pl.program_id(0)
    length = q_ref.shape[0]
    low = lax.broadcasted_iota(jnp.int32, (1, 128), 1) < 64
    prod = (do_ref[...].astype(F32) * o_ref[...].astype(F32)).T
    dl_ref[0:1, :] = jnp.sum(prod[0:64], axis=0, keepdims=True)
    dl_ref[1:2, :] = jnp.sum(prod[64:128], axis=0, keepdims=True)

    def block(ks, kn, qs, qn):
        k = k_ref[pl.ds(ks, kn), :]
        v = v_ref[pl.ds(ks, kn), :]
        q = q_ref[pl.ds(qs, qn), :]
        do = do_ref[pl.ds(qs, qn), :]
        dks = []
        dvs = []
        dqs = []
        for h in range(2):
            sel = low if h == 0 else jnp.logical_not(low)
            km = jnp.where(sel, k, jnp.asarray(0, BF))
            vm = jnp.where(sel, v, jnp.asarray(0, BF))
            pt = jnp.exp2(dg(km, q, NT) - l_ref[0, 0, h : h + 1, pl.ds(qs, qn)])
            dst = (pt * (dg(vm, do, NT) - dl_ref[h : h + 1, pl.ds(qs, qn)])).astype(BF)
            dvs.append(dg(pt.astype(BF), do, NN))
            dks.append(dg(dst, q, NN))
            dqs.append(dg(km.T, dst, NN))
        return jnp.where(low, dks[0], dks[1]), jnp.where(low, dvs[0], dvs[1]), dqs[0] + dqs[1]

    def run(kn, qn, plan):
        seen = set()
        for ks, starts in plan:
            dk = dv = None
            for qs in starts:
                a, b, dq = block(ks, kn, qs, qn)
                dk = a if dk is None else dk + a
                dv = b if dv is None else dv + b
                if qs in seen:
                    dqt_ref[:, pl.ds(qs, qn)] += dq
                else:
                    dqt_ref[:, pl.ds(qs, qn)] = dq
                seen.add(qs)
            dk_ref[pl.ds(ks, kn), :] = (dk * LN2).astype(BF)
            dv_ref[pl.ds(ks, kn), :] = dv.astype(BF)
        dq_ref[...] = (dqt_ref[...].T * 0.125).astype(BF)

    @pl.when(tag_ref[r] == 0)
    def _():
        run(kb, qb, [(ks, range(0, length, qb)) for ks in range(0, length, kb)])

    @pl.when(tag_ref[r] != 0)
    def _():
        c = length // 4
        run(c, c, [(ks, [ks]) for ks in range(0, length, c)])


def attend_back(tag, q, k, v, do, o, lse, first, pairs, before=(), kb=512, qb=512):
    t, d = q.shape
    rows = tag.shape[0]
    length = t // rows
    blk = pl.BlockSpec((length, 128), lambda r, p, _: (r, p + first))
    lse_spec = pl.BlockSpec((1, 1, 2, length), lambda r, p, _: (r, p + first, 0, 0))
    return pl.pallas_call(
        functools.partial(attend_back_kernel, kb=kb, qb=qb),
        grid_spec=pltpu.PrefetchScalarGridSpec(
            num_scalar_prefetch=1,
            grid=(rows, pairs),
            in_specs=[blk] * 5 + [lse_spec] + [ANY] * len(before),
            out_specs=[blk] * 3,
            scratch_shapes=[pltpu.VMEM((2, length), F32), pltpu.VMEM((128, length), F32)],
        ),
        out_shape=[SDS((t, d), BF)] * 3,
        input_output_aliases={7: 0, 8: 1, 9: 2} if before else {},
        compiler_params=params(2),
        cost_estimate=cost(5120 * t * length * pairs, t * d * 16, t * length * 12),
        name="attend_back",
    )(tag, q, k, v, do, o, lse, *before)


def grad_qkv_kernel(idx_ref, h_any, dq_any, dk_any, dv_any, *refs, rows):
    h_ref, d_ref, sem = refs[-3:]
    w = d_ref.shape[2]
    half = idx_ref[1] if rows is not None else 1 - idx_ref[1]
    cols = pl.ds(pl.multiple_of(half * w, 128), w)
    going = [pltpu.make_async_copy(h_any, h_ref, sem.at[3])]
    for m, ref in enumerate((dq_any, dk_any, dv_any)):
        going.append(pltpu.make_async_copy(ref.at[:, cols], d_ref.at[m], sem.at[m]))
    for cp in going:
        cp.start()
    going[0].wait()
    for m in range(3):
        at = slice(m * w, (m + 1) * w)
        going[1 + m].wait()
        part = dg(h_ref[...], d_ref[m], TN)
        if rows is None:
            refs[0][:, at] = part.astype(BF)
        else:
            outs, sum_ref = refs[1:-4], refs[-4]
            q = len(outs)
            sum_ref[...] = part + refs[0][:, at].astype(F32)
            for e in range(q):
                for z in range(4):
                    s = z * q + lax.bitwise_xor(idx_ref[0] % q, jnp.int32(e))
                    outs[e][z, :, at] = sum_ref[pl.ds(pl.multiple_of(s * rows, 8), rows), :].astype(BF)


def grad_qkv(idx, h1, dq, dk, dv, recv=None, n=None):
    t, d = h1.shape
    w = d // 2
    own = recv is not None
    outs = [(4, d // n, 3 * w)] * (n // 4) if own else [(d, 3 * w)]
    return pl.pallas_call(
        functools.partial(grad_qkv_kernel, rows=d // n if own else None),
        grid_spec=pltpu.PrefetchScalarGridSpec(
            num_scalar_prefetch=1,
            grid=(1,),
            in_specs=[ANY] * 4 + [whole((d, 3 * w))] * own,
            out_specs=[fixed(o) for o in outs],
            scratch_shapes=[pltpu.VMEM((d, w), F32)] * own
            + [pltpu.VMEM((t, d), BF), pltpu.VMEM((3, t, w), BF), pltpu.SemaphoreType.DMA((4,))],
        ),
        out_shape=[pltpu.HBM(o, BF) for o in outs],
        compiler_params=params(),
        cost_estimate=cost(6 * t * d * w, t * d * 6),
        name="grad_qkv_own" if own else "grad_qkv_other",
    )(idx, h1, dq, dk, dv, *([recv] * own))


def tokens_back_kernel(idx_ref, x_ref, vt_ref, dx2_ref, dq_ref, dk_ref, dv_ref, *refs):
    pieces = refs[:-4]
    tg_ref, s_ref, w_ref, sem = refs[-4:]
    d = x_ref.shape[1]

    @pl.when(pl.program_id(0) == 0)
    def _():
        going = load_qkv(idx_ref, pieces, w_ref, sem)
        s_ref[...] = jnp.zeros_like(s_ref)
        for cp in going:
            cp.wait()

    dh = dg(dq_ref[...], w_ref[:, :d], NT)
    dh = dh + dg(dk_ref[...], w_ref[:, d : 2 * d], NT)
    dh = dh + dg(dv_ref[...], w_ref[:, 2 * d :], NT)
    ones = jnp.ones((8, x_ref.shape[0]), BF)
    s_ref[2:3, :] += dg(ones, dq_ref[...], NN)[0:1]
    s_ref[3:4, :] += dg(ones, dv_ref[...], NN)[0:1]
    c, r = norm_stats(x_ref[...].astype(F32))
    xh = c * r
    s_ref[0:1, :] += jnp.sum(dh * xh, axis=0, keepdims=True)
    s_ref[1:2, :] += jnp.sum(dh, axis=0, keepdims=True)
    dz = dh * vt_ref[0:1, :]
    m1 = jnp.sum(dz, axis=-1, keepdims=True) * (1.0 / d)
    m2 = jnp.sum(dz * xh, axis=-1, keepdims=True) * (1.0 / d)
    tg_ref[...] = dx2_ref[...] + r * (dz - m1 - xh * m2)


def tokens_back(idx, dq, dk, dv, x, vt, dx2, pieces, tb=512):
    t, d = x.shape
    return pl.pallas_call(
        tokens_back_kernel,
        grid_spec=pltpu.PrefetchScalarGridSpec(
            num_scalar_prefetch=1,
            grid=(t // tb,),
            in_specs=[rows_of(tb, d), whole(vt.shape)] + [rows_of(tb, d)] * 4 + [ANY] * len(pieces),
            out_specs=[rows_of(tb, d), fixed((8, d))],
            scratch_shapes=[pltpu.VMEM((d, 3 * d), BF), pltpu.SemaphoreType.DMA],
        ),
        out_shape=[SDS((t, d), F32), SDS((8, d), F32)],
        compiler_params=params(),
        cost_estimate=cost(9 * t * d * d, t * d * 16 + d * d * 6),
        name="tokens_back",
    )(idx, x, vt, dx2, dq, dk, dv, *pieces)


def hop(x, groups):
    return lax.all_to_all(x, "fsdp", split_axis=0, concat_axis=0, tiled=True, axis_index_groups=groups)


def sum_cores_kernel(idx_ref, *refs, q):
    outs = refs[-q:]
    rows = outs[0].shape[1]
    for e in range(q):
        at = lax.bitwise_xor(idx_ref[0] % q, jnp.int32(e))
        start = 0
        for a_ref, b_ref in zip(refs[:-q:2], refs[1:-q:2], strict=True):
            total = a_ref[at] + b_ref[at]
            w = total.shape[1]
            for j in range(total.shape[0] // rows):
                outs[e][0, :, start : start + w] = total[j * rows : (j + 1) * rows]
                start += w


def sum_cores(idx, pairs, rows, n):
    q = n // 4
    ops, specs, width = [], [], 0
    for pair in pairs:
        shape = (pair[0].shape[0] // n, pair[0].shape[1])
        width += shape[0] // rows * shape[1]
        ops += [x.reshape((n,) + shape) for x in pair]
        specs += [pl.BlockSpec((q,) + shape, lambda z, _: (z, 0, 0))] * 2
    return pl.pallas_call(
        functools.partial(sum_cores_kernel, q=q),
        grid_spec=pltpu.PrefetchScalarGridSpec(
            num_scalar_prefetch=1,
            grid=(4,),
            in_specs=specs,
            out_specs=[pl.BlockSpec((1, rows, width), lambda z, _: (z, 0, 0))] * q,
        ),
        out_shape=[pltpu.HBM((4, rows, width), BF)] * q,
        compiler_params=params(),
        cost_estimate=cost(n * rows * width, n * rows * width * 6),
        name="sum_cores",
    )(idx, *ops)


def spread(parts, n):
    return [parts[0]] + [xor_pp(parts[e], e, n) for e in range(1, n // 4)]


def sum_parts_kernel(*refs):
    total = refs[0][...].astype(F32)
    for x in refs[1:-1]:
        total = total + x[...].astype(F32)
    refs[-1][...] = total.astype(BF)


def sum_parts(parts):
    shape = (1,) + parts[0].shape[1:]
    spec = pl.BlockSpec(shape, lambda i: (i, 0, 0))
    return pl.pallas_call(
        sum_parts_kernel,
        grid=(4,),
        in_specs=[spec] * len(parts),
        out_specs=spec,
        out_shape=pltpu.HBM(parts[0].shape, BF),
        compiler_params=params(),
        cost_estimate=cost(4 * len(parts) * math.prod(shape), 8 * len(parts) * math.prod(shape)),
        name="sum_parts",
    )(*parts)


def sum_qkv_kernel(idx_ref, *refs, q):
    for d in range(4):
        at = lax.bitwise_xor(idx_ref[0] // q, jnp.int32(d))
        start = 0
        for parts in (refs[:q], refs[q : 2 * q]):
            total = parts[0][at].astype(F32)
            for x in parts[1:]:
                total = total + x[at].astype(F32)
            w = total.shape[1]
            refs[2 * q + d][:, start : start + w] = total.astype(BF)
            start += w


def sum_qkv(idx, far, vecs, n):
    _, rows, w = far[0].shape
    width = w + vecs[0].shape[2]
    ops = list(far) + list(vecs)
    near = pl.pallas_call(
        functools.partial(sum_qkv_kernel, q=n // 4),
        grid_spec=pltpu.PrefetchScalarGridSpec(
            num_scalar_prefetch=1,
            grid=(1,),
            in_specs=[whole(x.shape) for x in ops],
            out_specs=[fixed((rows, width))] * 4,
        ),
        out_shape=[pltpu.HBM((rows, width), BF)] * 4,
        compiler_params=params(),
        cost_estimate=cost(n * rows * width, n * rows * width * 3),
        name="sum_qkv",
    )(idx, *ops)
    return near


def reduce_last(near, n, m):
    total = near[0].astype(F32)
    for x in near[1:]:
        total = total + x.astype(F32)
    return over_pairs(total, m)


def over_pairs(total, m):
    b = 2
    while b < m:
        total = total + lax.ppermute(total.astype(BF), "dp", [(i, i ^ b) for i in range(m)]).astype(F32)
        b *= 2
    return total


def vec_table_kernel(idx_ref, a, c, u, *refs, q):
    table_ref = refs[q]
    d = a.shape[1]
    rows = refs[0].shape[1]
    wide = u.shape[1] // d
    bias = [
        jnp.concatenate(
            [u[:, (s * wide + j) * rows : (s * wide + j + 1) * rows] for s in range(4 * q)], axis=1
        )
        for j in range(wide)
    ]
    lines = [c[0:4, :], a[3:4, :], a[1:3, :], a[0:1, :]] + bias + [jnp.zeros((120 - wide, d), F32)]
    table_ref[...] = jnp.concatenate(lines, axis=0).T
    for e in range(q):
        for z in range(4):
            s = z * q + lax.bitwise_xor(idx_ref[0] % q, jnp.int32(e))
            refs[e][z] = table_ref[pl.ds(pl.multiple_of(s * rows, 8), rows), :].astype(BF)


def vec_table(idx, s_mlp, s_tok, gbu, n):
    d = s_mlp.shape[1]
    q = n // 4
    return pl.pallas_call(
        functools.partial(vec_table_kernel, q=q),
        grid_spec=pltpu.PrefetchScalarGridSpec(
            num_scalar_prefetch=1,
            grid=(1,),
            in_specs=[whole(s_mlp.shape), whole(s_tok.shape), whole(gbu.shape)],
            out_specs=[fixed((4, d // n, 128))] * q,
            scratch_shapes=[pltpu.VMEM((d, 128), F32)],
        ),
        out_shape=[SDS((4, d // n, 128), BF)] * q,
        compiler_params=params(),
        cost_estimate=cost(d * 128, d * 1024),
        name="vec_table",
    )(idx, s_mlp, s_tok, gbu)


def local(
    tokens,
    sensor_tag,
    owner_order,
    ln1_gain,
    ln1_bias,
    w_qkv,
    b_query,
    b_value,
    w_out,
    b_out,
    ln2_gain,
    ln2_bias,
    w_up,
    b_up,
    w_down,
    b_down,
    out_grad,
    *,
    n,
    m,
):
    t, d = tokens.shape
    ff = w_up.shape[1]
    rows = d // n
    wide = ff // d
    f = lax.axis_index("fsdp")
    c = lax.axis_index("dp") % 2
    idx = jnp.stack([f, c]).astype(jnp.int32)
    use = idx if fits(rows, n) else jnp.zeros_like(idx)

    def core_half(x):
        h = x.shape[1] // 2
        return jnp.where(c == 0, x[:, :h], x[:, h:])

    vec = jnp.stack([ln1_gain, ln1_bias, b_query, b_value, b_out, ln2_gain, ln2_bias, b_down], axis=1)
    vec = jnp.concatenate([vec, b_up.reshape(wide, rows).T], axis=1)
    vec = jnp.pad(vec, ((0, 0), (0, 128 - vec.shape[1])))
    shard_a = jnp.concatenate([core_half(w_qkv), vec], axis=1)
    shard_b = jnp.concatenate(
        [core_half(jnp.concatenate([w_out, w_up], axis=1))]
        + [core_half(w_down[j * rows : (j + 1) * rows]) for j in range(wide)],
        axis=1,
    )
    q = n // 4
    everyone = jnp.arange(n)

    near_a = gather_near(shard_a, n)
    near_b = hop(jnp.broadcast_to(after(shard_b, near_a)[None], (4,) + shard_b.shape), tops(n))
    own_a = gather_far(near_a, n)
    cast = after(out_grad, near_a).astype(BF)
    own_a[1:] = after(own_a[1:], cast)
    swap_a = [core_swap(near_a, m), core_swap(jnp.stack(own_a[1:]), m)]
    if fits(rows, n):
        pieces_a = own_a + swap_a
    else:
        pieces_a = settle(own_a + swap_a[:1] + [swap_a[1][e] for e in range(q - 1)], f ^ everyone, c, n)
    near_b = after(near_b, own_a[1:])
    qh, kh, vh, h1, vt, bu = qkv(use, after(tokens, near_b), pieces_a)
    pairs = d // 128
    early = pairs * 2 // 3
    cut = (d + ff) // 2
    if fits(rows, n):
        x, y = near_b[..., :cut], near_b[..., cut:]
        x1, y2 = after((xor_pp(x, 1, n), xor_pp(y, 2, n)), vt)
        x2, y1 = xor_pp(x, 2, n), xor_pp(y, 1, n)
        x3, y3 = xor_pp(x1, 2, n), xor_pp(y2, 1, n)
        part = attend(sensor_tag, after(qh, x1, y2), kh, vh, 0, early)
        side = [near_b] + after([x1, x2, x3, y1, y2, y3], part[0])
        pieces_b = []
        for x in side:
            pieces_b += [x, core_swap(x, m)]
        gate = side[1:]
    else:
        far_b = gather_far(near_b, n)
        side = settle(
            far_b + [core_swap(x, m) for x in far_b], everyone // q * q + (everyone ^ f) % q, c, n, wide
        )
        part = attend(sensor_tag, qh, kh, vh, 0, early)
        pieces_b = [side[0], side[4]]
        for e in range(1, 4):
            pieces_b += [side[e][..., :cut], side[4 + e][..., :cut]]
        for e in range(1, 4):
            pieces_b += [side[e][..., cut:], side[4 + e][..., cut:]]
        gate = far_b
    returned = lax.all_to_all(after(cast, gate), "fsdp", split_axis=0, concat_axis=0, tiled=True)
    mixed, lse = attend(sensor_tag, qh, kh, vh, early, pairs - early, part)

    x2, active, slope, y = mlp(use, tokens, mixed, vt, bu, pieces_b)
    sent = permute(owner_order, y)
    encoded = lax.all_to_all(sent, "fsdp", split_axis=0, concat_axis=0, tiled=True)

    returned = after(returned, sent)
    dm, du, dx2, do, h2, s_mlp, gbu, out_own, out_other = mlp_back(
        use, owner_order, returned, slope, x2, mixed, vt, pieces_b
    )
    out_recv = core_swap(out_other, m)
    down_own, down_other, up_own, up_other = grad_mlp(idx, active, dm, h2, du)
    down_recv = core_swap(down_other, m)
    up_recv = core_swap(up_other, m)
    part = attend_back(sensor_tag, qh, kh, vh, after(do, up_own, encoded), mixed, lse, 0, 1)
    out_recv, down_recv, up_recv = after((out_recv, down_recv, up_recv), part[0])
    pairs_b = [(up_own, up_recv), (out_own, out_recv), (down_own, down_recv)]
    far_b = sum_cores(idx, pairs_b, rows, n)
    do = after(do, far_b[0])
    far_b = spread(far_b, n)
    dj = attend_back(sensor_tag, qh, kh, vh, do, mixed, lse, 1, pairs - 1, part)
    (qkv_other,) = grad_qkv(idx, h1, *dj)
    qkv_recv = core_swap(qkv_other, m)
    far_b = after(far_b, dj[0])
    near_b = sum_parts([after(far_b[0], qkv_other)] + far_b[1:])
    total_b = hop(near_b, tops(n))
    far_a = grad_qkv(idx, after(h1, near_b), *dj, qkv_recv, n)
    dj = after(dj, far_a[0])
    far_a = spread(far_a, n)
    tokens_grad, s_tok = tokens_back(use, *dj, tokens, vt, dx2, pieces_a)
    far_a, total_b = after((far_a, total_b), tokens_grad)
    total_b = over_pairs(jnp.sum(total_b.astype(F32), axis=0), m).astype(BF)
    other_b = core_swap(total_b, m)
    far_v = spread(vec_table(idx, s_mlp, s_tok, after(gbu, far_a), n), n)

    near_a = sum_qkv(idx, after(far_a, total_b), far_v, n)
    encoded = after(encoded, near_a[0]).astype(F32)
    near_a = [near_a[0]] + [xor_pp(near_a[i], i * q, n) for i in range(1, 4)]
    def both(mine, other):
        first = c == 0
        return jnp.where(first, mine, other).astype(F32), jnp.where(first, other, mine).astype(F32)

    def join(pair, start, width, parts, axis=1):
        out = []
        for p in range(parts):
            at = slice(start + p * width, start + (p + 1) * width)
            out.append(jnp.concatenate([pair[0][:, at], pair[1][:, at]], axis=1))
        return jnp.concatenate(out, axis=axis)

    h = d // 2
    g_mlp = both(total_b, other_b)
    grad_up_out = join(g_mlp, 0, h, wide)
    grad_out_out = join(g_mlp, ff // 2, h, 1)
    grad_down_out = join(g_mlp, (d + ff) // 2, h, wide, 0)
    near_a = after(near_a, grad_up_out, grad_out_out, grad_down_out, encoded)
    total_a = reduce_last(near_a, n, m)
    other_a = core_swap(total_a.astype(BF), m)
    cut = 3 * d // 2
    vecs = (total_a[:, cut:] + other_a[:, cut:].astype(F32)).T
    total_a, other_a = total_a[:, :cut].astype(BF), other_a[:, :cut]

    grad_qkv_out = join(both(total_a, other_a), 0, h, 3)
    return (
        encoded,
        tokens_grad,
        vecs[0],
        vecs[1],
        grad_qkv_out,
        vecs[2],
        vecs[3],
        grad_out_out,
        vecs[4],
        vecs[5],
        vecs[6],
        grad_up_out,
        vecs[8 : 8 + wide].reshape(ff // n),
        grad_down_out,
        vecs[7],
    )


def solution(mesh):
    n = mesh.shape["fsdp"]
    m = mesh.shape["dp"]
    both = P(("dp", "fsdp"), None)
    vec = P("fsdp")
    mat = P("fsdp", None)
    in_specs = (both, P(("dp", "fsdp")), both, vec, vec, mat, vec, vec, mat, vec, vec, vec, mat, vec, mat, vec, both)
    out_specs = (both, both, vec, vec, mat, vec, vec, mat, vec, vec, vec, mat, vec, mat, vec)
    return jax.shard_map(
        functools.partial(local, n=n, m=m), mesh=mesh, in_specs=in_specs, out_specs=out_specs, check_vma=False
    )
```

profile of v0, /device:TPU:0, one launch (start us, length us, event | category | flops | bytes accessed | tf_op | source)
XLA Modules:
  0.0 447.7 jit_solution(7721038742955354039)
XLA Ops:
  3.3 4.1 collective-permute-start.1
  18.5 5.4 %all-to-all-start = ((bf16[4,48,3456]{2,1,0:T(8,128)(2,1)}), bf16[4,48,3456]{2,1,0:T(8,128)(2,1)S(1)}, u32[]{:S(2)}, u32[]{:S(2)}) async-start(bf16[4,48,3456]{2,1,0:T(8,128)(2,1)} %broadcast_in_dim.2), calls=%async_computation | async-start | bytes 2654208 | tf_op jit(solution)/shard_map/all_to_all | solution.py:703
  27.3 4.8 %convert_element_type.41 = bf16[2048,768]{1,0:T(8,128)(2,1)} convert(f32[2048,768]{1,0:T(8,128)} %param.33) | non-fusion elementwise | flops 1572864 | bytes 9437184 | tf_op jit(solution)/shard_map/convert_element_type | solution.py:905
  32.1 6.8 %collective-permute-done.5.refs_3_ = bf16[4,48,1280]{2,1,0:T(8,128)(2,1)S(1)} collective-permute-done((bf16[4,48,1280]{2,1,0:T(8,128)(2,1)S(1)}, bf16[4,48,1280]{2,1,0:T(8,128)(2,1)S(1)}, u32[]{:S(2)}, u32[]{:S(2)}) %collective-permute-start.5) | collective-permute-done | bytes 491552 | tf_op jit(solution)/shard_map/ppermute | solution.py:64
  38.9 9.2 %collective-permute-done.4.refs_2_ = bf16[4,48,1280]{2,1,0:T(8,128)(2,1)S(1)} collective-permute-done((bf16[4,48,1280]{2,1,0:T(8,128)(2,1)S(1)}, bf16[4,48,1280]{2,1,0:T(8,128)(2,1)S(1)}, u32[]{:S(2)}, u32[]{:S(2)}) %collective-permute-start.4) | collective-permute-done | bytes 491552 | tf_op jit(solution)/shard_map/ppermute | solution.py:64
  50.4 5.3 %all-to-all-done.refs_0_ = bf16[4,48,3456]{2,1,0:T(8,128)(2,1)S(1)} async-done(((bf16[4,48,3456]{2,1,0:T(8,128)(2,1)}), bf16[4,48,3456]{2,1,0:T(8,128)(2,1)S(1)}, u32[]{:S(2)}, u32[]{:S(2)}) %all-to-all-start) | async-done | bytes 1327136 | tf_op jit(solution)/shard_map/all_to_all | solution.py:703
  63.7 14.6 %qkv.1 = (bf16[2048,768]{1,0:T(8,128)(2,1)}, bf16[2048,768]{1,0:T(8,128)(2,1)}, bf16[2048,768]{1,0:T(8,128)(2,1)}, bf16[2048,768]{1,0:T(8,128)(2,1)}, f32[16,768]{1,0:T(8,128)}, /*index=5*/f32[1,3072]{1,0:T(1,128)}) custom-call(s32[2]{0:T(128)} %pad_add_fusion.idx_ref, bf16[2048,768]{1,0:T(8,128)(2,1)} %x_ref.4, bf16[4,48,1280]{2,1,0:T(8,128)(2,1)} %copy-done.3, ...), custom_call_target="tpu_custom_call" | custom-call | flops 7077888 | bytes 15744 | tf_op jit(solution)/shard_map/qkv/pallas_call | solution.py:201
  81.0 28.6 %attend.2 = (bf16[2048,768]{1,0:T(8,128)(2,1)}, f32[2,6,2,1024]{3,2,1,0:T(2,128)}) custom-call(s32[2]{0:T(128)} %tag_ref.7, bf16[2048,768]{1,0:T(8,128)(2,1)} %get-tuple-element.126.q_ref, bf16[2048,768]{1,0:T(8,128)(2,1)} %get-tuple-element.121.k_ref, bf16[2048,768]{1,0:T(8,128)(2,1)} %get-tuple-element.122.v_ref), custom_call_target="tpu_custom_call" | custom-call | flops 16777216 | bytes 12288 | tf_op jit(solution)/shard_map/attend/pallas_call | solution.py:265
  110.5 4.7 %all-to-all-start.2 = ((bf16[16,128,768]{2,1,0:T(8,128)(2,1)}), bf16[16,128,768]{2,1,0:T(8,128)(2,1)}, u32[]{:S(2)}, u32[]{:S(2)}) async-start(bf16[16,128,768]{2,1,0:T(8,128)(2,1)} %bitcast.33), calls=%async_computation.2 | async-start | bytes 6291456 | tf_op jit(solution)/shard_map/all_to_all | solution.py:940
  120.2 15.6 %attend.3 = (bf16[2048,768]{1,0:T(8,128)(2,1)}, f32[2,6,2,1024]{3,2,1,0:T(2,128)}) custom-call(s32[2]{0:T(128)} %tag_ref.7, bf16[2048,768]{1,0:T(8,128)(2,1)} %get-tuple-element.126.q_ref, bf16[2048,768]{1,0:T(8,128)(2,1)} %get-tuple-element.121.k_ref, bf16[2048,768]{1,0:T(8,128)(2,1)} %get-tuple-element.122.v_ref, ...), custom_call_target="tpu_custom_call", output_to_operand_aliasing={{0}: (4, {}), {1}: (5, {})} | custom-call | flops 8388608 | bytes 12288 | tf_op jit(solution)/shard_map/attend/pallas_call | solution.py:265
  137.6 44.3 %mlp.1 = (f32[2048,768]{1,0:T(8,128)}, bf16[2048,3072]{1,0:T(8,128)(2,1)}, bf16[2048,3072]{1,0:T(8,128)(2,1)}, bf16[2048,768]{1,0:T(8,128)(2,1)}) custom-call(s32[2]{0:T(128)} %pad_add_fusion.idx_ref, bf16[2048,768]{1,0:T(8,128)(2,1)} %x_ref.4, bf16[2048,768]{1,0:T(8,128)(2,1)} %get-tuple-element.129.o_ref, f32[16,768]{1,0:T(8,128)} %get-tuple-element.123.vt_ref, ...), custom_call_target="tpu_custom_call" | custom-call | flops 42467328 | bytes 49152 | tf_op jit(solution)/shard_map/mlp/pallas_call | solution.py:330
  181.9 11.1 %permute.1 = bf16[2048,768]{1,0:T(8,128)(2,1)} custom-call(s32[1,2048]{1,0:T(1,128)} %ord_ref.3, bf16[2048,768]{1,0:T(8,128)(2,1)} %get-tuple-element.137.y_ref), custom_call_target="tpu_custom_call" | custom-call | flops 6291456 | bytes 6144 | tf_op jit(solution)/shard_map/permute/pallas_call | solution.py:360
  193.0 5.5 %all-to-all-start.1 = ((bf16[16,128,768]{2,1,0:T(8,128)(2,1)}), bf16[16,128,768]{2,1,0:T(8,128)(2,1)S(1)}, u32[]{:S(2)}, u32[]{:S(2)}) async-start(bf16[16,128,768]{2,1,0:T(8,128)(2,1)} %bitcast.31), calls=%async_computation.1 | async-start | bytes 6291456 | tf_op jit(solution)/shard_map/all_to_all | solution.py:945
  198.5 50.0 %mlp_back.1 = (bf16[2048,768]{1,0:T(8,128)(2,1)}, bf16[2048,3072]{1,0:T(8,128)(2,1)}, f32[2048,768]{1,0:T(8,128)}, bf16[2048,768]{1,0:T(8,128)(2,1)}, bf16[2048,...) custom-call(s32[2]{0:T(128)} %pad_add_fusion.idx_ref, ...), custom_call_target="tpu_custom_call" | custom-call | flops 41287680 | bytes 55296 | tf_op jit(solution)/shard_map/mlp_back/pallas_call | solution.py:436
  248.5 27.7 %grad_mlp.1 = (bf16[3072,384]{1,0:T(8,128)(2,1)}, bf16[3072,384]{1,0:T(8,128)(2,1)}, bf16[768,1536]{1,0:T(8,128)(2,1)}, bf16[768,1536]{1,0:T(8,128)(2,1)}) custom-call(s32[2]{0:T(128)} %pad_add_fusion.idx_ref, bf16[2048,3072]{1,0:T(8,128)(2,1)} %get-tuple-element.139.g_ref, bf16[2048,768]{1,0:T(8,128)(2,1)} %get-tuple-element.144.dm_ref, ...), custom_call_target="tpu_custom_call" | custom-call | flops 28311552 | bytes 39936 | tf_op jit(solution)/shard_map/grad_mlp/pallas_call | solution.py:505
  277.6 14.0 %attend_back.2 = (bf16[2048,768]{1,0:T(8,128)(2,1)}, bf16[2048,768]{1,0:T(8,128)(2,1)}, bf16[2048,768]{1,0:T(8,128)(2,1)}) custom-call(s32[2]{0:T(128)} %tag_ref.7, bf16[2048,768]{1,0:T(8,128)(2,1)} %get-tuple-element.126.q_ref, bf16[2048,768]{1,0:T(8,128)(2,1)} %get-tuple-element.121.k_ref, bf16[2048,768]{1,0:T(8,128)(2,1)} %get-tuple-element.122.v_ref, ...), custom_call_target="tpu_custom_call" | custom-call | flops 10485760 | bytes 24576 | tf_op jit(solution)/shard_map/attend_back/pallas_call | solution.py:590
  291.6 7.3 %sum_cores.1 = (bf16[4,48,3456]{2,1,0:T(8,128)(2,1)}, bf16[4,48,3456]{2,1,0:T(8,128)(2,1)}, bf16[4,48,3456]{2,1,0:T(8,128)(2,1)}, bf16[4,48,3456]{2,1,0:T(8,128)(2,1)}) custom-call(s32[2]{0:T(128)} %pad_add_fusion.idx_ref, bf16[16,48,1536]{2,1,0:T(8,128)(2,1)} %bitcast.38, bf16[16,48,1536]{2,1,0:T(8,128)(2,1)} %bitcast.23.refs_1_, ...), custom_call_target="tpu_custom_call" | custom-call | flops 2592 | bytes 15552 | tf_op jit(solution)/shard_map/sum_cores/pallas_call | solution.py:728
  302.4 57.9 %attend_back.3 = (bf16[2048,768]{1,0:T(8,128)(2,1)}, bf16[2048,768]{1,0:T(8,128)(2,1)}, bf16[2048,768]{1,0:T(8,128)(2,1)}) custom-call(s32[2]{0:T(128)} %tag_ref.7, bf16[2048,768]{1,0:T(8,128)(2,1)} %get-tuple-element.126.q_ref, bf16[2048,768]{1,0:T(8,128)(2,1)} %get-tuple-element.121.k_ref, ...), custom_call_target="tpu_custom_call", output_to_operand_aliasing={{0}: (7, {}), {1}: (8, {}), {2}: (9, {})} | custom-call | flops 52428800 | bytes 24576 | tf_op jit(solution)/shard_map/attend_back/pallas_call | solution.py:590
  360.4 9.7 %grad_qkv_other.1 = bf16[768,1152]{1,0:T(8,128)(2,1)} custom-call(s32[2]{0:T(128)} %pad_add_fusion.idx_ref, bf16[2048,768]{1,0:T(8,128)(2,1)} %get-tuple-element.175.h_any, bf16[2048,768]{1,0:T(8,128)(2,1)} %get-tuple-element.181.dq_any.dq_ref, bf16[2048,768]{1,0:T(8,128)(2,1)} %get-tuple-element.182.dk_any.dk_ref, ...), custom_call_target="tpu_custom_call" | custom-call | flops 3538944 | bytes 9216 | tf_op jit(solution)/shard_map/grad_qkv_other/pallas_call | solution.py:639
  371.6 4.4 sum_parts.1
  376.1 4.6 %all-to-all-start.3 = ((bf16[4,48,3456]{2,1,0:T(8,128)(2,1)}), bf16[4,48,3456]{2,1,0:T(8,128)(2,1)}, u32[]{:S(2)}, u32[]{:S(2)}) async-start(bf16[4,48,3456]{2,1,0:T(8,128)(2,1)} %sum_parts.1), calls=%async_computation.3 | async-start | bytes 2654208 | tf_op jit(solution)/shard_map/all_to_all | solution.py:703
  380.7 11.3 %grad_qkv_own.1 = (bf16[4,48,1152]{2,1,0:T(8,128)(2,1)}, bf16[4,48,1152]{2,1,0:T(8,128)(2,1)}, bf16[4,48,1152]{2,1,0:T(8,128)(2,1)}, bf16[4,48,1152]{2,1,0:T(8,128)(2,1)}) custom-call(s32[2]{0:T(128)} %pad_add_fusion.idx_ref, bf16[2048,768]{1,0:T(8,128)(2,1)} %get-tuple-element.175.h_any, bf16[2048,768]{1,0:T(8,128)(2,1)} %get-tuple-element.181.dq_any.dq_ref, ...), custom_call_target="tpu_custom_call" | custom-call | flops 3538944 | bytes 9216 | tf_op jit(solution)/shard_map/grad_qkv_own/pallas_call | solution.py:639
  395.6 18.2 %tokens_back.1 = (f32[2048,768]{1,0:T(8,128)}, f32[8,768]{1,0:T(8,128)}) custom-call(s32[2]{0:T(128)} %pad_add_fusion.idx_ref, bf16[2048,768]{1,0:T(8,128)(2,1)} %x_ref.4, f32[16,768]{1,0:T(8,128)} %get-tuple-element.123.vt_ref, f32[2048,768]{1,0:T(8,128)} %get-tuple-element.180.dx2_ref, bf16[2048,768]{1,0:T(8,128)(2,1)} %get-tuple-element.181.dq_any.dq_ref, ...), custom_call_target="tpu_custom_call" | custom-call | flops 10616832 | bytes 28032 | tf_op jit(solution)/shard_map/tokens_back/pallas_call | solution.py:686
  439.5 3.7 collective-permute-done.35
  (167 shorter events, 77.1 us)
Async XLA Ops:
  18.5 37.3 %all-to-all-start = ((bf16[4,48,3456]{2,1,0:T(8,128)(2,1)}), bf16[4,48,3456]{2,1,0:T(8,128)(2,1)S(1)}, u32[]{:S(2)}, u32[]{:S(2)}) async-start(bf16[4,48,3456]{2,1,0:T(8,128)(2,1)} %broadcast_in_dim.2), calls=%async_computation | async-start | bytes 2654208 | tf_op jit(solution)/shard_map/all_to_all | solution.py:703
  26.3 21.8 %collective-permute-start.4 = (bf16[4,48,1280]{2,1,0:T(8,128)(2,1)S(1)}, bf16[4,48,1280]{2,1,0:T(8,128)(2,1)S(1)}, u32[]{:S(2)}, u32[]{:S(2)}) collective-permute-start(bf16[4,48,1280]{2,1,0:T(8,128)(2,1)S(1)} %pad_maximum_fusion.1.refs_0_), channel_id=1, source_target_pairs={{0,2},{1,3},{2,0},{3,1},{4,6},{5,7},{6,4},{7,5},{8,10},{9,11},{10,... | collective-permute-start | bytes 1474568 | tf_op jit(solution)/shard_map/ppermute | solution.py:64
  26.8 21.4 %collective-permute-start.3 = (bf16[4,48,1280]{2,1,0:T(8,128)(2,1)S(1)}, bf16[4,48,1280]{2,1,0:T(8,128)(2,1)S(1)}, u32[]{:S(2)}, u32[]{:S(2)}) collective-permute-start(bf16[4,48,1280]{2,1,0:T(8,128)(2,1)S(1)} %pad_maximum_fusion.1.refs_0_), channel_id=1, source_target_pairs={{0,1},{1,0},{2,3},{3,2},{4,5},{5,4},{6,7},{7,6},{8,9},{9,8},{10,11... | collective-permute-start | bytes 1474568 | tf_op jit(solution)/shard_map/ppermute | solution.py:64
  56.7 21.6 %collective-permute-start.8 = (bf16[4,48,1920]{2,1,0:T(8,128)(2,1)}, bf16[4,48,1920]{2,1,0:T(8,128)(2,1)}, u32[]{:S(2)}, u32[]{:S(2)}) collective-permute-start(bf16[4,48,1920]{2,1,0:T(8,128)(2,1)} %slice.178), channel_id=1, source_target_pairs={{0,1},{1,0},{2,3},{3,2},{4,5},{5,4},{6,7},{7,6},{8,9},{9,8},{10,11... | collective-permute-start | bytes 2211848 | tf_op jit(solution)/shard_map/ppermute | solution.py:64
  59.0 19.3 %collective-permute-start.9 = (bf16[4,48,1536]{2,1,0:T(8,128)(2,1)}, bf16[4,48,1536]{2,1,0:T(8,128)(2,1)}, u32[]{:S(2)}, u32[]{:S(2)}) collective-permute-start(bf16[4,48,1536]{2,1,0:T(8,128)(2,1)} %slice.179), channel_id=1, source_target_pairs={{0,2},{1,3},{2,0},{3,1},{4,6},{5,7},{6,4},{7,5},{8,10},{9,11},{10,... | collective-permute-start | bytes 1769480 | tf_op jit(solution)/shard_map/ppermute | solution.py:64
  61.2 48.5 %collective-permute-start.11 = (bf16[4,48,1920]{2,1,0:T(8,128)(2,1)}, bf16[4,48,1920]{2,1,0:T(8,128)(2,1)}, u32[]{:S(2)}, u32[]{:S(2)}) collective-permute-start(bf16[4,48,1920]{2,1,0:T(8,128)(2,1)} %slice.178), channel_id=1, source_target_pairs={{0,2},{1,3},{2,0},{3,1},{4,6},{5,7},{6,4},{7,5},{8,10},{9,11},{10,... | collective-permute-start | bytes 2211848 | tf_op jit(solution)/shard_map/ppermute | solution.py:64
  78.3 31.4 %collective-permute-start.12 = (bf16[4,48,1920]{2,1,0:T(8,128)(2,1)}, bf16[4,48,1920]{2,1,0:T(8,128)(2,1)S(1)}, u32[]{:S(2)}, u32[]{:S(2)}) collective-permute-start(bf16[4,48,1920]{2,1,0:T(8,128)(2,1)} %collective-permute-done.8.refs_2_), channel_id=1, source_target_pairs={{0,2},{1,3},{2,0},{3,1},{4,6},{5,7},{6,4},{7,5},{8,10},{9,11},{10,... | collective-permute-start | bytes 2211848 | tf_op jit(solution)/shard_map/ppermute | solution.py:64
  79.0 30.6 %collective-permute-start.13 = (bf16[4,48,1536]{2,1,0:T(8,128)(2,1)}, bf16[4,48,1536]{2,1,0:T(8,128)(2,1)}, u32[]{:S(2)}, u32[]{:S(2)}) collective-permute-start(bf16[4,48,1536]{2,1,0:T(8,128)(2,1)} %slice.179), channel_id=1, source_target_pairs={{0,1},{1,0},{2,3},{3,2},{4,5},{5,4},{6,7},{7,6},{8,9},{9,8},{10,11... | collective-permute-start | bytes 1769480 | tf_op jit(solution)/shard_map/ppermute | solution.py:64
  79.6 30.1 %collective-permute-start.14 = (bf16[4,48,1536]{2,1,0:T(8,128)(2,1)}, bf16[4,48,1536]{2,1,0:T(8,128)(2,1)S(1)}, u32[]{:S(2)}, u32[]{:S(2)}) collective-permute-start(bf16[4,48,1536]{2,1,0:T(8,128)(2,1)} %collective-permute-done.9.refs_10_), channel_id=1, source_target_pairs={{0,1},{1,0},{2,3},{3,2},{4,5},{5,4},{6,7},{7,6},{8,9},{9,8},{10,11... | collective-permute-start | bytes 1769480 | tf_op jit(solution)/shard_map/ppermute | solution.py:64
  110.5 82.5 %all-to-all-start.2 = ((bf16[16,128,768]{2,1,0:T(8,128)(2,1)}), bf16[16,128,768]{2,1,0:T(8,128)(2,1)}, u32[]{:S(2)}, u32[]{:S(2)}) async-start(bf16[16,128,768]{2,1,0:T(8,128)(2,1)} %bitcast.33), calls=%async_computation.2 | async-start | bytes 6291456 | tf_op jit(solution)/shard_map/all_to_all | solution.py:940
  115.8 20.1 %collective-permute-start.15 = (bf16[4,48,1920]{2,1,0:T(8,128)(2,1)}, bf16[4,48,1920]{2,1,0:T(8,128)(2,1)S(1)}, u32[]{:S(2)}, u32[]{:S(2)}) collective-permute-start(bf16[4,48,1920]{2,1,0:T(8,128)(2,1)} %collective-permute-done.8.refs_2_), channel_id=1, source_target_pairs={{0,16},{16,0},{1,17},{17,1},{2,18},{18,2},{3,19},{19,3},{4,20},{20... | collective-permute-start | bytes 2211848 | tf_op jit(solution)/shard_map/ppermute | solution.py:68
  115.8 20.0 %collective-permute-start.16 = (bf16[4,48,1920]{2,1,0:T(8,128)(2,1)}, bf16[4,48,1920]{2,1,0:T(8,128)(2,1)S(1)}, u32[]{:S(2)}, u32[]{:S(2)}) collective-permute-start(bf16[4,48,1920]{2,1,0:T(8,128)(2,1)} %collective-permute-done.11.refs_4_), channel_id=1, source_target_pairs={{0,16},{16,0},{1,17},{17,1},{2,18},{18,2},{3,19},{19,3},{4,20},{20... | collective-permute-start | bytes 2211848 | tf_op jit(solution)/shard_map/ppermute | solution.py:68
  116.3 19.6 %collective-permute-start.17 = (bf16[4,48,1920]{2,1,0:T(8,128)(2,1)S(1)}, bf16[4,48,1920]{2,1,0:T(8,128)(2,1)S(1)}, u32[]{:S(2)}, u32[]{:S(2)}) collective-permute-start(bf16[4,48,1920]{2,1,0:T(8,128)(2,1)S(1)} %collective-permute-done.12.refs_6_), channel_id=1, source_target_pairs={{0,16},{16,0},{1,17},{17,1},{2,18},{18,2},{3,19},{19,3},{4,20},{20... | collective-permute-start | bytes 2211848 | tf_op jit(solution)/shard_map/ppermute | solution.py:68
  119.4 16.4 %collective-permute-start.19 = (bf16[4,48,1536]{2,1,0:T(8,128)(2,1)}, bf16[4,48,1536]{2,1,0:T(8,128)(2,1)S(1)}, u32[]{:S(2)}, u32[]{:S(2)}) collective-permute-start(bf16[4,48,1536]{2,1,0:T(8,128)(2,1)} %collective-permute-done.9.refs_10_), channel_id=1, source_target_pairs={{0,16},{16,0},{1,17},{17,1},{2,18},{18,2},{3,19},{19,3},{4,20},{20... | collective-permute-start | bytes 1769480 | tf_op jit(solution)/shard_map/ppermute | solution.py:68
  119.8 16.0 %collective-permute-start.20 = (bf16[4,48,1536]{2,1,0:T(8,128)(2,1)}, bf16[4,48,1536]{2,1,0:T(8,128)(2,1)S(1)}, u32[]{:S(2)}, u32[]{:S(2)}) collective-permute-start(bf16[4,48,1536]{2,1,0:T(8,128)(2,1)} %copy-done.11), channel_id=1, source_target_pairs={{0,16},{16,0},{1,17},{17,1},{2,18},{18,2},{3,19},{19,3},{4,20},{20... | collective-permute-start | bytes 1769480 | tf_op jit(solution)/shard_map/ppermute | solution.py:68
  193.0 84.6 %all-to-all-start.1 = ((bf16[16,128,768]{2,1,0:T(8,128)(2,1)}), bf16[16,128,768]{2,1,0:T(8,128)(2,1)S(1)}, u32[]{:S(2)}, u32[]{:S(2)}) async-start(bf16[16,128,768]{2,1,0:T(8,128)(2,1)} %bitcast.31), calls=%async_computation.1 | async-start | bytes 6291456 | tf_op jit(solution)/shard_map/all_to_all | solution.py:945
  298.9 71.2 %collective-permute-start.24 = (bf16[4,48,3456]{2,1,0:T(8,128)(2,1)}, bf16[4,48,3456]{2,1,0:T(8,128)(2,1)S(1)}, u32[]{:S(2)}, u32[]{:S(2)}) collective-permute-start(bf16[4,48,3456]{2,1,0:T(8,128)(2,1)} %get-tuple-element.161), channel_id=1, source_target_pairs={{0,1},{1,0},{2,3},{3,2},{4,5},{5,4},{6,7},{7,6},{8,9},{9,8},{10,11... | collective-permute-start | bytes 3981320 | tf_op jit(solution)/shard_map/ppermute | solution.py:64
  299.0 71.2 %collective-permute-start.25 = (bf16[4,48,3456]{2,1,0:T(8,128)(2,1)}, bf16[4,48,3456]{2,1,0:T(8,128)(2,1)S(1)}, u32[]{:S(2)}, u32[]{:S(2)}) collective-permute-start(bf16[4,48,3456]{2,1,0:T(8,128)(2,1)} %get-tuple-element.162), channel_id=1, source_target_pairs={{0,2},{1,3},{2,0},{3,1},{4,6},{5,7},{6,4},{7,5},{8,10},{9,11},{10,... | collective-permute-start | bytes 3981320 | tf_op jit(solution)/shard_map/ppermute | solution.py:64
  299.0 71.2 %collective-permute-start.26 = (bf16[4,48,3456]{2,1,0:T(8,128)(2,1)}, bf16[4,48,3456]{2,1,0:T(8,128)(2,1)}, u32[]{:S(2)}, u32[]{:S(2)}) collective-permute-start(bf16[4,48,3456]{2,1,0:T(8,128)(2,1)} %get-tuple-element.163), channel_id=1, source_target_pairs={{0,3},{1,2},{2,1},{3,0},{4,7},{5,6},{6,5},{7,4},{8,11},{9,10},{10,... | collective-permute-start | bytes 3981320 | tf_op jit(solution)/shard_map/ppermute | solution.py:64
  376.1 38.5 %all-to-all-start.3 = ((bf16[4,48,3456]{2,1,0:T(8,128)(2,1)}), bf16[4,48,3456]{2,1,0:T(8,128)(2,1)}, u32[]{:S(2)}, u32[]{:S(2)}) async-start(bf16[4,48,3456]{2,1,0:T(8,128)(2,1)} %sum_parts.1), calls=%async_computation.3 | async-start | bytes 2654208 | tf_op jit(solution)/shard_map/all_to_all | solution.py:703
  392.0 21.8 %collective-permute-start.28 = (bf16[4,48,1152]{2,1,0:T(8,128)(2,1)}, bf16[4,48,1152]{2,1,0:T(8,128)(2,1)}, u32[]{:S(2)}, u32[]{:S(2)}) collective-permute-start(bf16[4,48,1152]{2,1,0:T(8,128)(2,1)} %get-tuple-element.177), channel_id=1, source_target_pairs={{0,1},{1,0},{2,3},{3,2},{4,5},{5,4},{6,7},{7,6},{8,9},{9,8},{10,11... | collective-permute-start | bytes 1327112 | tf_op jit(solution)/shard_map/ppermute | solution.py:64
  393.3 21.3 %collective-permute-start.29 = (bf16[4,48,1152]{2,1,0:T(8,128)(2,1)}, bf16[4,48,1152]{2,1,0:T(8,128)(2,1)}, u32[]{:S(2)}, u32[]{:S(2)}) collective-permute-start(bf16[4,48,1152]{2,1,0:T(8,128)(2,1)} %get-tuple-element.178), channel_id=1, source_target_pairs={{0,2},{1,3},{2,0},{3,1},{4,6},{5,7},{6,4},{7,5},{8,10},{9,11},{10,... | collective-permute-start | bytes 1327112 | tf_op jit(solution)/shard_map/ppermute | solution.py:64
  393.7 20.9 %collective-permute-start.30 = (bf16[4,48,1152]{2,1,0:T(8,128)(2,1)}, bf16[4,48,1152]{2,1,0:T(8,128)(2,1)}, u32[]{:S(2)}, u32[]{:S(2)}) collective-permute-start(bf16[4,48,1152]{2,1,0:T(8,128)(2,1)} %get-tuple-element.179), channel_id=1, source_target_pairs={{0,3},{1,2},{2,1},{3,0},{4,7},{5,6},{6,5},{7,4},{8,11},{9,10},{10,... | collective-permute-start | bytes 1327112 | tf_op jit(solution)/shard_map/ppermute | solution.py:64
  416.2 21.5 %collective-permute-start.37 = (bf16[48,3456]{1,0:T(8,128)(2,1)S(1)}, bf16[48,3456]{1,0:T(8,128)(2,1)S(1)}, u32[]{:S(2)}, u32[]{:S(2)}) collective-permute-start(bf16[48,3456]{1,0:T(8,128)(2,1)S(1)} %reduce_sum.12), channel_id=1, source_target_pairs={{0,16},{16,0},{1,17},{17,1},{2,18},{18,2},{3,19},{19,3},{4,20},{20... | collective-permute-start | bytes 995336 | tf_op jit(solution)/shard_map/ppermute | solution.py:68
  (42 other events, 348.9 us)
where the time goes:
time: 456 us; the launch traced here: 448 us
  Pallas kernels  320 us (70%)
  starting transfers between devices  54.5 us (12%)
  waiting for transfers between devices  39 us (9%)
  other arithmetic  18.5 us (4%)
  local copies, waits for them, and re-layouts  13.8 us (3%)
    pallas_call x2, Pallas kernels, attend_back(): pl.pallas_call(functools.partial(attend_back_kernel, kb=kb, qb=qb), grid_...  72 us
    pallas_call x1, Pallas kernels, mlp_back(): pl.pallas_call(functools.partial(mlp_back_kernel, fc=fc), grid_spec=pltpu...  50 us
    pallas_call x1, Pallas kernels, mlp(): pl.pallas_call(functools.partial(mlp_kernel, fc=fc), grid_spec=pltpu.Pref...  44.3 us
    pallas_call x2, Pallas kernels, attend(): pl.pallas_call(functools.partial(attend_kernel, qb=qb), grid_spec=pltpu.P...  44.2 us
    ppermute x24, starting transfers between devices, xor_pp(): return lax.ppermute(x, 'fsdp', [(i, i ^ b) for i in range(n)])  31.1 us
    ppermute x24, waiting for transfers between devices, xor_pp(): return lax.ppermute(x, 'fsdp', [(i, i ^ b) for i in range(n)])  28 us
    pallas_call x1, Pallas kernels, grad_mlp(): pl.pallas_call(grad_mlp_kernel, grid_spec=pltpu.PrefetchScalarGridSpec(nu...  27.7 us
    pallas_call x2, Pallas kernels, grad_qkv(): pl.pallas_call(functools.partial(grad_qkv_kernel, rows=d // n if own else...  21 us
  transfers between devices with their start and end apart: 43, of which 15 were waited for; matrix products, arithmetic and copies ran while one was open for 4% of the time, Pallas kernels for 70%

commit v1 on v0

--- a/solution.py
+++ b/solution.py
@@ -17,6 +17,7 @@
 TN = (((0,), (0,)), ((), ()))
 NN = (((1,), (0,)), ((), ()))
 ANY = pl.BlockSpec(memory_space=pl.ANY)
+SAFE_SCORE = 90.0
 VECS = 16
 SDS = jax.ShapeDtypeStruct
 
@@ -168,8 +169,8 @@
 
 
 def qkv_kernel(idx_ref, x_ref, *refs):
-    pieces = refs[:-9]
-    q_ref, k_ref, v_ref, h_ref, vt_ref, bu_ref, w_ref, vec_ref, sem = refs[-9:]
+    pieces = refs[:-11]
+    q_ref, k_ref, v_ref, h_ref, vt_ref, bu_ref, qn_ref, kn_ref, w_ref, vec_ref, sem = refs[-11:]
     d = x_ref.shape[1]
 
     @pl.when(pl.program_id(0) == 0)
@@ -190,9 +191,15 @@
     c, r = norm_stats(x_ref[...].astype(F32))
     h = (c * r * vt_ref[0:1, :] + vt_ref[1:2, :]).astype(BF)
     h_ref[...] = h
-    q = dg(h, w_ref[:, :d], NN)
-    q_ref[...] = ((q + vt_ref[2:3, :]) * (0.125 * LOG2E)).astype(BF)
-    k_ref[...] = dg(h, w_ref[:, d : 2 * d], NN).astype(BF)
+    q = (dg(h, w_ref[:, :d], NN) + vt_ref[2:3, :]) * (0.125 * LOG2E)
+    q_ref[...] = q.astype(BF)
+    k = dg(h, w_ref[:, d : 2 * d], NN)
+    k_ref[...] = k.astype(BF)
+    lane = lax.broadcasted_iota(jnp.int32, (d, 128), 0)
+    head = lax.broadcasted_iota(jnp.int32, (d, 128), 1) * 64
+    of_head = jnp.where((lane >= head) & (lane < head + 64), 1.0, 0.0).astype(BF)
+    for x, n_ref in ((q, qn_ref), (k, kn_ref)):
+        n_ref[0] = jnp.max(dg((x * x).astype(BF), of_head, NN), axis=0, keepdims=True)
     v_ref[...] = (dg(h, w_ref[:, 2 * d :], NN) + vt_ref[3:4, :]).astype(BF)
 
 
@@ -204,27 +211,43 @@
             num_scalar_prefetch=1,
             grid=(t // tb,),
             in_specs=[rows_of(tb, d)] + [ANY] * len(pieces),
-            out_specs=[rows_of(tb, d)] * 4 + [fixed((VECS, d)), fixed((1, 4 * d))],
+            out_specs=[rows_of(tb, d)] * 4
+            + [fixed((VECS, d)), fixed((1, 4 * d))]
+            + [pl.BlockSpec((1, 1, 128), lambda i, _: (i, 0, 0))] * 2,
             scratch_shapes=[
                 pltpu.VMEM((d, 3 * d), BF),
                 pltpu.VMEM((d, 128), BF),
                 pltpu.SemaphoreType.DMA((2,)),
             ],
         ),
-        out_shape=[SDS((t, d), BF)] * 4 + [SDS((VECS, d), F32), SDS((1, 4 * d), F32)],
+        out_shape=[SDS((t, d), BF)] * 4
+        + [SDS((VECS, d), F32), SDS((1, 4 * d), F32)]
+        + [SDS((t // tb, 1, 128), F32)] * 2,
         compiler_params=params(),
         cost_estimate=cost(6 * t * d * d, t * d * 8 + d * d * 6),
         name="qkv",
     )(idx, x, *pieces)
 
 
-def attend_kernel(tag_ref, q_ref, k_ref, v_ref, *refs, qb):
+def attend_kernel(tag_ref, qn_ref, kn_ref, q_ref, k_ref, v_ref, *refs, qb, first):
     o_ref, l_ref = refs[-2:]
     r = pl.program_id(0)
     length = q_ref.shape[0]
     low = lax.broadcasted_iota(jnp.int32, (1, 128), 1) < 64
 
-    def block(qs, qn, ks, kn):
+    steps = qn_ref.shape[0] // tag_ref.shape[0]
+    safe = True
+    for h in range(2):
+        head = 2 * (pl.program_id(1) + first) + h
+        top = []
+        for n_ref in (qn_ref, kn_ref):
+            most = n_ref[r * steps, 0, head]
+            for i in range(1, steps):
+                most = jnp.maximum(most, n_ref[r * steps + i, 0, head])
+            top.append(most)
+        safe = jnp.logical_and(safe, top[0] * top[1] <= SAFE_SCORE**2)
+
+    def block(qs, qn, ks, kn, plain):
         q = q_ref[pl.ds(qs, qn), :]
         k = k_ref[pl.ds(ks, kn), :]
         v = v_ref[pl.ds(ks, kn), :]
@@ -234,48 +257,55 @@
             qm = jnp.where(sel, q, jnp.asarray(0, BF))
             vm = jnp.where(sel, v, jnp.asarray(1, BF))
             s = dg(qm, k, NT)
-            m = jnp.max(s, axis=1, keepdims=True)
-            outs.append((dg(jnp.exp2(s - m).astype(BF), vm, NN), m))
+            if plain:
+                outs.append((dg(jnp.exp2(s).astype(BF), vm, NN), 0.0))
+            else:
+                m = jnp.max(s, axis=1, keepdims=True)
+                outs.append((dg(jnp.exp2(s - m).astype(BF), vm, NN), m))
         (a, ma), (b, mb) = outs
         acc = jnp.where(low, a, b)
         total = pltpu.roll(jnp.where(low, b, a), 64, 1)
         o_ref[pl.ds(qs, qn), :] = (acc / total).astype(o_ref.dtype)
-        lse = (jnp.where(low, ma, mb) + jnp.log2(total)).T
+        lse = jnp.log2(total) if plain else jnp.where(low, ma, mb) + jnp.log2(total)
+        lse = lse.T
         l_ref[0, 0, 0:1, pl.ds(qs, qn)] = lse[0:1]
         l_ref[0, 0, 1:2, pl.ds(qs, qn)] = lse[64:65]
 
-    @pl.when(tag_ref[r] == 0)
-    def _():
-        for i in range(length // qb):
-            block(i * qb, qb, 0, length)
-
-    @pl.when(tag_ref[r] != 0)
-    def _():
-        c = length // 4
-        for i in range(4):
-            block(i * c, c, i * c, c)
-
-
-def attend(tag, q, k, v, first, pairs, before=(), qb=512):
+    for plain in (True, False):
+        chosen = safe if plain else jnp.logical_not(safe)
+
+        @pl.when(jnp.logical_and(tag_ref[r] == 0, chosen))
+        def _(plain=plain):
+            for i in range(length // qb):
+                block(i * qb, qb, 0, length, plain)
+
+        @pl.when(jnp.logical_and(tag_ref[r] != 0, chosen))
+        def _(plain=plain):
+            c = length // 4
+            for i in range(4):
+                block(i * c, c, i * c, c, plain)
+
+
+def attend(tag, qn, kn, q, k, v, first, pairs, before=(), qb=512):
     t, d = q.shape
     rows = tag.shape[0]
     length = t // rows
     blk = pl.BlockSpec((length, 128), lambda r, p, _: (r, p + first))
     lse = pl.BlockSpec((1, 1, 2, length), lambda r, p, _: (r, p + first, 0, 0))
     return pl.pallas_call(
-        functools.partial(attend_kernel, qb=qb),
+        functools.partial(attend_kernel, qb=qb, first=first),
         grid_spec=pltpu.PrefetchScalarGridSpec(
             num_scalar_prefetch=1,
             grid=(rows, pairs),
-            in_specs=[blk] * 3 + [ANY] * len(before),
+            in_specs=[pl.BlockSpec(memory_space=pltpu.SMEM)] * 2 + [blk] * 3 + [ANY] * len(before),
             out_specs=[blk, lse],
         ),
         out_shape=[SDS((t, d), BF), SDS((rows, d // 128, 2, length), F32)],
-        input_output_aliases={4: 0, 5: 1} if before else {},
+        input_output_aliases={6: 0, 7: 1} if before else {},
         compiler_params=params(2),
         cost_estimate=cost(2048 * t * length * pairs, t * d * 8, t * length * 12),
         name="attend",
-    )(tag, q, k, v, *before)
+    )(tag, qn, kn, q, k, v, *before)
 
 
 ODDS = (2.3021649, 1.05007451e-1, -2.545477e-4, -1.0560537e-4, 4.093017e-6)
@@ -469,7 +499,7 @@
 
 
 def grad_mlp_kernel(
-    idx_ref, g_ref, dm_ref, h2_any, du_ref, down_own, down_other, up_own, up_other, h2_ref, sem
+    idx_ref, g_ref, dm_ref, h2_any, du_ref, u, down_own, down_other, up_own, up_other, bias_ref, h2_ref, sem, *, rows
 ):
     i = pl.program_id(0)
     steps = pl.num_programs(0) // 2
@@ -485,13 +515,18 @@
     @pl.when(i < steps)
     def _():
         split_halves(idx_ref[1], dg(g_ref[...], dm_ref[...], TN).astype(BF), down_own, down_other)
+        d = dm_ref.shape[1]
+        wide = u.shape[1] // d
+        for j in range(wide):
+            parts = [u[:, (s * wide + j) * rows : (s * wide + j + 1) * rows] for s in range(d // rows)]
+            bias_ref[j : j + 1, :] = jnp.concatenate(parts, axis=1)
 
     @pl.when(i >= steps)
     def _():
         split_halves(idx_ref[1], dg(h2_ref[...], du_ref[...], TN).astype(BF), up_own, up_other)
 
 
-def grad_mlp(idx, g, dm, h2, du):
+def grad_mlp(idx, g, dm, h2, du, gbu, rows):
     t, ff = g.shape
     d = dm.shape[1]
     steps = ff // d
@@ -503,7 +538,7 @@
         return jnp.maximum(i - steps, 0)
 
     return pl.pallas_call(
-        grad_mlp_kernel,
+        functools.partial(grad_mlp_kernel, rows=rows),
         grid_spec=pltpu.PrefetchScalarGridSpec(
             num_scalar_prefetch=1,
             grid=(2 * steps,),
@@ -512,16 +547,20 @@
                 whole((t, d)),
                 ANY,
                 pl.BlockSpec((t, d), lambda i, _: (0, up(i))),
+                whole(gbu.shape),
             ],
             out_specs=[pl.BlockSpec((d, d // 2), lambda i, _: (down(i), 0))] * 2
-            + [pl.BlockSpec((d, d // 2), lambda i, _: (0, up(i)))] * 2,
+            + [pl.BlockSpec((d, d // 2), lambda i, _: (0, up(i)))] * 2
+            + [fixed((steps, d))],
             scratch_shapes=[pltpu.VMEM((t, d), BF), pltpu.SemaphoreType.DMA],
         ),
-        out_shape=[pltpu.HBM((ff, d // 2), BF)] * 2 + [pltpu.HBM((d, ff // 2), BF)] * 2,
+        out_shape=[pltpu.HBM((ff, d // 2), BF)] * 2
+        + [pltpu.HBM((d, ff // 2), BF)] * 2
+        + [SDS((steps, d), F32)],
         compiler_params=params(),
         cost_estimate=cost(6 * t * ff * d, 4 * t * (ff + d) + 4 * ff * d),
         name="grad_mlp",
-    )(idx, g, dm, h2, du)
+    )(idx, g, dm, h2, du, gbu)
 
 
 def attend_back_kernel(
@@ -653,9 +692,9 @@
     )(idx, h1, dq, dk, dv, *([recv] * own))
 
 
-def tokens_back_kernel(idx_ref, x_ref, vt_ref, dx2_ref, dq_ref, dk_ref, dv_ref, *refs):
-    pieces = refs[:-4]
-    tg_ref, s_ref, w_ref, sem = refs[-4:]
+def tokens_back_kernel(idx_ref, me_ref, x_ref, vt_ref, dx2_ref, dq_ref, dk_ref, dv_ref, a_ref, u_ref, *refs, q):
+    pieces = refs[: -5 - q]
+    tg_ref, *outs, s_ref, table_ref, w_ref, sem = refs[-5 - q :]
     d = x_ref.shape[1]
 
     @pl.when(pl.program_id(0) == 0)
@@ -680,23 +719,43 @@
     m2 = jnp.sum(dz * xh, axis=-1, keepdims=True) * (1.0 / d)
     tg_ref[...] = dx2_ref[...] + r * (dz - m1 - xh * m2)
 
-
-def tokens_back(idx, dq, dk, dv, x, vt, dx2, pieces, tb=512):
+    @pl.when(pl.program_id(0) == pl.num_programs(0) - 1)
+    def _():
+        rows = outs[0].shape[1]
+        wide = u_ref.shape[0]
+        lines = [s_ref[0:4, :], a_ref[3:4, :], a_ref[1:3, :], a_ref[0:1, :], u_ref[...]]
+        table_ref[...] = jnp.concatenate(lines + [jnp.zeros((120 - wide, d), F32)], axis=0).T
+        for e in range(q):
+            for z in range(4):
+                s = z * q + lax.bitwise_xor(me_ref[0] % q, jnp.int32(e))
+                outs[e][z] = table_ref[pl.ds(pl.multiple_of(s * rows, 8), rows), :].astype(BF)
+
+
+def tokens_back(idx, me, dq, dk, dv, x, vt, dx2, s_mlp, bias, pieces, n, tb=512):
     t, d = x.shape
+    q = n // 4
     return pl.pallas_call(
-        tokens_back_kernel,
+        functools.partial(tokens_back_kernel, q=q),
         grid_spec=pltpu.PrefetchScalarGridSpec(
-            num_scalar_prefetch=1,
+            num_scalar_prefetch=2,
             grid=(t // tb,),
-            in_specs=[rows_of(tb, d), whole(vt.shape)] + [rows_of(tb, d)] * 4 + [ANY] * len(pieces),
-            out_specs=[rows_of(tb, d), fixed((8, d))],
-            scratch_shapes=[pltpu.VMEM((d, 3 * d), BF), pltpu.SemaphoreType.DMA],
+            in_specs=[rows_of(tb, d), whole(vt.shape)]
+            + [rows_of(tb, d)] * 4
+            + [whole(s_mlp.shape), whole(bias.shape)]
+            + [ANY] * len(pieces),
+            out_specs=[rows_of(tb, d)] + [fixed((4, d // n, 128))] * q,
+            scratch_shapes=[
+                pltpu.VMEM((8, d), F32),
+                pltpu.VMEM((d, 128), F32),
+                pltpu.VMEM((d, 3 * d), BF),
+                pltpu.SemaphoreType.DMA,
+            ],
         ),
-        out_shape=[SDS((t, d), F32), SDS((8, d), F32)],
+        out_shape=[SDS((t, d), F32)] + [pltpu.HBM((4, d // n, 128), BF)] * q,
         compiler_params=params(),
         cost_estimate=cost(9 * t * d * d, t * d * 16 + d * d * 6),
         name="tokens_back",
-    )(idx, x, vt, dx2, dq, dk, dv, *pieces)
+    )(idx, me, x, vt, dx2, dq, dk, dv, s_mlp, bias, *pieces)
 
 
 def hop(x, groups):
@@ -767,6 +826,7 @@
 
 
 def sum_qkv_kernel(idx_ref, *refs, q):
+    outs = refs[2 * q + 1 :]
     for d in range(4):
         at = lax.bitwise_xor(idx_ref[0] // q, jnp.int32(d))
         start = 0
@@ -775,28 +835,32 @@
             for x in parts[1:]:
                 total = total + x[at].astype(F32)
             w = total.shape[1]
-            refs[2 * q + d][:, start : start + w] = total.astype(BF)
+            outs[d][:, start : start + w] = total.astype(BF)
             start += w
-
-
-def sum_qkv(idx, far, vecs, n):
+    last = refs[2 * q]
+    outs[4][...] = (
+        last[0].astype(F32) + last[1].astype(F32) + last[2].astype(F32) + last[3].astype(F32)
+    ).astype(BF)
+
+
+def sum_qkv(idx, far, vecs, last, n):
     _, rows, w = far[0].shape
     width = w + vecs[0].shape[2]
-    ops = list(far) + list(vecs)
-    near = pl.pallas_call(
+    ops = list(far) + list(vecs) + [last]
+    *near, total = pl.pallas_call(
         functools.partial(sum_qkv_kernel, q=n // 4),
         grid_spec=pltpu.PrefetchScalarGridSpec(
             num_scalar_prefetch=1,
             grid=(1,),
             in_specs=[whole(x.shape) for x in ops],
-            out_specs=[fixed((rows, width))] * 4,
+            out_specs=[fixed((rows, width))] * 4 + [fixed(last.shape[1:])],
         ),
-        out_shape=[pltpu.HBM((rows, width), BF)] * 4,
+        out_shape=[pltpu.HBM((rows, width), BF)] * 4 + [pltpu.HBM(last.shape[1:], BF)],
         compiler_params=params(),
         cost_estimate=cost(n * rows * width, n * rows * width * 3),
         name="sum_qkv",
     )(idx, *ops)
-    return near
+    return near, total
 
 
 def reduce_last(near, n, m):
@@ -812,44 +876,6 @@
         total = total + lax.ppermute(total.astype(BF), "dp", [(i, i ^ b) for i in range(m)]).astype(F32)
         b *= 2
     return total
-
-
-def vec_table_kernel(idx_ref, a, c, u, *refs, q):
-    table_ref = refs[q]
-    d = a.shape[1]
-    rows = refs[0].shape[1]
-    wide = u.shape[1] // d
-    bias = [
-        jnp.concatenate(
-            [u[:, (s * wide + j) * rows : (s * wide + j + 1) * rows] for s in range(4 * q)], axis=1
-        )
-        for j in range(wide)
-    ]
-    lines = [c[0:4, :], a[3:4, :], a[1:3, :], a[0:1, :]] + bias + [jnp.zeros((120 - wide, d), F32)]
-    table_ref[...] = jnp.concatenate(lines, axis=0).T
-    for e in range(q):
-        for z in range(4):
-            s = z * q + lax.bitwise_xor(idx_ref[0] % q, jnp.int32(e))
-            refs[e][z] = table_ref[pl.ds(pl.multiple_of(s * rows, 8), rows), :].astype(BF)
-
-
-def vec_table(idx, s_mlp, s_tok, gbu, n):
-    d = s_mlp.shape[1]
-    q = n // 4
-    return pl.pallas_call(
-        functools.partial(vec_table_kernel, q=q),
-        grid_spec=pltpu.PrefetchScalarGridSpec(
-            num_scalar_prefetch=1,
-            grid=(1,),
-            in_specs=[whole(s_mlp.shape), whole(s_tok.shape), whole(gbu.shape)],
-            out_specs=[fixed((4, d // n, 128))] * q,
-            scratch_shapes=[pltpu.VMEM((d, 128), F32)],
-        ),
-        out_shape=[SDS((4, d // n, 128), BF)] * q,
-        compiler_params=params(),
-        cost_estimate=cost(d * 128, d * 1024),
-        name="vec_table",
-    )(idx, s_mlp, s_tok, gbu)
 
 
 def local(
@@ -910,7 +936,7 @@
     else:
         pieces_a = settle(own_a + swap_a[:1] + [swap_a[1][e] for e in range(q - 1)], f ^ everyone, c, n)
     near_b = after(near_b, own_a[1:])
-    qh, kh, vh, h1, vt, bu = qkv(use, after(tokens, near_b), pieces_a)
+    qh, kh, vh, h1, vt, bu, qn, kn = qkv(use, after(tokens, near_b), pieces_a)
     pairs = d // 128
     early = pairs * 2 // 3
     cut = (d + ff) // 2
@@ -919,7 +945,7 @@
         x1, y2 = after((xor_pp(x, 1, n), xor_pp(y, 2, n)), vt)
         x2, y1 = xor_pp(x, 2, n), xor_pp(y, 1, n)
         x3, y3 = xor_pp(x1, 2, n), xor_pp(y2, 1, n)
-        part = attend(sensor_tag, after(qh, x1, y2), kh, vh, 0, early)
+        part = attend(sensor_tag, qn, kn, after(qh, x1, y2), kh, vh, 0, early)
         side = [near_b] + after([x1, x2, x3, y1, y2, y3], part[0])
         pieces_b = []
         for x in side:
@@ -930,7 +956,7 @@
         side = settle(
             far_b + [core_swap(x, m) for x in far_b], everyone // q * q + (everyone ^ f) % q, c, n, wide
         )
-        part = attend(sensor_tag, qh, kh, vh, 0, early)
+        part = attend(sensor_tag, qn, kn, qh, kh, vh, 0, early)
         pieces_b = [side[0], side[4]]
         for e in range(1, 4):
             pieces_b += [side[e][..., :cut], side[4 + e][..., :cut]]
@@ -938,7 +964,7 @@
             pieces_b += [side[e][..., cut:], side[4 + e][..., cut:]]
         gate = far_b
     returned = lax.all_to_all(after(cast, gate), "fsdp", split_axis=0, concat_axis=0, tiled=True)
-    mixed, lse = attend(sensor_tag, qh, kh, vh, early, pairs - early, part)
+    mixed, lse = attend(sensor_tag, qn, kn, qh, kh, vh, early, pairs - early, part)
 
     x2, active, slope, y = mlp(use, tokens, mixed, vt, bu, pieces_b)
     sent = permute(owner_order, y)
@@ -949,7 +975,7 @@
         use, owner_order, returned, slope, x2, mixed, vt, pieces_b
     )
     out_recv = core_swap(out_other, m)
-    down_own, down_other, up_own, up_other = grad_mlp(idx, active, dm, h2, du)
+    down_own, down_other, up_own, up_other, bias = grad_mlp(idx, active, dm, h2, du, gbu, rows)
     down_recv = core_swap(down_other, m)
     up_recv = core_swap(up_other, m)
     part = attend_back(sensor_tag, qh, kh, vh, after(do, up_own, encoded), mixed, lse, 0, 1)
@@ -967,13 +993,14 @@
     far_a = grad_qkv(idx, after(h1, near_b), *dj, qkv_recv, n)
     dj = after(dj, far_a[0])
     far_a = spread(far_a, n)
-    tokens_grad, s_tok = tokens_back(use, *dj, tokens, vt, dx2, pieces_a)
+    tokens_grad, *far_v = tokens_back(use, idx, *dj, tokens, vt, dx2, s_mlp, bias, pieces_a, n)
     far_a, total_b = after((far_a, total_b), tokens_grad)
-    total_b = over_pairs(jnp.sum(total_b.astype(F32), axis=0), m).astype(BF)
+    far_v = spread([far_v[0]] + after(far_v[1:], far_a), n)
+
+    near_a, total_b = sum_qkv(idx, far_a, far_v, total_b, n)
+    if m > 2:
+        total_b = over_pairs(total_b.astype(F32), m).astype(BF)
     other_b = core_swap(total_b, m)
-    far_v = spread(vec_table(idx, s_mlp, s_tok, after(gbu, far_a), n), n)
-
-    near_a = sum_qkv(idx, after(far_a, total_b), far_v, n)
     encoded = after(encoded, near_a[0]).astype(F32)
     near_a = [near_a[0]] + [xor_pp(near_a[i], i * q, n) for i in range(1, 4)]
     def both(mine, other):

time: 456 us -> 450 us (0.987)
  Pallas kernels: 320 us -> 259 us
  starting transfers between devices: 54.5 us -> 98.1 us
  waiting for transfers between devices: 39 us -> 54.6 us
    pallas_call x2, Pallas kernels: 72 us -> 34.6 us  [attend_back(): pl.pallas_call(functools.partial(attend_back_kernel, kb=kb, qb=qb), grid_...]
    pallas_call x5 -> x4, Pallas kernels: 92.5 us -> 66.6 us  [the longest x1 27.7 us: grad_mlp(): pl.pallas_call(functools.partial(grad_mlp_kernel, rows=rows), grid_spec=p...]
    ppermute x15, starting transfers between devices: 3.27 us -> 24 us  [core_swap(): return lax.ppermute(x, 'dp', [(i, i ^ 1) for i in range(m)])]
    all_to_all x2, starting transfers between devices: 9.94 us -> 26 us  [hop(): lax.all_to_all(x, 'fsdp', split_axis=0, concat_axis=0, tiled=True, axis_i...]
    ppermute x24, waiting for transfers between devices: 28 us -> 43.3 us  [xor_pp(): return lax.ppermute(x, 'fsdp', [(i, i ^ b) for i in range(n)])]
    all_to_all x1, starting transfers between devices: 5.52 us -> 12.4 us  [local(): lax.all_to_all(sent, 'fsdp', split_axis=0, concat_axis=0, tiled=True)]
  transfers between devices with their start and end apart: 43 -> 43, of which waited for: 15 -> 18; matrix products, arithmetic and copies ran while one was open for 4% -> 4% of each run, Pallas kernels for 70% -> 56%
where the time goes in v1:
time: 450 us; the launch traced here: 444 us
  Pallas kernels  259 us (58%)
  starting transfers between devices  98.1 us (22%)
  waiting for transfers between devices  54.6 us (12%)
  other arithmetic  17 us (4%)
  local copies, waits for them, and re-layouts  13.9 us (3%)
    pallas_call x1, Pallas kernels, mlp_back(): pl.pallas_call(functools.partial(mlp_back_kernel, fc=fc), grid_spec=pltpu...  50 us
    pallas_call x1, Pallas kernels, mlp(): pl.pallas_call(functools.partial(mlp_kernel, fc=fc), grid_spec=pltpu.Pref...  44.5 us
    ppermute x24, waiting for transfers between devices, xor_pp(): return lax.ppermute(x, 'fsdp', [(i, i ^ b) for i in range(n)])  43.3 us
    pallas_call x2, Pallas kernels, attend_back(): pl.pallas_call(functools.partial(attend_back_kernel, kb=kb, qb=qb), grid_...  34.6 us
    ppermute x24, starting transfers between devices, xor_pp(): return lax.ppermute(x, 'fsdp', [(i, i ^ b) for i in range(n)])  30.7 us
    pallas_call x1, Pallas kernels, grad_mlp(): pl.pallas_call(functools.partial(grad_mlp_kernel, rows=rows), grid_spec=p...  27.7 us
    all_to_all x2, starting transfers between devices, hop(): lax.all_to_all(x, 'fsdp', split_axis=0, concat_axis=0, tiled=True, axis_i...  26 us
    ppermute x15, starting transfers between devices, core_swap(): return lax.ppermute(x, 'dp', [(i, i ^ 1) for i in range(m)])  24 us
  transfers between devices with their start and end apart: 43, of which 18 were waited for; matrix products, arithmetic and copies ran while one was open for 4% of the time, Pallas kernels for 56%

profile of v1, /device:TPU:0, one launch (start us, length us, event | category | flops | bytes accessed | tf_op | source)
XLA Modules:
  0.0 444.3 jit_solution(9485981694775049466)
XLA Ops:
  18.5 5.4 %all-to-all-start = ((bf16[4,48,3456]{2,1,0:T(8,128)(2,1)}), bf16[4,48,3456]{2,1,0:T(8,128)(2,1)S(1)}, u32[]{:S(2)}, u32[]{:S(2)}) async-start(bf16[4,48,3456]{2,1,0:T(8,128)(2,1)} %broadcast_in_dim.2), calls=%async_computation | async-start | bytes 2654208 | tf_op jit(solution)/shard_map/all_to_all | solution.py:762
  27.3 4.8 %convert_element_type.39 = bf16[2048,768]{1,0:T(8,128)(2,1)} convert(f32[2048,768]{1,0:T(8,128)} %param.33) | non-fusion elementwise | flops 1572864 | bytes 9437184 | tf_op jit(solution)/shard_map/convert_element_type | solution.py:931
  32.1 6.8 %collective-permute-done.5.refs_3_ = bf16[4,48,1280]{2,1,0:T(8,128)(2,1)S(1)} collective-permute-done((bf16[4,48,1280]{2,1,0:T(8,128)(2,1)S(1)}, bf16[4,48,1280]{2,1,0:T(8,128)(2,1)S(1)}, u32[]{:S(2)}, u32[]{:S(2)}) %collective-permute-start.5) | collective-permute-done | bytes 491552 | tf_op jit(solution)/shard_map/ppermute | solution.py:65
  38.9 9.2 %collective-permute-done.4.refs_2_ = bf16[4,48,1280]{2,1,0:T(8,128)(2,1)S(1)} collective-permute-done((bf16[4,48,1280]{2,1,0:T(8,128)(2,1)S(1)}, bf16[4,48,1280]{2,1,0:T(8,128)(2,1)S(1)}, u32[]{:S(2)}, u32[]{:S(2)}) %collective-permute-start.4) | collective-permute-done | bytes 491552 | tf_op jit(solution)/shard_map/ppermute | solution.py:65
  50.4 5.3 %all-to-all-done.refs_0_ = bf16[4,48,3456]{2,1,0:T(8,128)(2,1)S(1)} async-done(((bf16[4,48,3456]{2,1,0:T(8,128)(2,1)}), bf16[4,48,3456]{2,1,0:T(8,128)(2,1)S(1)}, u32[]{:S(2)}, u32[]{:S(2)}) %all-to-all-start) | async-done | bytes 1327136 | tf_op jit(solution)/shard_map/all_to_all | solution.py:762
  63.7 16.2 %qkv.1 = (bf16[2048,768]{1,0:T(8,128)(2,1)}, bf16[2048,768]{1,0:T(8,128)(2,1)}, bf16[2048,768]{1,0:T(8,128)(2,1)}, bf16[2048,768]{1,0:T(8,128)(2,1)}, f32[16,768...) custom-call(s32[2]{0:T(128)} %pad_add_fusion.idx_ref.me_ref, ...), custom_call_target="tpu_custom_call" | custom-call | flops 7077888 | bytes 15744 | tf_op jit(solution)/shard_map/qkv/pallas_call | solution.py:208
  82.6 12.5 %attend.2 = (bf16[2048,768]{1,0:T(8,128)(2,1)}, f32[2,6,2,1024]{3,2,1,0:T(2,128)}) custom-call(s32[2]{0:T(128)} %tag_ref.7, f32[4,1,128]{2,1,0:T(1,128)} %get-tuple-element.121.qn_ref, f32[4,1,128]{2,1,0:T(1,128)} %get-tuple-element.122.kn_ref, bf16[2048,768]{1,0:T(8,128)(2,1)} %get-tuple-element.129.q_ref, bf16[2048,768]{1,0:T(8,128)(2,1)} %get-tuple-element.124.k_ref, ...), custom_call_target="tpu_custom_call" | custom-call | flops 16777216 | bytes 12288 | tf_op jit(solution)/shard_map/attend/pallas_call | solution.py:295
  97.1 11.5 %collective-permute-done.14.refs_12_ = bf16[4,48,1536]{2,1,0:T(8,128)(2,1)S(1)} collective-permute-done((bf16[4,48,1536]{2,1,0:T(8,128)(2,1)}, bf16[4,48,1536]{2,1,0:T(8,128)(2,1)S(1)}, u32[]{:S(2)}, u32[]{:S(2)}) %collective-permute-start.14) | collective-permute-done | bytes 589856 | tf_op jit(solution)/shard_map/ppermute | solution.py:65
  109.4 5.0 %all-to-all-start.2 = ((bf16[16,128,768]{2,1,0:T(8,128)(2,1)}), bf16[16,128,768]{2,1,0:T(8,128)(2,1)}, u32[]{:S(2)}, u32[]{:S(2)}) async-start(bf16[16,128,768]{2,1,0:T(8,128)(2,1)} %bitcast.33), calls=%async_computation.2 | async-start | bytes 6291456 | tf_op jit(solution)/shard_map/all_to_all | solution.py:966
  119.5 7.4 %attend.3 = (bf16[2048,768]{1,0:T(8,128)(2,1)}, f32[2,6,2,1024]{3,2,1,0:T(2,128)}) custom-call(s32[2]{0:T(128)} %tag_ref.7, f32[4,1,128]{2,1,0:T(1,128)} %get-tuple-element.121.qn_ref, f32[4,1,128]{2,1,0:T(1,128)} %get-tuple-element.122.kn_ref, bf16[2048,768]{1,0:T(8,128)(2,1)} %get-tuple-element.129.q_ref, ...), custom_call_target="tpu_custom_call", output_to_operand_aliasing={{0}: (6, {}), {1}: (7, {})} | custom-call | flops 8388608 | bytes 12288 | tf_op jit(solution)/shard_map/attend/pallas_call | solution.py:295
  128.6 44.5 %mlp.1 = (f32[2048,768]{1,0:T(8,128)}, bf16[2048,3072]{1,0:T(8,128)(2,1)}, bf16[2048,3072]{1,0:T(8,128)(2,1)}, bf16[2048,768]{1,0:T(8,128)(2,1)}) custom-call(s32[2]{0:T(128)} %pad_add_fusion.idx_ref.me_ref, bf16[2048,768]{1,0:T(8,128)(2,1)} %x_ref.4, bf16[2048,768]{1,0:T(8,128)(2,1)} %get-tuple-element.132.o_ref, f32[16,768]{1,0:T(8,128)} %get-tuple-element.126.vt_ref, ...), custom_call_target="tpu_custom_call" | custom-call | flops 42467328 | bytes 49152 | tf_op jit(solution)/shard_map/mlp/pallas_call | solution.py:360
  173.1 11.1 %permute.1 = bf16[2048,768]{1,0:T(8,128)(2,1)} custom-call(s32[1,2048]{1,0:T(1,128)} %ord_ref.3, bf16[2048,768]{1,0:T(8,128)(2,1)} %get-tuple-element.140.y_ref), custom_call_target="tpu_custom_call" | custom-call | flops 6291456 | bytes 6144 | tf_op jit(solution)/shard_map/permute/pallas_call | solution.py:390
  184.2 12.4 %all-to-all-start.1 = ((bf16[16,128,768]{2,1,0:T(8,128)(2,1)}), bf16[16,128,768]{2,1,0:T(8,128)(2,1)S(1)}, u32[]{:S(2)}, u32[]{:S(2)}) async-start(bf16[16,128,768]{2,1,0:T(8,128)(2,1)} %bitcast.31), calls=%async_computation.1 | async-start | bytes 6291456 | tf_op jit(solution)/shard_map/all_to_all | solution.py:971
  196.6 50.0 %mlp_back.1 = (bf16[2048,768]{1,0:T(8,128)(2,1)}, bf16[2048,3072]{1,0:T(8,128)(2,1)}, f32[2048,768]{1,0:T(8,128)}, bf16[2048,768]{1,0:T(8,128)(2,1)}, bf16[2048,...) custom-call(s32[2]{0:T(128)} %pad_add_fusion.idx_ref.me_ref, ...), custom_call_target="tpu_custom_call" | custom-call | flops 41287680 | bytes 55296 | tf_op jit(solution)/shard_map/mlp_back/pallas_call | solution.py:466
  246.6 27.7 %grad_mlp.1 = (bf16[3072,384]{1,0:T(8,128)(2,1)}, bf16[3072,384]{1,0:T(8,128)(2,1)}, bf16[768,1536]{1,0:T(8,128)(2,1)}, bf16[768,1536]{1,0:T(8,128)(2,1)}, f32[4,768]{1,0:T(4,128)}) custom-call(s32[2]{0:T(128)} %pad_add_fusion.idx_ref.me_ref, bf16[2048,3072]{1,0:T(8,128)(2,1)} %get-tuple-element.142.g_ref, bf16[2048,768]{1,0:T(8,128)(2,1)} %get-tuple-element.147.dm_ref, ...), custom_call_target="tpu_custom_call" | custom-call | flops 28311552 | bytes 39936 | tf_op jit(solution)/shard_map/grad_mlp/pallas_call | solution.py:540
  275.6 7.8 %attend_back.2 = (bf16[2048,768]{1,0:T(8,128)(2,1)}, bf16[2048,768]{1,0:T(8,128)(2,1)}, bf16[2048,768]{1,0:T(8,128)(2,1)}) custom-call(s32[2]{0:T(128)} %tag_ref.7, bf16[2048,768]{1,0:T(8,128)(2,1)} %get-tuple-element.129.q_ref, bf16[2048,768]{1,0:T(8,128)(2,1)} %get-tuple-element.124.k_ref, bf16[2048,768]{1,0:T(8,128)(2,1)} %get-tuple-element.125.v_ref, ...), custom_call_target="tpu_custom_call" | custom-call | flops 10485760 | bytes 24576 | tf_op jit(solution)/shard_map/attend_back/pallas_call | solution.py:629
  283.8 7.4 %sum_cores.1 = (bf16[4,48,3456]{2,1,0:T(8,128)(2,1)}, bf16[4,48,3456]{2,1,0:T(8,128)(2,1)}, bf16[4,48,3456]{2,1,0:T(8,128)(2,1)}, bf16[4,48,3456]{2,1,0:T(8,128)(2,1)}) custom-call(s32[2]{0:T(128)} %pad_add_fusion.idx_ref.me_ref, bf16[16,48,1536]{2,1,0:T(8,128)(2,1)} %bitcast.38, bf16[16,48,1536]{2,1,0:T(8,128)(2,1)} %bitcast.23.refs_1_, ...), custom_call_target="tpu_custom_call" | custom-call | flops 2592 | bytes 15552 | tf_op jit(solution)/shard_map/sum_cores/pallas_call | solution.py:787
  294.6 26.8 %attend_back.3 = (bf16[2048,768]{1,0:T(8,128)(2,1)}, bf16[2048,768]{1,0:T(8,128)(2,1)}, bf16[2048,768]{1,0:T(8,128)(2,1)}) custom-call(s32[2]{0:T(128)} %tag_ref.7, bf16[2048,768]{1,0:T(8,128)(2,1)} %get-tuple-element.129.q_ref, bf16[2048,768]{1,0:T(8,128)(2,1)} %get-tuple-element.124.k_ref, ...), custom_call_target="tpu_custom_call", output_to_operand_aliasing={{0}: (7, {}), {1}: (8, {}), {2}: (9, {})} | custom-call | flops 52428800 | bytes 24576 | tf_op jit(solution)/shard_map/attend_back/pallas_call | solution.py:629
  321.4 9.7 %grad_qkv_other.1 = bf16[768,1152]{1,0:T(8,128)(2,1)} custom-call(s32[2]{0:T(128)} %pad_add_fusion.idx_ref.me_ref, bf16[2048,768]{1,0:T(8,128)(2,1)} %get-tuple-element.179.h_any, bf16[2048,768]{1,0:T(8,128)(2,1)} %get-tuple-element.185.dq_any.dq_ref, bf16[2048,768]{1,0:T(8,128)(2,1)} %get-tuple-element.186.dk_any.dk_ref, ...), custom_call_target="tpu_custom_call" | custom-call | flops 3538944 | bytes 9216 | tf_op jit(solution)/shard_map/grad_qkv_other/pallas_call | solution.py:678
  331.1 20.9 %collective-permute-start.27 = (bf16[768,1152]{1,0:T(8,128)(2,1)}, bf16[768,1152]{1,0:T(8,128)(2,1)}, u32[]{:S(2)}, u32[]{:S(2)}) collective-permute-start(bf16[768,1152]{1,0:T(8,128)(2,1)} %grad_qkv_other.1), channel_id=1, source_target_pairs={{0,16},{16,0},{1,17},{17,1},{2,18},{18,2},{3,19},{19,3},{4,20},{20... | collective-permute-start | bytes 5308424 | tf_op jit(solution)/shard_map/ppermute | solution.py:69
  358.0 20.6 %all-to-all-start.3 = ((bf16[4,48,3456]{2,1,0:T(8,128)(2,1)}), bf16[4,48,3456]{2,1,0:T(8,128)(2,1)}, u32[]{:S(2)}, u32[]{:S(2)}) async-start(bf16[4,48,3456]{2,1,0:T(8,128)(2,1)} %sum_parts.1), calls=%async_computation.3 | async-start | bytes 2654208 | tf_op jit(solution)/shard_map/all_to_all | solution.py:762
  378.6 11.4 %grad_qkv_own.1 = (bf16[4,48,1152]{2,1,0:T(8,128)(2,1)}, bf16[4,48,1152]{2,1,0:T(8,128)(2,1)}, bf16[4,48,1152]{2,1,0:T(8,128)(2,1)}, bf16[4,48,1152]{2,1,0:T(8,128)(2,1)}) custom-call(s32[2]{0:T(128)} %pad_add_fusion.idx_ref.me_ref, bf16[2048,768]{1,0:T(8,128)(2,1)} %get-tuple-element.179.h_any, bf16[2048,768]{1,0:T(8,128)(2,1)} %get-tuple-element.185.dq_any.dq_ref, ...), custom_call_target="tpu_custom_call" | custom-call | flops 3538944 | bytes 9216 | tf_op jit(solution)/shard_map/grad_qkv_own/pallas_call | solution.py:678
  393.9 19.1 %tokens_back.1 = (f32[2048,768]{1,0:T(8,128)}, bf16[4,48,128]{2,1,0:T(8,128)(2,1)}, bf16[4,48,128]{2,1,0:T(8,128)(2,1)}, bf16[4,48,128]{2,1,0:T(8,128)(2,1)}, bf16[4,48,128]{2,1,0:T(8,128)(2,1)}) custom-call(s32[2]{0:T(128)} %pad_add_fusion.idx_ref.me_ref, s32[2]{0:T(128)} %pad_add_fusion.idx_ref.me_ref, bf16[2048,768]{1,0:T(8,128)(2,1)} %x_ref.4, ...), custom_call_target="tpu_custom_call" | custom-call | flops 10616832 | bytes 28032 | tf_op jit(solution)/shard_map/tokens_back/pallas_call | solution.py:737
  435.2 4.9 %collective-permute-done.35 = bf16[48,1280]{1,0:T(8,128)(2,1)S(1)} collective-permute-done((bf16[48,1280]{1,0:T(8,128)(2,1)}, bf16[48,1280]{1,0:T(8,128)(2,1)S(1)}, u32[]{:S(2)}, u32[]{:S(2)}) %collective-permute-start.35) | collective-permute-done | bytes 122912 | tf_op jit(solution)/shard_map/ppermute | solution.py:65
  (167 shorter events, 84.9 us)
Async XLA Ops:
  18.5 37.3 %all-to-all-start = ((bf16[4,48,3456]{2,1,0:T(8,128)(2,1)}), bf16[4,48,3456]{2,1,0:T(8,128)(2,1)S(1)}, u32[]{:S(2)}, u32[]{:S(2)}) async-start(bf16[4,48,3456]{2,1,0:T(8,128)(2,1)} %broadcast_in_dim.2), calls=%async_computation | async-start | bytes 2654208 | tf_op jit(solution)/shard_map/all_to_all | solution.py:762
  23.8 15.1 %collective-permute-start.5 = (bf16[4,48,1280]{2,1,0:T(8,128)(2,1)S(1)}, bf16[4,48,1280]{2,1,0:T(8,128)(2,1)S(1)}, u32[]{:S(2)}, u32[]{:S(2)}) collective-permute-start(bf16[4,48,1280]{2,1,0:T(8,128)(2,1)S(1)} %pad_maximum_fusion.1.refs_0_), channel_id=1, source_target_pairs={{0,3},{1,2},{2,1},{3,0},{4,7},{5,6},{6,5},{7,4},{8,11},{9,10},{10,... | collective-permute-start | bytes 1474568 | tf_op jit(solution)/shard_map/ppermute | solution.py:65
  26.3 21.8 %collective-permute-start.4 = (bf16[4,48,1280]{2,1,0:T(8,128)(2,1)S(1)}, bf16[4,48,1280]{2,1,0:T(8,128)(2,1)S(1)}, u32[]{:S(2)}, u32[]{:S(2)}) collective-permute-start(bf16[4,48,1280]{2,1,0:T(8,128)(2,1)S(1)} %pad_maximum_fusion.1.refs_0_), channel_id=1, source_target_pairs={{0,2},{1,3},{2,0},{3,1},{4,6},{5,7},{6,4},{7,5},{8,10},{9,11},{10,... | collective-permute-start | bytes 1474568 | tf_op jit(solution)/shard_map/ppermute | solution.py:65
  26.8 21.4 %collective-permute-start.3 = (bf16[4,48,1280]{2,1,0:T(8,128)(2,1)S(1)}, bf16[4,48,1280]{2,1,0:T(8,128)(2,1)S(1)}, u32[]{:S(2)}, u32[]{:S(2)}) collective-permute-start(bf16[4,48,1280]{2,1,0:T(8,128)(2,1)S(1)} %pad_maximum_fusion.1.refs_0_), channel_id=1, source_target_pairs={{0,1},{1,0},{2,3},{3,2},{4,5},{5,4},{6,7},{7,6},{8,9},{9,8},{10,11... | collective-permute-start | bytes 1474568 | tf_op jit(solution)/shard_map/ppermute | solution.py:65
  50.4 12.2 %collective-permute-start.7 = (bf16[3,4,48,1280]{3,2,1,0:T(8,128)(2,1)}, bf16[3,4,48,1280]{3,2,1,0:T(8,128)(2,1)S(1)}, u32[]{:S(2)}, u32[]{:S(2)}) collective-permute-start(bf16[3,4,48,1280]{3,2,1,0:T(8,128)(2,1)} %pad_maximum_fusion), channel_id=1, source_target_pairs={{0,16},{16,0},{1,17},{17,1},{2,18},{18,2},{3,19},{19,3},{4,20},{20... | collective-permute-start | bytes 4423688 | tf_op jit(solution)/shard_map/ppermute | solution.py:69
  56.7 23.2 %collective-permute-start.8 = (bf16[4,48,1920]{2,1,0:T(8,128)(2,1)}, bf16[4,48,1920]{2,1,0:T(8,128)(2,1)}, u32[]{:S(2)}, u32[]{:S(2)}) collective-permute-start(bf16[4,48,1920]{2,1,0:T(8,128)(2,1)} %slice.178), channel_id=1, source_target_pairs={{0,1},{1,0},{2,3},{3,2},{4,5},{5,4},{6,7},{7,6},{8,9},{9,8},{10,11... | collective-permute-start | bytes 2211848 | tf_op jit(solution)/shard_map/ppermute | solution.py:65
  59.1 20.8 %collective-permute-start.9 = (bf16[4,48,1536]{2,1,0:T(8,128)(2,1)}, bf16[4,48,1536]{2,1,0:T(8,128)(2,1)}, u32[]{:S(2)}, u32[]{:S(2)}) collective-permute-start(bf16[4,48,1536]{2,1,0:T(8,128)(2,1)} %slice.179), channel_id=1, source_target_pairs={{0,2},{1,3},{2,0},{3,1},{4,6},{5,7},{6,4},{7,5},{8,10},{9,11},{10,... | collective-permute-start | bytes 1769480 | tf_op jit(solution)/shard_map/ppermute | solution.py:65
  61.2 35.9 %collective-permute-start.11 = (bf16[4,48,1920]{2,1,0:T(8,128)(2,1)}, bf16[4,48,1920]{2,1,0:T(8,128)(2,1)}, u32[]{:S(2)}, u32[]{:S(2)}) collective-permute-start(bf16[4,48,1920]{2,1,0:T(8,128)(2,1)} %slice.178), channel_id=1, source_target_pairs={{0,2},{1,3},{2,0},{3,1},{4,6},{5,7},{6,4},{7,5},{8,10},{9,11},{10,... | collective-permute-start | bytes 2211848 | tf_op jit(solution)/shard_map/ppermute | solution.py:65
  79.9 28.7 %collective-permute-start.12 = (bf16[4,48,1920]{2,1,0:T(8,128)(2,1)}, bf16[4,48,1920]{2,1,0:T(8,128)(2,1)S(1)}, u32[]{:S(2)}, u32[]{:S(2)}) collective-permute-start(bf16[4,48,1920]{2,1,0:T(8,128)(2,1)} %collective-permute-done.8.refs_2_), channel_id=1, source_target_pairs={{0,2},{1,3},{2,0},{3,1},{4,6},{5,7},{6,4},{7,5},{8,10},{9,11},{10,... | collective-permute-start | bytes 2211848 | tf_op jit(solution)/shard_map/ppermute | solution.py:65
  80.6 16.5 %collective-permute-start.13 = (bf16[4,48,1536]{2,1,0:T(8,128)(2,1)}, bf16[4,48,1536]{2,1,0:T(8,128)(2,1)}, u32[]{:S(2)}, u32[]{:S(2)}) collective-permute-start(bf16[4,48,1536]{2,1,0:T(8,128)(2,1)} %slice.179), channel_id=1, source_target_pairs={{0,1},{1,0},{2,3},{3,2},{4,5},{5,4},{6,7},{7,6},{8,9},{9,8},{10,11... | collective-permute-start | bytes 1769480 | tf_op jit(solution)/shard_map/ppermute | solution.py:65
  81.1 27.5 %collective-permute-start.14 = (bf16[4,48,1536]{2,1,0:T(8,128)(2,1)}, bf16[4,48,1536]{2,1,0:T(8,128)(2,1)S(1)}, u32[]{:S(2)}, u32[]{:S(2)}) collective-permute-start(bf16[4,48,1536]{2,1,0:T(8,128)(2,1)} %collective-permute-done.9.refs_10_), channel_id=1, source_target_pairs={{0,1},{1,0},{2,3},{3,2},{4,5},{5,4},{6,7},{7,6},{8,9},{9,8},{10,11... | collective-permute-start | bytes 1769480 | tf_op jit(solution)/shard_map/ppermute | solution.py:65
  109.4 74.8 %all-to-all-start.2 = ((bf16[16,128,768]{2,1,0:T(8,128)(2,1)}), bf16[16,128,768]{2,1,0:T(8,128)(2,1)}, u32[]{:S(2)}, u32[]{:S(2)}) async-start(bf16[16,128,768]{2,1,0:T(8,128)(2,1)} %bitcast.33), calls=%async_computation.2 | async-start | bytes 6291456 | tf_op jit(solution)/shard_map/all_to_all | solution.py:966
  115.0 11.9 %collective-permute-start.15 = (bf16[4,48,1920]{2,1,0:T(8,128)(2,1)}, bf16[4,48,1920]{2,1,0:T(8,128)(2,1)S(1)}, u32[]{:S(2)}, u32[]{:S(2)}) collective-permute-start(bf16[4,48,1920]{2,1,0:T(8,128)(2,1)} %collective-permute-done.8.refs_2_), channel_id=1, source_target_pairs={{0,16},{16,0},{1,17},{17,1},{2,18},{18,2},{3,19},{19,3},{4,20},{20... | collective-permute-start | bytes 2211848 | tf_op jit(solution)/shard_map/ppermute | solution.py:69
  115.1 11.8 %collective-permute-start.16 = (bf16[4,48,1920]{2,1,0:T(8,128)(2,1)}, bf16[4,48,1920]{2,1,0:T(8,128)(2,1)S(1)}, u32[]{:S(2)}, u32[]{:S(2)}) collective-permute-start(bf16[4,48,1920]{2,1,0:T(8,128)(2,1)} %collective-permute-done.11.refs_4_), channel_id=1, source_target_pairs={{0,16},{16,0},{1,17},{17,1},{2,18},{18,2},{3,19},{19,3},{4,20},{20... | collective-permute-start | bytes 2211848 | tf_op jit(solution)/shard_map/ppermute | solution.py:69
  184.2 91.4 %all-to-all-start.1 = ((bf16[16,128,768]{2,1,0:T(8,128)(2,1)}), bf16[16,128,768]{2,1,0:T(8,128)(2,1)S(1)}, u32[]{:S(2)}, u32[]{:S(2)}) async-start(bf16[16,128,768]{2,1,0:T(8,128)(2,1)} %bitcast.31), calls=%async_computation.1 | async-start | bytes 6291456 | tf_op jit(solution)/shard_map/all_to_all | solution.py:971
  291.2 60.9 %collective-permute-start.24 = (bf16[4,48,3456]{2,1,0:T(8,128)(2,1)}, bf16[4,48,3456]{2,1,0:T(8,128)(2,1)S(1)}, u32[]{:S(2)}, u32[]{:S(2)}) collective-permute-start(bf16[4,48,3456]{2,1,0:T(8,128)(2,1)} %get-tuple-element.165), channel_id=1, source_target_pairs={{0,1},{1,0},{2,3},{3,2},{4,5},{5,4},{6,7},{7,6},{8,9},{9,8},{10,11... | collective-permute-start | bytes 3981320 | tf_op jit(solution)/shard_map/ppermute | solution.py:65
  292.9 59.2 %collective-permute-start.25 = (bf16[4,48,3456]{2,1,0:T(8,128)(2,1)}, bf16[4,48,3456]{2,1,0:T(8,128)(2,1)S(1)}, u32[]{:S(2)}, u32[]{:S(2)}) collective-permute-start(bf16[4,48,3456]{2,1,0:T(8,128)(2,1)} %get-tuple-element.166), channel_id=1, source_target_pairs={{0,2},{1,3},{2,0},{3,1},{4,6},{5,7},{6,4},{7,5},{8,10},{9,11},{10,... | collective-permute-start | bytes 3981320 | tf_op jit(solution)/shard_map/ppermute | solution.py:65
  294.4 57.7 %collective-permute-start.26 = (bf16[4,48,3456]{2,1,0:T(8,128)(2,1)}, bf16[4,48,3456]{2,1,0:T(8,128)(2,1)}, u32[]{:S(2)}, u32[]{:S(2)}) collective-permute-start(bf16[4,48,3456]{2,1,0:T(8,128)(2,1)} %get-tuple-element.167), channel_id=1, source_target_pairs={{0,3},{1,2},{2,1},{3,0},{4,7},{5,6},{6,5},{7,4},{8,11},{9,10},{10,... | collective-permute-start | bytes 3981320 | tf_op jit(solution)/shard_map/ppermute | solution.py:65
  331.1 47.5 %collective-permute-start.27 = (bf16[768,1152]{1,0:T(8,128)(2,1)}, bf16[768,1152]{1,0:T(8,128)(2,1)}, u32[]{:S(2)}, u32[]{:S(2)}) collective-permute-start(bf16[768,1152]{1,0:T(8,128)(2,1)} %grad_qkv_other.1), channel_id=1, source_target_pairs={{0,16},{16,0},{1,17},{17,1},{2,18},{18,2},{3,19},{19,3},{4,20},{20... | collective-permute-start | bytes 5308424 | tf_op jit(solution)/shard_map/ppermute | solution.py:69
  358.0 55.9 %all-to-all-start.3 = ((bf16[4,48,3456]{2,1,0:T(8,128)(2,1)}), bf16[4,48,3456]{2,1,0:T(8,128)(2,1)}, u32[]{:S(2)}, u32[]{:S(2)}) async-start(bf16[4,48,3456]{2,1,0:T(8,128)(2,1)} %sum_parts.1), calls=%async_computation.3 | async-start | bytes 2654208 | tf_op jit(solution)/shard_map/all_to_all | solution.py:762
  390.0 23.0 %collective-permute-start.28 = (bf16[4,48,1152]{2,1,0:T(8,128)(2,1)}, bf16[4,48,1152]{2,1,0:T(8,128)(2,1)}, u32[]{:S(2)}, u32[]{:S(2)}) collective-permute-start(bf16[4,48,1152]{2,1,0:T(8,128)(2,1)} %get-tuple-element.181), channel_id=1, source_target_pairs={{0,1},{1,0},{2,3},{3,2},{4,5},{5,4},{6,7},{7,6},{8,9},{9,8},{10,11... | collective-permute-start | bytes 1327112 | tf_op jit(solution)/shard_map/ppermute | solution.py:65
  390.7 22.3 %collective-permute-start.29 = (bf16[4,48,1152]{2,1,0:T(8,128)(2,1)}, bf16[4,48,1152]{2,1,0:T(8,128)(2,1)}, u32[]{:S(2)}, u32[]{:S(2)}) collective-permute-start(bf16[4,48,1152]{2,1,0:T(8,128)(2,1)} %get-tuple-element.182), channel_id=1, source_target_pairs={{0,2},{1,3},{2,0},{3,1},{4,6},{5,7},{6,4},{7,5},{8,10},{9,11},{10,... | collective-permute-start | bytes 1327112 | tf_op jit(solution)/shard_map/ppermute | solution.py:65
  393.1 20.8 %collective-permute-start.30 = (bf16[4,48,1152]{2,1,0:T(8,128)(2,1)}, bf16[4,48,1152]{2,1,0:T(8,128)(2,1)}, u32[]{:S(2)}, u32[]{:S(2)}) collective-permute-start(bf16[4,48,1152]{2,1,0:T(8,128)(2,1)} %get-tuple-element.183), channel_id=1, source_target_pairs={{0,3},{1,2},{2,1},{3,0},{4,7},{5,6},{6,5},{7,4},{8,11},{9,10},{10,... | collective-permute-start | bytes 1327112 | tf_op jit(solution)/shard_map/ppermute | solution.py:65
  427.5 12.6 %collective-permute-start.35 = (bf16[48,1280]{1,0:T(8,128)(2,1)}, bf16[48,1280]{1,0:T(8,128)(2,1)S(1)}, u32[]{:S(2)}, u32[]{:S(2)}) collective-permute-start(bf16[48,1280]{1,0:T(8,128)(2,1)} %get-tuple-element.206), channel_id=1, source_target_pairs={{0,8},{1,9},{2,10},{3,11},{4,12},{5,13},{6,14},{7,15},{8,0},{9,1},... | collective-permute-start | bytes 368648 | tf_op jit(solution)/shard_map/ppermute | solution.py:65
  (43 other events, 308.0 us)

commit v2 on v1

--- a/solution.py
+++ b/solution.py
@@ -322,11 +322,14 @@
     return u * phi, phi + u * density
 
 
-def mlp_kernel(idx_ref, x_ref, o_ref, vt_ref, bu_ref, *refs, fc):
+def mlp_kernel(idx_ref, x_ref, o_ref, vt_ref, bu_ref, ord_ref, *refs, fc, steps):
     pieces = refs[:14]
-    x2_ref, gl_ref, gp_ref, y_ref, w1_ref, w2_ref, sem = refs[14:]
+    x2_ref, gl_ref, gp_ref, sent_ref, y_ref, w1_ref, w2_ref, sem = refs[14:]
     d = x_ref.shape[1]
     ff = w2_ref.shape[0]
+
+    i = pl.program_id(0)
+    tb = x_ref.shape[0]
 
     @pl.when(pl.program_id(0) == 0)
     def _():
@@ -334,69 +337,67 @@
         for cp in going:
             cp.wait()
 
-    x2 = x_ref[...].astype(F32) + dg(o_ref[...], w1_ref[:, :d], NN) + vt_ref[4:5, :]
-    x2_ref[...] = x2
-    c, r = norm_stats(x2)
-    h = (c * r * vt_ref[5:6, :] + vt_ref[6:7, :]).astype(BF)
-    y = x2 + vt_ref[7:8, :]
-
-    @pl.when(pl.program_id(0) == 0)
-    def _():
-        wait_mlp(w2_ref, sem.at[1])
-
-    for f in range(0, ff, fc):
-        u = dg(h, w1_ref[:, d + f : d + f + fc], NN) + bu_ref[:, f : f + fc]
-        g, gp = gelu_both(u)
-        g = g.astype(BF)
-        gl_ref[:, f : f + fc] = g
-        gp_ref[:, f : f + fc] = gp.astype(BF)
-        y = y + dg(g, w2_ref[f : f + fc, :], NN)
-    y_ref[...] = y.astype(BF)
-
-
-def mlp(idx, x, o, vt, bu, pieces, tb=256, fc=768):
+    @pl.when(i < steps)
+    def _():
+        x2 = x_ref[...].astype(F32) + dg(o_ref[...], w1_ref[:, :d], NN) + vt_ref[4:5, :]
+        x2_ref[...] = x2
+        c, r = norm_stats(x2)
+        h = (c * r * vt_ref[5:6, :] + vt_ref[6:7, :]).astype(BF)
+        y = x2 + vt_ref[7:8, :]
+
+        @pl.when(pl.program_id(0) == 0)
+        def _():
+            wait_mlp(w2_ref, sem.at[1])
+
+        for f in range(0, ff, fc):
+            u = dg(h, w1_ref[:, d + f : d + f + fc], NN) + bu_ref[:, f : f + fc]
+            g, gp = gelu_both(u)
+            g = g.astype(BF)
+            gl_ref[:, f : f + fc] = g
+            gp_ref[:, f : f + fc] = gp.astype(BF)
+            y = y + dg(g, w2_ref[f : f + fc, :], NN)
+        y_ref[pl.ds(pl.multiple_of(i * tb, tb), tb), :] = y.astype(BF)
+
+    @pl.when(i >= steps)
+    def _():
+        pb, t = sent_ref.shape[0], y_ref.shape[0]
+        order = jnp.broadcast_to(ord_ref[...].astype(F32), (8, pb)).T[:, 0:1]
+        hot = jnp.where(order == lax.broadcasted_iota(jnp.int32, (pb, t), 1).astype(F32), 1.0, 0.0)
+        sent_ref[...] = dg(hot.astype(BF), y_ref[...], NN).astype(BF)
+
+
+def mlp(idx, x, o, vt, bu, order, pieces, tb=256, fc=768, pb=512):
     t, d = x.shape
     ff = bu.shape[1]
+    steps = t // tb
+
+    def rows(height, width):
+        return pl.BlockSpec((height, width), lambda i, _: (jnp.minimum(i, steps - 1), 0))
+
+    def late(i):
+        return jnp.maximum(i - steps, 0)
+
     return pl.pallas_call(
-        functools.partial(mlp_kernel, fc=fc),
+        functools.partial(mlp_kernel, fc=fc, steps=steps),
         grid_spec=pltpu.PrefetchScalarGridSpec(
             num_scalar_prefetch=1,
-            grid=(t // tb,),
-            in_specs=[rows_of(tb, d)] * 2 + [whole(vt.shape), whole(bu.shape)] + [ANY] * 14,
-            out_specs=[rows_of(tb, d), rows_of(tb, ff), rows_of(tb, ff), rows_of(tb, d)],
+            grid=(steps + t // pb,),
+            in_specs=[rows(tb, d)] * 2
+            + [whole(vt.shape), whole(bu.shape), pl.BlockSpec((1, pb), lambda i, _: (0, late(i)))]
+            + [ANY] * 14,
+            out_specs=[rows(tb, d), rows(tb, ff), rows(tb, ff), pl.BlockSpec((pb, d), lambda i, _: (late(i), 0))],
             scratch_shapes=[
+                pltpu.VMEM((t, d), BF),
                 pltpu.VMEM((d, d + ff), BF),
                 pltpu.VMEM((ff, d), BF),
                 pltpu.SemaphoreType.DMA((2,)),
             ],
         ),
-        out_shape=[SDS((t, d), F32), SDS((t, ff), BF), SDS((t, ff), BF), SDS((t, d), BF)],
+        out_shape=[SDS((t, d), F32), SDS((t, ff), BF), SDS((t, ff), BF), pltpu.HBM((t, d), BF)],
         compiler_params=params(),
         cost_estimate=cost(4 * t * d * (d + 2 * ff), t * (10 * d + 4 * ff) + 4 * d * ff, 2 * t * ff),
         name="mlp",
-    )(idx, x, o, vt, bu, *pieces)
-
-
-def permute_kernel(ord_ref, y_ref, o_ref):
-    jb = o_ref.shape[0]
-    t = y_ref.shape[0]
-    order = jnp.broadcast_to(ord_ref[...].astype(F32), (8, jb)).T[:, 0:1]
-    hot = jnp.where(order == lax.broadcasted_iota(jnp.int32, (jb, t), 1).astype(F32), 1.0, 0.0)
-    o_ref[...] = dg(hot.astype(BF), y_ref[...], NN).astype(BF)
-
-
-def permute(order, y, jb=512):
-    t, d = y.shape
-    return pl.pallas_call(
-        permute_kernel,
-        grid=(t // jb,),
-        in_specs=[pl.BlockSpec((1, jb), lambda i: (0, i)), whole((t, d))],
-        out_specs=rows_of(jb, d),
-        out_shape=pltpu.HBM((t, d), BF),
-        compiler_params=params(),
-        cost_estimate=cost(2 * t * t * d, t * d * 4),
-        name="permute",
-    )(order, y)
+    )(idx, x, o, vt, bu, order, *pieces)
 
 
 def split_halves(c, r, mine_ref, theirs_ref):
@@ -966,8 +967,7 @@
     returned = lax.all_to_all(after(cast, gate), "fsdp", split_axis=0, concat_axis=0, tiled=True)
     mixed, lse = attend(sensor_tag, qn, kn, qh, kh, vh, early, pairs - early, part)
 
-    x2, active, slope, y = mlp(use, tokens, mixed, vt, bu, pieces_b)
-    sent = permute(owner_order, y)
+    x2, active, slope, sent = mlp(use, tokens, mixed, vt, bu, owner_order, pieces_b)
     encoded = lax.all_to_all(sent, "fsdp", split_axis=0, concat_axis=0, tiled=True)
 
     returned = after(returned, sent)

time: 450 us -> 448 us (level)
  waiting for transfers between devices: 54.6 us -> 77.2 us
  starting transfers between devices: 98.1 us -> 77 us
    ppermute x24, waiting for transfers between devices: 43.3 us -> 65.6 us  [xor_pp(): return lax.ppermute(x, 'fsdp', [(i, i ^ b) for i in range(n)])]
    ppermute x15, starting transfers between devices: 24 us -> 2.48 us  [core_swap(): return lax.ppermute(x, 'dp', [(i, i ^ 1) for i in range(m)])]
    all_to_all x2, starting transfers between devices: 26 us -> 18.5 us  [hop(): lax.all_to_all(x, 'fsdp', split_axis=0, concat_axis=0, tiled=True, axis_i...]
    ppermute x24, starting transfers between devices: 30.7 us -> 37.8 us  [xor_pp(): return lax.ppermute(x, 'fsdp', [(i, i ^ b) for i in range(n)])]
    pallas_call x2 -> x1, Pallas kernels: 55.6 us -> 54 us  [mlp(): pl.pallas_call(functools.partial(mlp_kernel, fc=fc, steps=steps), grid_sp...]
  transfers between devices with their start and end apart: 43 -> 43, of which waited for: 18 -> 19; matrix products, arithmetic and copies ran while one was open for 4% -> 4% of each run, Pallas kernels for 56% -> 56%
where the time goes in v2:
time: 448 us; the launch traced here: 444 us
  Pallas kernels  258 us (58%)
  waiting for transfers between devices  77.2 us (17%)
  starting transfers between devices  77 us (17%)
  other arithmetic  16.9 us (4%)
  local copies, waits for them, and re-layouts  13.5 us (3%)
    ppermute x24, waiting for transfers between devices, xor_pp(): return lax.ppermute(x, 'fsdp', [(i, i ^ b) for i in range(n)])  65.6 us
    pallas_call x1, Pallas kernels, mlp(): pl.pallas_call(functools.partial(mlp_kernel, fc=fc, steps=steps), grid_sp...  54 us
    pallas_call x1, Pallas kernels, mlp_back(): pl.pallas_call(functools.partial(mlp_back_kernel, fc=fc), grid_spec=pltpu...  49.9 us
    ppermute x24, starting transfers between devices, xor_pp(): return lax.ppermute(x, 'fsdp', [(i, i ^ b) for i in range(n)])  37.8 us
    pallas_call x2, Pallas kernels, attend_back(): pl.pallas_call(functools.partial(attend_back_kernel, kb=kb, qb=qb), grid_...  34.6 us
    pallas_call x1, Pallas kernels, grad_mlp(): pl.pallas_call(functools.partial(grad_mlp_kernel, rows=rows), grid_spec=p...  27.7 us
    pallas_call x2, Pallas kernels, grad_qkv(): pl.pallas_call(functools.partial(grad_qkv_kernel, rows=d // n if own else...  21.1 us
    pallas_call x2, Pallas kernels, attend(): pl.pallas_call(functools.partial(attend_kernel, qb=qb, first=first), grid...  19.9 us
  transfers between devices with their start and end apart: 43, of which 19 were waited for; matrix products, arithmetic and copies ran while one was open for 4% of the time, Pallas kernels for 56%

profile of v2, /device:TPU:0, one launch (start us, length us, event | category | flops | bytes accessed | tf_op | source)
XLA Modules:
  0.0 443.9 jit_solution(17929488614327524331)
XLA Ops:
  18.5 5.4 %all-to-all-start = ((bf16[4,48,3456]{2,1,0:T(8,128)(2,1)}), bf16[4,48,3456]{2,1,0:T(8,128)(2,1)S(1)}, u32[]{:S(2)}, u32[]{:S(2)}) async-start(bf16[4,48,3456]{2,1,0:T(8,128)(2,1)} %broadcast_in_dim.2), calls=%async_computation | async-start | bytes 2654208 | tf_op jit(solution)/shard_map/all_to_all | solution.py:763
  27.4 4.8 %convert_element_type.39 = bf16[2048,768]{1,0:T(8,128)(2,1)} convert(f32[2048,768]{1,0:T(8,128)} %param.33) | non-fusion elementwise | flops 1572864 | bytes 9437184 | tf_op jit(solution)/shard_map/convert_element_type | solution.py:932
  32.2 6.8 %collective-permute-done.5.refs_3_ = bf16[4,48,1280]{2,1,0:T(8,128)(2,1)S(1)} collective-permute-done((bf16[4,48,1280]{2,1,0:T(8,128)(2,1)S(1)}, bf16[4,48,1280]{2,1,0:T(8,128)(2,1)S(1)}, u32[]{:S(2)}, u32[]{:S(2)}) %collective-permute-start.5) | collective-permute-done | bytes 491552 | tf_op jit(solution)/shard_map/ppermute | solution.py:65
  39.0 9.2 %collective-permute-done.4.refs_2_ = bf16[4,48,1280]{2,1,0:T(8,128)(2,1)S(1)} collective-permute-done((bf16[4,48,1280]{2,1,0:T(8,128)(2,1)S(1)}, bf16[4,48,1280]{2,1,0:T(8,128)(2,1)S(1)}, u32[]{:S(2)}, u32[]{:S(2)}) %collective-permute-start.4) | collective-permute-done | bytes 491552 | tf_op jit(solution)/shard_map/ppermute | solution.py:65
  50.5 5.3 %all-to-all-done.refs_0_ = bf16[4,48,3456]{2,1,0:T(8,128)(2,1)S(1)} async-done(((bf16[4,48,3456]{2,1,0:T(8,128)(2,1)}), bf16[4,48,3456]{2,1,0:T(8,128)(2,1)S(1)}, u32[]{:S(2)}, u32[]{:S(2)}) %all-to-all-start) | async-done | bytes 1327136 | tf_op jit(solution)/shard_map/all_to_all | solution.py:763
  63.7 16.2 %qkv.1 = (bf16[2048,768]{1,0:T(8,128)(2,1)}, bf16[2048,768]{1,0:T(8,128)(2,1)}, bf16[2048,768]{1,0:T(8,128)(2,1)}, bf16[2048,768]{1,0:T(8,128)(2,1)}, f32[16,768...) custom-call(s32[2]{0:T(128)} %pad_add_fusion.idx_ref.me_ref, ...), custom_call_target="tpu_custom_call" | custom-call | flops 7077888 | bytes 15744 | tf_op jit(solution)/shard_map/qkv/pallas_call | solution.py:208
  82.6 12.5 %attend.2 = (bf16[2048,768]{1,0:T(8,128)(2,1)}, f32[2,6,2,1024]{3,2,1,0:T(2,128)}) custom-call(s32[2]{0:T(128)} %tag_ref.7, f32[4,1,128]{2,1,0:T(1,128)} %get-tuple-element.121.qn_ref, f32[4,1,128]{2,1,0:T(1,128)} %get-tuple-element.122.kn_ref, bf16[2048,768]{1,0:T(8,128)(2,1)} %get-tuple-element.129.q_ref, bf16[2048,768]{1,0:T(8,128)(2,1)} %get-tuple-element.124.k_ref, ...), custom_call_target="tpu_custom_call" | custom-call | flops 16777216 | bytes 12288 | tf_op jit(solution)/shard_map/attend/pallas_call | solution.py:295
  97.1 11.5 %collective-permute-done.14.refs_12_ = bf16[4,48,1536]{2,1,0:T(8,128)(2,1)S(1)} collective-permute-done((bf16[4,48,1536]{2,1,0:T(8,128)(2,1)}, bf16[4,48,1536]{2,1,0:T(8,128)(2,1)S(1)}, u32[]{:S(2)}, u32[]{:S(2)}) %collective-permute-start.14) | collective-permute-done | bytes 589856 | tf_op jit(solution)/shard_map/ppermute | solution.py:65
  109.5 5.0 %all-to-all-start.2 = ((bf16[16,128,768]{2,1,0:T(8,128)(2,1)}), bf16[16,128,768]{2,1,0:T(8,128)(2,1)}, u32[]{:S(2)}, u32[]{:S(2)}) async-start(bf16[16,128,768]{2,1,0:T(8,128)(2,1)} %bitcast.32), calls=%async_computation.2 | async-start | bytes 6291456 | tf_op jit(solution)/shard_map/all_to_all | solution.py:967
  119.5 7.4 %attend.3 = (bf16[2048,768]{1,0:T(8,128)(2,1)}, f32[2,6,2,1024]{3,2,1,0:T(2,128)}) custom-call(s32[2]{0:T(128)} %tag_ref.7, f32[4,1,128]{2,1,0:T(1,128)} %get-tuple-element.121.qn_ref, f32[4,1,128]{2,1,0:T(1,128)} %get-tuple-element.122.kn_ref, bf16[2048,768]{1,0:T(8,128)(2,1)} %get-tuple-element.129.q_ref, ...), custom_call_target="tpu_custom_call", output_to_operand_aliasing={{0}: (6, {}), {1}: (7, {})} | custom-call | flops 8388608 | bytes 12288 | tf_op jit(solution)/shard_map/attend/pallas_call | solution.py:295
  128.7 54.0 %mlp.1 = (f32[2048,768]{1,0:T(8,128)}, bf16[2048,3072]{1,0:T(8,128)(2,1)}, bf16[2048,3072]{1,0:T(8,128)(2,1)}, bf16[2048,768]{1,0:T(8,128)(2,1)}) custom-call(s32[2]{0:T(128)} %pad_add_fusion.idx_ref.me_ref, bf16[2048,768]{1,0:T(8,128)(2,1)} %x_ref.4, bf16[2048,768]{1,0:T(8,128)(2,1)} %get-tuple-element.132.o_ref, f32[16,768]{1,0:T(8,128)} %get-tuple-element.126.vt_ref, ...), custom_call_target="tpu_custom_call" | custom-call | flops 42467328 | bytes 49152 | tf_op jit(solution)/shard_map/mlp/pallas_call | solution.py:380
  182.7 13.3 %all-to-all-start.1 = ((bf16[16,128,768]{2,1,0:T(8,128)(2,1)}), bf16[16,128,768]{2,1,0:T(8,128)(2,1)S(1)}, u32[]{:S(2)}, u32[]{:S(2)}) async-start(bf16[16,128,768]{2,1,0:T(8,128)(2,1)} %bitcast.36), calls=%async_computation.1 | async-start | bytes 6291456 | tf_op jit(solution)/shard_map/all_to_all | solution.py:971
  196.0 49.9 %mlp_back.1 = (bf16[2048,768]{1,0:T(8,128)(2,1)}, bf16[2048,3072]{1,0:T(8,128)(2,1)}, f32[2048,768]{1,0:T(8,128)}, bf16[2048,768]{1,0:T(8,128)(2,1)}, bf16[2048,...) custom-call(s32[2]{0:T(128)} %pad_add_fusion.idx_ref.me_ref, ...), custom_call_target="tpu_custom_call" | custom-call | flops 41287680 | bytes 55296 | tf_op jit(solution)/shard_map/mlp_back/pallas_call | solution.py:467
  246.0 27.7 %grad_mlp.1 = (bf16[3072,384]{1,0:T(8,128)(2,1)}, bf16[3072,384]{1,0:T(8,128)(2,1)}, bf16[768,1536]{1,0:T(8,128)(2,1)}, bf16[768,1536]{1,0:T(8,128)(2,1)}, f32[4,768]{1,0:T(4,128)}) custom-call(s32[2]{0:T(128)} %pad_add_fusion.idx_ref.me_ref, bf16[2048,3072]{1,0:T(8,128)(2,1)} %get-tuple-element.142.g_ref, bf16[2048,768]{1,0:T(8,128)(2,1)} %get-tuple-element.147.dm_ref, ...), custom_call_target="tpu_custom_call" | custom-call | flops 28311552 | bytes 39936 | tf_op jit(solution)/shard_map/grad_mlp/pallas_call | solution.py:541
  274.3 7.8 %attend_back.2 = (bf16[2048,768]{1,0:T(8,128)(2,1)}, bf16[2048,768]{1,0:T(8,128)(2,1)}, bf16[2048,768]{1,0:T(8,128)(2,1)}) custom-call(s32[2]{0:T(128)} %tag_ref.7, bf16[2048,768]{1,0:T(8,128)(2,1)} %get-tuple-element.129.q_ref, bf16[2048,768]{1,0:T(8,128)(2,1)} %get-tuple-element.124.k_ref, bf16[2048,768]{1,0:T(8,128)(2,1)} %get-tuple-element.125.v_ref, ...), custom_call_target="tpu_custom_call" | custom-call | flops 10485760 | bytes 24576 | tf_op jit(solution)/shard_map/attend_back/pallas_call | solution.py:630
  282.9 7.3 %sum_cores.1 = (bf16[4,48,3456]{2,1,0:T(8,128)(2,1)}, bf16[4,48,3456]{2,1,0:T(8,128)(2,1)}, bf16[4,48,3456]{2,1,0:T(8,128)(2,1)}, bf16[4,48,3456]{2,1,0:T(8,128)(2,1)}) custom-call(s32[2]{0:T(128)} %pad_add_fusion.idx_ref.me_ref, bf16[16,48,1536]{2,1,0:T(8,128)(2,1)} %bitcast.38, bf16[16,48,1536]{2,1,0:T(8,128)(2,1)} %bitcast.23.refs_1_, ...), custom_call_target="tpu_custom_call" | custom-call | flops 2592 | bytes 15552 | tf_op jit(solution)/shard_map/sum_cores/pallas_call | solution.py:788
  294.7 4.6 %collective-permute-start.25 = (bf16[4,48,3456]{2,1,0:T(8,128)(2,1)}, bf16[4,48,3456]{2,1,0:T(8,128)(2,1)S(1)}, u32[]{:S(2)}, u32[]{:S(2)}) collective-permute-start(bf16[4,48,3456]{2,1,0:T(8,128)(2,1)} %get-tuple-element.166), channel_id=1, source_target_pairs={{0,2},{1,3},{2,0},{3,1},{4,6},{5,7},{6,4},{7,5},{8,10},{9,11},{10,... | collective-permute-start | bytes 3981320 | tf_op jit(solution)/shard_map/ppermute | solution.py:65
  299.3 26.8 %attend_back.3 = (bf16[2048,768]{1,0:T(8,128)(2,1)}, bf16[2048,768]{1,0:T(8,128)(2,1)}, bf16[2048,768]{1,0:T(8,128)(2,1)}) custom-call(s32[2]{0:T(128)} %tag_ref.7, bf16[2048,768]{1,0:T(8,128)(2,1)} %get-tuple-element.129.q_ref, bf16[2048,768]{1,0:T(8,128)(2,1)} %get-tuple-element.124.k_ref, ...), custom_call_target="tpu_custom_call", output_to_operand_aliasing={{0}: (7, {}), {1}: (8, {}), {2}: (9, {})} | custom-call | flops 52428800 | bytes 24576 | tf_op jit(solution)/shard_map/attend_back/pallas_call | solution.py:630
  326.0 9.7 %grad_qkv_other.1 = bf16[768,1152]{1,0:T(8,128)(2,1)} custom-call(s32[2]{0:T(128)} %pad_add_fusion.idx_ref.me_ref, bf16[2048,768]{1,0:T(8,128)(2,1)} %get-tuple-element.179.h_any, bf16[2048,768]{1,0:T(8,128)(2,1)} %get-tuple-element.185.dq_any.dq_ref, bf16[2048,768]{1,0:T(8,128)(2,1)} %get-tuple-element.186.dk_any.dk_ref, ...), custom_call_target="tpu_custom_call" | custom-call | flops 3538944 | bytes 9216 | tf_op jit(solution)/shard_map/grad_qkv_other/pallas_call | solution.py:679
  335.9 21.8 %collective-permute-done.25.refs_2_ = bf16[4,48,3456]{2,1,0:T(8,128)(2,1)S(1)} collective-permute-done((bf16[4,48,3456]{2,1,0:T(8,128)(2,1)}, bf16[4,48,3456]{2,1,0:T(8,128)(2,1)S(1)}, u32[]{:S(2)}, u32[]{:S(2)}) %collective-permute-start.25) | collective-permute-done | bytes 1327136 | tf_op jit(solution)/shard_map/ppermute | solution.py:65
  363.2 13.1 %all-to-all-start.3 = ((bf16[4,48,3456]{2,1,0:T(8,128)(2,1)}), bf16[4,48,3456]{2,1,0:T(8,128)(2,1)}, u32[]{:S(2)}, u32[]{:S(2)}) async-start(bf16[4,48,3456]{2,1,0:T(8,128)(2,1)} %sum_parts.1), calls=%async_computation.3 | async-start | bytes 2654208 | tf_op jit(solution)/shard_map/all_to_all | solution.py:763
  376.3 11.4 %grad_qkv_own.1 = (bf16[4,48,1152]{2,1,0:T(8,128)(2,1)}, bf16[4,48,1152]{2,1,0:T(8,128)(2,1)}, bf16[4,48,1152]{2,1,0:T(8,128)(2,1)}, bf16[4,48,1152]{2,1,0:T(8,128)(2,1)}) custom-call(s32[2]{0:T(128)} %pad_add_fusion.idx_ref.me_ref, bf16[2048,768]{1,0:T(8,128)(2,1)} %get-tuple-element.179.h_any, bf16[2048,768]{1,0:T(8,128)(2,1)} %get-tuple-element.185.dq_any.dq_ref, ...), custom_call_target="tpu_custom_call" | custom-call | flops 3538944 | bytes 9216 | tf_op jit(solution)/shard_map/grad_qkv_own/pallas_call | solution.py:679
  392.9 19.1 %tokens_back.1 = (f32[2048,768]{1,0:T(8,128)}, bf16[4,48,128]{2,1,0:T(8,128)(2,1)}, bf16[4,48,128]{2,1,0:T(8,128)(2,1)}, bf16[4,48,128]{2,1,0:T(8,128)(2,1)}, bf16[4,48,128]{2,1,0:T(8,128)(2,1)}) custom-call(s32[2]{0:T(128)} %pad_add_fusion.idx_ref.me_ref, s32[2]{0:T(128)} %pad_add_fusion.idx_ref.me_ref, bf16[2048,768]{1,0:T(8,128)(2,1)} %x_ref.4, ...), custom_call_target="tpu_custom_call" | custom-call | flops 10616832 | bytes 28032 | tf_op jit(solution)/shard_map/tokens_back/pallas_call | solution.py:738
  434.6 5.1 %collective-permute-done.35 = bf16[48,1280]{1,0:T(8,128)(2,1)S(1)} collective-permute-done((bf16[48,1280]{1,0:T(8,128)(2,1)}, bf16[48,1280]{1,0:T(8,128)(2,1)S(1)}, u32[]{:S(2)}, u32[]{:S(2)}) %collective-permute-start.35) | collective-permute-done | bytes 122912 | tf_op jit(solution)/shard_map/ppermute | solution.py:65
  (166 shorter events, 86.9 us)
Async XLA Ops:
  18.5 37.3 %all-to-all-start = ((bf16[4,48,3456]{2,1,0:T(8,128)(2,1)}), bf16[4,48,3456]{2,1,0:T(8,128)(2,1)S(1)}, u32[]{:S(2)}, u32[]{:S(2)}) async-start(bf16[4,48,3456]{2,1,0:T(8,128)(2,1)} %broadcast_in_dim.2), calls=%async_computation | async-start | bytes 2654208 | tf_op jit(solution)/shard_map/all_to_all | solution.py:763
  23.9 15.1 %collective-permute-start.5 = (bf16[4,48,1280]{2,1,0:T(8,128)(2,1)S(1)}, bf16[4,48,1280]{2,1,0:T(8,128)(2,1)S(1)}, u32[]{:S(2)}, u32[]{:S(2)}) collective-permute-start(bf16[4,48,1280]{2,1,0:T(8,128)(2,1)S(1)} %pad_maximum_fusion.1.refs_0_), channel_id=1, source_target_pairs={{0,3},{1,2},{2,1},{3,0},{4,7},{5,6},{6,5},{7,4},{8,11},{9,10},{10,... | collective-permute-start | bytes 1474568 | tf_op jit(solution)/shard_map/ppermute | solution.py:65
  26.4 21.8 %collective-permute-start.4 = (bf16[4,48,1280]{2,1,0:T(8,128)(2,1)S(1)}, bf16[4,48,1280]{2,1,0:T(8,128)(2,1)S(1)}, u32[]{:S(2)}, u32[]{:S(2)}) collective-permute-start(bf16[4,48,1280]{2,1,0:T(8,128)(2,1)S(1)} %pad_maximum_fusion.1.refs_0_), channel_id=1, source_target_pairs={{0,2},{1,3},{2,0},{3,1},{4,6},{5,7},{6,4},{7,5},{8,10},{9,11},{10,... | collective-permute-start | bytes 1474568 | tf_op jit(solution)/shard_map/ppermute | solution.py:65
  26.9 21.4 %collective-permute-start.3 = (bf16[4,48,1280]{2,1,0:T(8,128)(2,1)S(1)}, bf16[4,48,1280]{2,1,0:T(8,128)(2,1)S(1)}, u32[]{:S(2)}, u32[]{:S(2)}) collective-permute-start(bf16[4,48,1280]{2,1,0:T(8,128)(2,1)S(1)} %pad_maximum_fusion.1.refs_0_), channel_id=1, source_target_pairs={{0,1},{1,0},{2,3},{3,2},{4,5},{5,4},{6,7},{7,6},{8,9},{9,8},{10,11... | collective-permute-start | bytes 1474568 | tf_op jit(solution)/shard_map/ppermute | solution.py:65
  50.4 12.2 %collective-permute-start.7 = (bf16[3,4,48,1280]{3,2,1,0:T(8,128)(2,1)}, bf16[3,4,48,1280]{3,2,1,0:T(8,128)(2,1)S(1)}, u32[]{:S(2)}, u32[]{:S(2)}) collective-permute-start(bf16[3,4,48,1280]{3,2,1,0:T(8,128)(2,1)} %pad_maximum_fusion), channel_id=1, source_target_pairs={{0,16},{16,0},{1,17},{17,1},{2,18},{18,2},{3,19},{19,3},{4,20},{20... | collective-permute-start | bytes 4423688 | tf_op jit(solution)/shard_map/ppermute | solution.py:69
  56.8 23.2 %collective-permute-start.8 = (bf16[4,48,1920]{2,1,0:T(8,128)(2,1)}, bf16[4,48,1920]{2,1,0:T(8,128)(2,1)}, u32[]{:S(2)}, u32[]{:S(2)}) collective-permute-start(bf16[4,48,1920]{2,1,0:T(8,128)(2,1)} %slice.178), channel_id=1, source_target_pairs={{0,1},{1,0},{2,3},{3,2},{4,5},{5,4},{6,7},{7,6},{8,9},{9,8},{10,11... | collective-permute-start | bytes 2211848 | tf_op jit(solution)/shard_map/ppermute | solution.py:65
  59.1 20.8 %collective-permute-start.9 = (bf16[4,48,1536]{2,1,0:T(8,128)(2,1)}, bf16[4,48,1536]{2,1,0:T(8,128)(2,1)}, u32[]{:S(2)}, u32[]{:S(2)}) collective-permute-start(bf16[4,48,1536]{2,1,0:T(8,128)(2,1)} %slice.179), channel_id=1, source_target_pairs={{0,2},{1,3},{2,0},{3,1},{4,6},{5,7},{6,4},{7,5},{8,10},{9,11},{10,... | collective-permute-start | bytes 1769480 | tf_op jit(solution)/shard_map/ppermute | solution.py:65
  61.2 35.9 %collective-permute-start.11 = (bf16[4,48,1920]{2,1,0:T(8,128)(2,1)}, bf16[4,48,1920]{2,1,0:T(8,128)(2,1)}, u32[]{:S(2)}, u32[]{:S(2)}) collective-permute-start(bf16[4,48,1920]{2,1,0:T(8,128)(2,1)} %slice.178), channel_id=1, source_target_pairs={{0,2},{1,3},{2,0},{3,1},{4,6},{5,7},{6,4},{7,5},{8,10},{9,11},{10,... | collective-permute-start | bytes 2211848 | tf_op jit(solution)/shard_map/ppermute | solution.py:65
  79.9 28.7 %collective-permute-start.12 = (bf16[4,48,1920]{2,1,0:T(8,128)(2,1)}, bf16[4,48,1920]{2,1,0:T(8,128)(2,1)S(1)}, u32[]{:S(2)}, u32[]{:S(2)}) collective-permute-start(bf16[4,48,1920]{2,1,0:T(8,128)(2,1)} %collective-permute-done.8.refs_2_), channel_id=1, source_target_pairs={{0,2},{1,3},{2,0},{3,1},{4,6},{5,7},{6,4},{7,5},{8,10},{9,11},{10,... | collective-permute-start | bytes 2211848 | tf_op jit(solution)/shard_map/ppermute | solution.py:65
  80.6 16.5 %collective-permute-start.13 = (bf16[4,48,1536]{2,1,0:T(8,128)(2,1)}, bf16[4,48,1536]{2,1,0:T(8,128)(2,1)}, u32[]{:S(2)}, u32[]{:S(2)}) collective-permute-start(bf16[4,48,1536]{2,1,0:T(8,128)(2,1)} %slice.179), channel_id=1, source_target_pairs={{0,1},{1,0},{2,3},{3,2},{4,5},{5,4},{6,7},{7,6},{8,9},{9,8},{10,11... | collective-permute-start | bytes 1769480 | tf_op jit(solution)/shard_map/ppermute | solution.py:65
  81.2 27.5 %collective-permute-start.14 = (bf16[4,48,1536]{2,1,0:T(8,128)(2,1)}, bf16[4,48,1536]{2,1,0:T(8,128)(2,1)S(1)}, u32[]{:S(2)}, u32[]{:S(2)}) collective-permute-start(bf16[4,48,1536]{2,1,0:T(8,128)(2,1)} %collective-permute-done.9.refs_10_), channel_id=1, source_target_pairs={{0,1},{1,0},{2,3},{3,2},{4,5},{5,4},{6,7},{7,6},{8,9},{9,8},{10,11... | collective-permute-start | bytes 1769480 | tf_op jit(solution)/shard_map/ppermute | solution.py:65
  109.5 73.2 %all-to-all-start.2 = ((bf16[16,128,768]{2,1,0:T(8,128)(2,1)}), bf16[16,128,768]{2,1,0:T(8,128)(2,1)}, u32[]{:S(2)}, u32[]{:S(2)}) async-start(bf16[16,128,768]{2,1,0:T(8,128)(2,1)} %bitcast.32), calls=%async_computation.2 | async-start | bytes 6291456 | tf_op jit(solution)/shard_map/all_to_all | solution.py:967
  115.1 11.9 %collective-permute-start.15 = (bf16[4,48,1920]{2,1,0:T(8,128)(2,1)}, bf16[4,48,1920]{2,1,0:T(8,128)(2,1)S(1)}, u32[]{:S(2)}, u32[]{:S(2)}) collective-permute-start(bf16[4,48,1920]{2,1,0:T(8,128)(2,1)} %collective-permute-done.8.refs_2_), channel_id=1, source_target_pairs={{0,16},{16,0},{1,17},{17,1},{2,18},{18,2},{3,19},{19,3},{4,20},{20... | collective-permute-start | bytes 2211848 | tf_op jit(solution)/shard_map/ppermute | solution.py:69
  115.1 11.8 %collective-permute-start.16 = (bf16[4,48,1920]{2,1,0:T(8,128)(2,1)}, bf16[4,48,1920]{2,1,0:T(8,128)(2,1)S(1)}, u32[]{:S(2)}, u32[]{:S(2)}) collective-permute-start(bf16[4,48,1920]{2,1,0:T(8,128)(2,1)} %collective-permute-done.11.refs_4_), channel_id=1, source_target_pairs={{0,16},{16,0},{1,17},{17,1},{2,18},{18,2},{3,19},{19,3},{4,20},{20... | collective-permute-start | bytes 2211848 | tf_op jit(solution)/shard_map/ppermute | solution.py:69
  182.7 91.7 %all-to-all-start.1 = ((bf16[16,128,768]{2,1,0:T(8,128)(2,1)}), bf16[16,128,768]{2,1,0:T(8,128)(2,1)S(1)}, u32[]{:S(2)}, u32[]{:S(2)}) async-start(bf16[16,128,768]{2,1,0:T(8,128)(2,1)} %bitcast.36), calls=%async_computation.1 | async-start | bytes 6291456 | tf_op jit(solution)/shard_map/all_to_all | solution.py:971
  290.2 45.7 %collective-permute-start.24 = (bf16[4,48,3456]{2,1,0:T(8,128)(2,1)}, bf16[4,48,3456]{2,1,0:T(8,128)(2,1)S(1)}, u32[]{:S(2)}, u32[]{:S(2)}) collective-permute-start(bf16[4,48,3456]{2,1,0:T(8,128)(2,1)} %get-tuple-element.165), channel_id=1, source_target_pairs={{0,1},{1,0},{2,3},{3,2},{4,5},{5,4},{6,7},{7,6},{8,9},{9,8},{10,11... | collective-permute-start | bytes 3981320 | tf_op jit(solution)/shard_map/ppermute | solution.py:65
  294.7 63.0 %collective-permute-start.25 = (bf16[4,48,3456]{2,1,0:T(8,128)(2,1)}, bf16[4,48,3456]{2,1,0:T(8,128)(2,1)S(1)}, u32[]{:S(2)}, u32[]{:S(2)}) collective-permute-start(bf16[4,48,3456]{2,1,0:T(8,128)(2,1)} %get-tuple-element.166), channel_id=1, source_target_pairs={{0,2},{1,3},{2,0},{3,1},{4,6},{5,7},{6,4},{7,5},{8,10},{9,11},{10,... | collective-permute-start | bytes 3981320 | tf_op jit(solution)/shard_map/ppermute | solution.py:65
  299.3 58.4 %collective-permute-start.26 = (bf16[4,48,3456]{2,1,0:T(8,128)(2,1)}, bf16[4,48,3456]{2,1,0:T(8,128)(2,1)}, u32[]{:S(2)}, u32[]{:S(2)}) collective-permute-start(bf16[4,48,3456]{2,1,0:T(8,128)(2,1)} %get-tuple-element.167), channel_id=1, source_target_pairs={{0,3},{1,2},{2,1},{3,0},{4,7},{5,6},{6,5},{7,4},{8,11},{9,10},{10,... | collective-permute-start | bytes 3981320 | tf_op jit(solution)/shard_map/ppermute | solution.py:65
  335.8 40.5 %collective-permute-start.27 = (bf16[768,1152]{1,0:T(8,128)(2,1)}, bf16[768,1152]{1,0:T(8,128)(2,1)}, u32[]{:S(2)}, u32[]{:S(2)}) collective-permute-start(bf16[768,1152]{1,0:T(8,128)(2,1)} %grad_qkv_other.1), channel_id=1, source_target_pairs={{0,16},{16,0},{1,17},{17,1},{2,18},{18,2},{3,19},{19,3},{4,20},{20... | collective-permute-start | bytes 5308424 | tf_op jit(solution)/shard_map/ppermute | solution.py:69
  363.2 50.0 %all-to-all-start.3 = ((bf16[4,48,3456]{2,1,0:T(8,128)(2,1)}), bf16[4,48,3456]{2,1,0:T(8,128)(2,1)}, u32[]{:S(2)}, u32[]{:S(2)}) async-start(bf16[4,48,3456]{2,1,0:T(8,128)(2,1)} %sum_parts.1), calls=%async_computation.3 | async-start | bytes 2654208 | tf_op jit(solution)/shard_map/all_to_all | solution.py:763
  387.6 24.4 %collective-permute-start.28 = (bf16[4,48,1152]{2,1,0:T(8,128)(2,1)}, bf16[4,48,1152]{2,1,0:T(8,128)(2,1)}, u32[]{:S(2)}, u32[]{:S(2)}) collective-permute-start(bf16[4,48,1152]{2,1,0:T(8,128)(2,1)} %get-tuple-element.181), channel_id=1, source_target_pairs={{0,1},{1,0},{2,3},{3,2},{4,5},{5,4},{6,7},{7,6},{8,9},{9,8},{10,11... | collective-permute-start | bytes 1327112 | tf_op jit(solution)/shard_map/ppermute | solution.py:65
  391.4 21.8 %collective-permute-start.29 = (bf16[4,48,1152]{2,1,0:T(8,128)(2,1)}, bf16[4,48,1152]{2,1,0:T(8,128)(2,1)}, u32[]{:S(2)}, u32[]{:S(2)}) collective-permute-start(bf16[4,48,1152]{2,1,0:T(8,128)(2,1)} %get-tuple-element.182), channel_id=1, source_target_pairs={{0,2},{1,3},{2,0},{3,1},{4,6},{5,7},{6,4},{7,5},{8,10},{9,11},{10,... | collective-permute-start | bytes 1327112 | tf_op jit(solution)/shard_map/ppermute | solution.py:65
  392.8 20.3 %collective-permute-start.30 = (bf16[4,48,1152]{2,1,0:T(8,128)(2,1)}, bf16[4,48,1152]{2,1,0:T(8,128)(2,1)}, u32[]{:S(2)}, u32[]{:S(2)}) collective-permute-start(bf16[4,48,1152]{2,1,0:T(8,128)(2,1)} %get-tuple-element.183), channel_id=1, source_target_pairs={{0,3},{1,2},{2,1},{3,0},{4,7},{5,6},{6,5},{7,4},{8,11},{9,10},{10,... | collective-permute-start | bytes 1327112 | tf_op jit(solution)/shard_map/ppermute | solution.py:65
  427.1 12.6 %collective-permute-start.35 = (bf16[48,1280]{1,0:T(8,128)(2,1)}, bf16[48,1280]{1,0:T(8,128)(2,1)S(1)}, u32[]{:S(2)}, u32[]{:S(2)}) collective-permute-start(bf16[48,1280]{1,0:T(8,128)(2,1)} %get-tuple-element.206), channel_id=1, source_target_pairs={{0,8},{1,9},{2,10},{3,11},{4,12},{5,13},{6,14},{7,15},{8,0},{9,1},... | collective-permute-start | bytes 368648 | tf_op jit(solution)/shard_map/ppermute | solution.py:65
  (43 other events, 328.1 us)

commit v3 on v2

--- a/solution.py
+++ b/solution.py
@@ -276,8 +276,9 @@
 
         @pl.when(jnp.logical_and(tag_ref[r] == 0, chosen))
         def _(plain=plain):
-            for i in range(length // qb):
-                block(i * qb, qb, 0, length, plain)
+            n = qb // 2 if plain else qb
+            for i in range(length // n):
+                block(i * n, n, 0, length, plain)
 
         @pl.when(jnp.logical_and(tag_ref[r] != 0, chosen))
         def _(plain=plain):

time: 448 us -> 448 us (level)
  Pallas kernels: 258 us -> 286 us
  waiting for transfers between devices: 77.2 us -> 52.7 us
  starting transfers between devices: 77 us -> 71.8 us
    ppermute x24, waiting for transfers between devices: 65.6 us -> 41.8 us  [xor_pp(): return lax.ppermute(x, 'fsdp', [(i, i ^ b) for i in range(n)])]
    pallas_call x2, Pallas kernels: 34.6 us -> 53.4 us  [attend_back(): pl.pallas_call(functools.partial(attend_back_kernel, kb=kb, qb=qb), grid_...]
    pallas_call x2, Pallas kernels: 19.9 us -> 28.6 us  [attend(): pl.pallas_call(functools.partial(attend_kernel, qb=qb, first=first), grid...]
    all_to_all x2, starting transfers between devices: 18.5 us -> 13.4 us  [hop(): lax.all_to_all(x, 'fsdp', split_axis=0, concat_axis=0, tiled=True, axis_i...]
  transfers between devices with their start and end apart: 43 -> 43, of which waited for: 19 -> 17; matrix products, arithmetic and copies ran while one was open for 4% -> 4% of each run, Pallas kernels for 56% -> 62%
where the time goes in v3:
time: 448 us; the launch traced here: 442 us
  Pallas kernels  286 us (64%)
  starting transfers between devices  71.8 us (16%)
  waiting for transfers between devices  52.7 us (12%)
  other arithmetic  16.9 us (4%)
  local copies, waits for them, and re-layouts  13.5 us (3%)
    pallas_call x1, Pallas kernels, mlp(): pl.pallas_call(functools.partial(mlp_kernel, fc=fc, steps=steps), grid_sp...  54 us
    pallas_call x2, Pallas kernels, attend_back(): pl.pallas_call(functools.partial(attend_back_kernel, kb=kb, qb=qb), grid_...  53.4 us
    pallas_call x1, Pallas kernels, mlp_back(): pl.pallas_call(functools.partial(mlp_back_kernel, fc=fc), grid_spec=pltpu...  49.9 us
    ppermute x24, waiting for transfers between devices, xor_pp(): return lax.ppermute(x, 'fsdp', [(i, i ^ b) for i in range(n)])  41.8 us
    ppermute x24, starting transfers between devices, xor_pp(): return lax.ppermute(x, 'fsdp', [(i, i ^ b) for i in range(n)])  41.7 us
    pallas_call x2, Pallas kernels, attend(): pl.pallas_call(functools.partial(attend_kernel, qb=qb, first=first), grid...  28.6 us
    pallas_call x1, Pallas kernels, grad_mlp(): pl.pallas_call(functools.partial(grad_mlp_kernel, rows=rows), grid_spec=p...  27.7 us
    pallas_call x2, Pallas kernels, grad_qkv(): pl.pallas_call(functools.partial(grad_qkv_kernel, rows=d // n if own else...  21.1 us
  transfers between devices with their start and end apart: 43, of which 17 were waited for; matrix products, arithmetic and copies ran while one was open for 4% of the time, Pallas kernels for 62%

profile of v3, /device:TPU:0, one launch (start us, length us, event | category | flops | bytes accessed | tf_op | source)
XLA Modules:
  0.0 441.8 jit_solution(7228319291556989894)
XLA Ops:
  18.5 5.4 %all-to-all-start = ((bf16[4,48,3456]{2,1,0:T(8,128)(2,1)}), bf16[4,48,3456]{2,1,0:T(8,128)(2,1)S(1)}, u32[]{:S(2)}, u32[]{:S(2)}) async-start(bf16[4,48,3456]{2,1,0:T(8,128)(2,1)} %broadcast_in_dim.2), calls=%async_computation | async-start | bytes 2654208 | tf_op jit(solution)/shard_map/all_to_all | solution.py:764
  27.4 4.8 %convert_element_type.39 = bf16[2048,768]{1,0:T(8,128)(2,1)} convert(f32[2048,768]{1,0:T(8,128)} %param.33) | non-fusion elementwise | flops 1572864 | bytes 9437184 | tf_op jit(solution)/shard_map/convert_element_type | solution.py:933
  32.2 6.8 %collective-permute-done.5.refs_3_ = bf16[4,48,1280]{2,1,0:T(8,128)(2,1)S(1)} collective-permute-done((bf16[4,48,1280]{2,1,0:T(8,128)(2,1)S(1)}, bf16[4,48,1280]{2,1,0:T(8,128)(2,1)S(1)}, u32[]{:S(2)}, u32[]{:S(2)}) %collective-permute-start.5) | collective-permute-done | bytes 491552 | tf_op jit(solution)/shard_map/ppermute | solution.py:65
  39.0 9.2 %collective-permute-done.4.refs_2_ = bf16[4,48,1280]{2,1,0:T(8,128)(2,1)S(1)} collective-permute-done((bf16[4,48,1280]{2,1,0:T(8,128)(2,1)S(1)}, bf16[4,48,1280]{2,1,0:T(8,128)(2,1)S(1)}, u32[]{:S(2)}, u32[]{:S(2)}) %collective-permute-start.4) | collective-permute-done | bytes 491552 | tf_op jit(solution)/shard_map/ppermute | solution.py:65
  50.5 5.3 %all-to-all-done.refs_0_ = bf16[4,48,3456]{2,1,0:T(8,128)(2,1)S(1)} async-done(((bf16[4,48,3456]{2,1,0:T(8,128)(2,1)}), bf16[4,48,3456]{2,1,0:T(8,128)(2,1)S(1)}, u32[]{:S(2)}, u32[]{:S(2)}) %all-to-all-start) | async-done | bytes 1327136 | tf_op jit(solution)/shard_map/all_to_all | solution.py:764
  63.7 16.2 %qkv.1 = (bf16[2048,768]{1,0:T(8,128)(2,1)}, bf16[2048,768]{1,0:T(8,128)(2,1)}, bf16[2048,768]{1,0:T(8,128)(2,1)}, bf16[2048,768]{1,0:T(8,128)(2,1)}, f32[16,768...) custom-call(s32[2]{0:T(128)} %pad_add_fusion.idx_ref.me_ref, ...), custom_call_target="tpu_custom_call" | custom-call | flops 7077888 | bytes 15744 | tf_op jit(solution)/shard_map/qkv/pallas_call | solution.py:208
  82.6 18.3 %attend.2 = (bf16[2048,768]{1,0:T(8,128)(2,1)}, f32[2,6,2,1024]{3,2,1,0:T(2,128)}) custom-call(s32[2]{0:T(128)} %tag_ref.7, f32[4,1,128]{2,1,0:T(1,128)} %get-tuple-element.121.qn_ref, f32[4,1,128]{2,1,0:T(1,128)} %get-tuple-element.122.kn_ref, bf16[2048,768]{1,0:T(8,128)(2,1)} %get-tuple-element.129.q_ref, bf16[2048,768]{1,0:T(8,128)(2,1)} %get-tuple-element.124.k_ref, ...), custom_call_target="tpu_custom_call" | custom-call | flops 16777216 | bytes 12288 | tf_op jit(solution)/shard_map/attend/pallas_call | solution.py:296
  101.0 7.7 %collective-permute-done.14.refs_12_ = bf16[4,48,1536]{2,1,0:T(8,128)(2,1)S(1)} collective-permute-done((bf16[4,48,1536]{2,1,0:T(8,128)(2,1)}, bf16[4,48,1536]{2,1,0:T(8,128)(2,1)S(1)}, u32[]{:S(2)}, u32[]{:S(2)}) %collective-permute-start.14) | collective-permute-done | bytes 589856 | tf_op jit(solution)/shard_map/ppermute | solution.py:65
  109.5 5.0 %all-to-all-start.2 = ((bf16[16,128,768]{2,1,0:T(8,128)(2,1)}), bf16[16,128,768]{2,1,0:T(8,128)(2,1)}, u32[]{:S(2)}, u32[]{:S(2)}) async-start(bf16[16,128,768]{2,1,0:T(8,128)(2,1)} %bitcast.32), calls=%async_computation.2 | async-start | bytes 6291456 | tf_op jit(solution)/shard_map/all_to_all | solution.py:968
  119.5 10.3 %attend.3 = (bf16[2048,768]{1,0:T(8,128)(2,1)}, f32[2,6,2,1024]{3,2,1,0:T(2,128)}) custom-call(s32[2]{0:T(128)} %tag_ref.7, f32[4,1,128]{2,1,0:T(1,128)} %get-tuple-element.121.qn_ref, f32[4,1,128]{2,1,0:T(1,128)} %get-tuple-element.122.kn_ref, bf16[2048,768]{1,0:T(8,128)(2,1)} %get-tuple-element.129.q_ref, ...), custom_call_target="tpu_custom_call", output_to_operand_aliasing={{0}: (6, {}), {1}: (7, {})} | custom-call | flops 8388608 | bytes 12288 | tf_op jit(solution)/shard_map/attend/pallas_call | solution.py:296
  131.6 54.0 %mlp.1 = (f32[2048,768]{1,0:T(8,128)}, bf16[2048,3072]{1,0:T(8,128)(2,1)}, bf16[2048,3072]{1,0:T(8,128)(2,1)}, bf16[2048,768]{1,0:T(8,128)(2,1)}) custom-call(s32[2]{0:T(128)} %pad_add_fusion.idx_ref.me_ref, bf16[2048,768]{1,0:T(8,128)(2,1)} %x_ref.4, bf16[2048,768]{1,0:T(8,128)(2,1)} %get-tuple-element.132.o_ref, f32[16,768]{1,0:T(8,128)} %get-tuple-element.126.vt_ref, ...), custom_call_target="tpu_custom_call" | custom-call | flops 42467328 | bytes 49152 | tf_op jit(solution)/shard_map/mlp/pallas_call | solution.py:381
  185.6 9.2 %all-to-all-start.1 = ((bf16[16,128,768]{2,1,0:T(8,128)(2,1)}), bf16[16,128,768]{2,1,0:T(8,128)(2,1)S(1)}, u32[]{:S(2)}, u32[]{:S(2)}) async-start(bf16[16,128,768]{2,1,0:T(8,128)(2,1)} %bitcast.36), calls=%async_computation.1 | async-start | bytes 6291456 | tf_op jit(solution)/shard_map/all_to_all | solution.py:972
  194.8 49.9 %mlp_back.1 = (bf16[2048,768]{1,0:T(8,128)(2,1)}, bf16[2048,3072]{1,0:T(8,128)(2,1)}, f32[2048,768]{1,0:T(8,128)}, bf16[2048,768]{1,0:T(8,128)(2,1)}, bf16[2048,...) custom-call(s32[2]{0:T(128)} %pad_add_fusion.idx_ref.me_ref, ...), custom_call_target="tpu_custom_call" | custom-call | flops 41287680 | bytes 55296 | tf_op jit(solution)/shard_map/mlp_back/pallas_call | solution.py:468
  244.8 27.7 %grad_mlp.1 = (bf16[3072,384]{1,0:T(8,128)(2,1)}, bf16[3072,384]{1,0:T(8,128)(2,1)}, bf16[768,1536]{1,0:T(8,128)(2,1)}, bf16[768,1536]{1,0:T(8,128)(2,1)}, f32[4,768]{1,0:T(4,128)}) custom-call(s32[2]{0:T(128)} %pad_add_fusion.idx_ref.me_ref, bf16[2048,3072]{1,0:T(8,128)(2,1)} %get-tuple-element.142.g_ref, bf16[2048,768]{1,0:T(8,128)(2,1)} %get-tuple-element.147.dm_ref, ...), custom_call_target="tpu_custom_call" | custom-call | flops 28311552 | bytes 39936 | tf_op jit(solution)/shard_map/grad_mlp/pallas_call | solution.py:542
  273.2 11.0 %attend_back.2 = (bf16[2048,768]{1,0:T(8,128)(2,1)}, bf16[2048,768]{1,0:T(8,128)(2,1)}, bf16[2048,768]{1,0:T(8,128)(2,1)}) custom-call(s32[2]{0:T(128)} %tag_ref.7, bf16[2048,768]{1,0:T(8,128)(2,1)} %get-tuple-element.129.q_ref, bf16[2048,768]{1,0:T(8,128)(2,1)} %get-tuple-element.124.k_ref, bf16[2048,768]{1,0:T(8,128)(2,1)} %get-tuple-element.125.v_ref, ...), custom_call_target="tpu_custom_call" | custom-call | flops 10485760 | bytes 24576 | tf_op jit(solution)/shard_map/attend_back/pallas_call | solution.py:631
  284.2 7.3 %sum_cores.1 = (bf16[4,48,3456]{2,1,0:T(8,128)(2,1)}, bf16[4,48,3456]{2,1,0:T(8,128)(2,1)}, bf16[4,48,3456]{2,1,0:T(8,128)(2,1)}, bf16[4,48,3456]{2,1,0:T(8,128)(2,1)}) custom-call(s32[2]{0:T(128)} %pad_add_fusion.idx_ref.me_ref, bf16[16,48,1536]{2,1,0:T(8,128)(2,1)} %bitcast.38, bf16[16,48,1536]{2,1,0:T(8,128)(2,1)} %bitcast.23.refs_1_, ...), custom_call_target="tpu_custom_call" | custom-call | flops 2592 | bytes 15552 | tf_op jit(solution)/shard_map/sum_cores/pallas_call | solution.py:789
  295.1 42.5 %attend_back.3 = (bf16[2048,768]{1,0:T(8,128)(2,1)}, bf16[2048,768]{1,0:T(8,128)(2,1)}, bf16[2048,768]{1,0:T(8,128)(2,1)}) custom-call(s32[2]{0:T(128)} %tag_ref.7, bf16[2048,768]{1,0:T(8,128)(2,1)} %get-tuple-element.129.q_ref, bf16[2048,768]{1,0:T(8,128)(2,1)} %get-tuple-element.124.k_ref, ...), custom_call_target="tpu_custom_call", output_to_operand_aliasing={{0}: (7, {}), {1}: (8, {}), {2}: (9, {})} | custom-call | flops 52428800 | bytes 24576 | tf_op jit(solution)/shard_map/attend_back/pallas_call | solution.py:631
  337.5 9.7 %grad_qkv_other.1 = bf16[768,1152]{1,0:T(8,128)(2,1)} custom-call(s32[2]{0:T(128)} %pad_add_fusion.idx_ref.me_ref, bf16[2048,768]{1,0:T(8,128)(2,1)} %get-tuple-element.179.h_any, bf16[2048,768]{1,0:T(8,128)(2,1)} %get-tuple-element.185.dq_any.dq_ref, bf16[2048,768]{1,0:T(8,128)(2,1)} %get-tuple-element.186.dk_any.dk_ref, ...), custom_call_target="tpu_custom_call" | custom-call | flops 3538944 | bytes 9216 | tf_op jit(solution)/shard_map/grad_qkv_other/pallas_call | solution.py:680
  347.3 4.7 %collective-permute-done.25.refs_2_ = bf16[4,48,3456]{2,1,0:T(8,128)(2,1)S(1)} collective-permute-done((bf16[4,48,3456]{2,1,0:T(8,128)(2,1)}, bf16[4,48,3456]{2,1,0:T(8,128)(2,1)S(1)}, u32[]{:S(2)}, u32[]{:S(2)}) %collective-permute-start.25) | collective-permute-done | bytes 1327136 | tf_op jit(solution)/shard_map/ppermute | solution.py:65
  357.5 8.0 %all-to-all-start.3 = ((bf16[4,48,3456]{2,1,0:T(8,128)(2,1)}), bf16[4,48,3456]{2,1,0:T(8,128)(2,1)}, u32[]{:S(2)}, u32[]{:S(2)}) async-start(bf16[4,48,3456]{2,1,0:T(8,128)(2,1)} %sum_parts.1), calls=%async_computation.3 | async-start | bytes 2654208 | tf_op jit(solution)/shard_map/all_to_all | solution.py:764
  365.6 11.4 %grad_qkv_own.1 = (bf16[4,48,1152]{2,1,0:T(8,128)(2,1)}, bf16[4,48,1152]{2,1,0:T(8,128)(2,1)}, bf16[4,48,1152]{2,1,0:T(8,128)(2,1)}, bf16[4,48,1152]{2,1,0:T(8,128)(2,1)}) custom-call(s32[2]{0:T(128)} %pad_add_fusion.idx_ref.me_ref, bf16[2048,768]{1,0:T(8,128)(2,1)} %get-tuple-element.179.h_any, bf16[2048,768]{1,0:T(8,128)(2,1)} %get-tuple-element.185.dq_any.dq_ref, ...), custom_call_target="tpu_custom_call" | custom-call | flops 3538944 | bytes 9216 | tf_op jit(solution)/shard_map/grad_qkv_own/pallas_call | solution.py:680
  376.9 13.3 %collective-permute-start.28 = (bf16[4,48,1152]{2,1,0:T(8,128)(2,1)}, bf16[4,48,1152]{2,1,0:T(8,128)(2,1)}, u32[]{:S(2)}, u32[]{:S(2)}) collective-permute-start(bf16[4,48,1152]{2,1,0:T(8,128)(2,1)} %get-tuple-element.181), channel_id=1, source_target_pairs={{0,1},{1,0},{2,3},{3,2},{4,5},{5,4},{6,7},{7,6},{8,9},{9,8},{10,11... | collective-permute-start | bytes 1327112 | tf_op jit(solution)/shard_map/ppermute | solution.py:65
  391.8 19.1 %tokens_back.1 = (f32[2048,768]{1,0:T(8,128)}, bf16[4,48,128]{2,1,0:T(8,128)(2,1)}, bf16[4,48,128]{2,1,0:T(8,128)(2,1)}, bf16[4,48,128]{2,1,0:T(8,128)(2,1)}, bf16[4,48,128]{2,1,0:T(8,128)(2,1)}) custom-call(s32[2]{0:T(128)} %pad_add_fusion.idx_ref.me_ref, s32[2]{0:T(128)} %pad_add_fusion.idx_ref.me_ref, bf16[2048,768]{1,0:T(8,128)(2,1)} %x_ref.4, ...), custom_call_target="tpu_custom_call" | custom-call | flops 10616832 | bytes 28032 | tf_op jit(solution)/shard_map/tokens_back/pallas_call | solution.py:739
  432.8 4.9 %collective-permute-done.35 = bf16[48,1280]{1,0:T(8,128)(2,1)S(1)} collective-permute-done((bf16[48,1280]{1,0:T(8,128)(2,1)}, bf16[48,1280]{1,0:T(8,128)(2,1)S(1)}, u32[]{:S(2)}, u32[]{:S(2)}) %collective-permute-start.35) | collective-permute-done | bytes 122912 | tf_op jit(solution)/shard_map/ppermute | solution.py:65
  (166 shorter events, 78.9 us)
Async XLA Ops:
  18.5 37.3 %all-to-all-start = ((bf16[4,48,3456]{2,1,0:T(8,128)(2,1)}), bf16[4,48,3456]{2,1,0:T(8,128)(2,1)S(1)}, u32[]{:S(2)}, u32[]{:S(2)}) async-start(bf16[4,48,3456]{2,1,0:T(8,128)(2,1)} %broadcast_in_dim.2), calls=%async_computation | async-start | bytes 2654208 | tf_op jit(solution)/shard_map/all_to_all | solution.py:764
  23.9 15.1 %collective-permute-start.5 = (bf16[4,48,1280]{2,1,0:T(8,128)(2,1)S(1)}, bf16[4,48,1280]{2,1,0:T(8,128)(2,1)S(1)}, u32[]{:S(2)}, u32[]{:S(2)}) collective-permute-start(bf16[4,48,1280]{2,1,0:T(8,128)(2,1)S(1)} %pad_maximum_fusion.1.refs_0_), channel_id=1, source_target_pairs={{0,3},{1,2},{2,1},{3,0},{4,7},{5,6},{6,5},{7,4},{8,11},{9,10},{10,... | collective-permute-start | bytes 1474568 | tf_op jit(solution)/shard_map/ppermute | solution.py:65
  26.4 21.8 %collective-permute-start.4 = (bf16[4,48,1280]{2,1,0:T(8,128)(2,1)S(1)}, bf16[4,48,1280]{2,1,0:T(8,128)(2,1)S(1)}, u32[]{:S(2)}, u32[]{:S(2)}) collective-permute-start(bf16[4,48,1280]{2,1,0:T(8,128)(2,1)S(1)} %pad_maximum_fusion.1.refs_0_), channel_id=1, source_target_pairs={{0,2},{1,3},{2,0},{3,1},{4,6},{5,7},{6,4},{7,5},{8,10},{9,11},{10,... | collective-permute-start | bytes 1474568 | tf_op jit(solution)/shard_map/ppermute | solution.py:65
  26.9 21.4 %collective-permute-start.3 = (bf16[4,48,1280]{2,1,0:T(8,128)(2,1)S(1)}, bf16[4,48,1280]{2,1,0:T(8,128)(2,1)S(1)}, u32[]{:S(2)}, u32[]{:S(2)}) collective-permute-start(bf16[4,48,1280]{2,1,0:T(8,128)(2,1)S(1)} %pad_maximum_fusion.1.refs_0_), channel_id=1, source_target_pairs={{0,1},{1,0},{2,3},{3,2},{4,5},{5,4},{6,7},{7,6},{8,9},{9,8},{10,11... | collective-permute-start | bytes 1474568 | tf_op jit(solution)/shard_map/ppermute | solution.py:65
  56.8 23.2 %collective-permute-start.8 = (bf16[4,48,1920]{2,1,0:T(8,128)(2,1)}, bf16[4,48,1920]{2,1,0:T(8,128)(2,1)}, u32[]{:S(2)}, u32[]{:S(2)}) collective-permute-start(bf16[4,48,1920]{2,1,0:T(8,128)(2,1)} %slice.178), channel_id=1, source_target_pairs={{0,1},{1,0},{2,3},{3,2},{4,5},{5,4},{6,7},{7,6},{8,9},{9,8},{10,11... | collective-permute-start | bytes 2211848 | tf_op jit(solution)/shard_map/ppermute | solution.py:65
  59.1 20.8 %collective-permute-start.9 = (bf16[4,48,1536]{2,1,0:T(8,128)(2,1)}, bf16[4,48,1536]{2,1,0:T(8,128)(2,1)}, u32[]{:S(2)}, u32[]{:S(2)}) collective-permute-start(bf16[4,48,1536]{2,1,0:T(8,128)(2,1)} %slice.179), channel_id=1, source_target_pairs={{0,2},{1,3},{2,0},{3,1},{4,6},{5,7},{6,4},{7,5},{8,10},{9,11},{10,... | collective-permute-start | bytes 1769480 | tf_op jit(solution)/shard_map/ppermute | solution.py:65
  61.2 39.8 %collective-permute-start.11 = (bf16[4,48,1920]{2,1,0:T(8,128)(2,1)}, bf16[4,48,1920]{2,1,0:T(8,128)(2,1)}, u32[]{:S(2)}, u32[]{:S(2)}) collective-permute-start(bf16[4,48,1920]{2,1,0:T(8,128)(2,1)} %slice.178), channel_id=1, source_target_pairs={{0,2},{1,3},{2,0},{3,1},{4,6},{5,7},{6,4},{7,5},{8,10},{9,11},{10,... | collective-permute-start | bytes 2211848 | tf_op jit(solution)/shard_map/ppermute | solution.py:65
  79.9 28.7 %collective-permute-start.12 = (bf16[4,48,1920]{2,1,0:T(8,128)(2,1)}, bf16[4,48,1920]{2,1,0:T(8,128)(2,1)S(1)}, u32[]{:S(2)}, u32[]{:S(2)}) collective-permute-start(bf16[4,48,1920]{2,1,0:T(8,128)(2,1)} %collective-permute-done.8.refs_2_), channel_id=1, source_target_pairs={{0,2},{1,3},{2,0},{3,1},{4,6},{5,7},{6,4},{7,5},{8,10},{9,11},{10,... | collective-permute-start | bytes 2211848 | tf_op jit(solution)/shard_map/ppermute | solution.py:65
  80.6 20.4 %collective-permute-start.13 = (bf16[4,48,1536]{2,1,0:T(8,128)(2,1)}, bf16[4,48,1536]{2,1,0:T(8,128)(2,1)}, u32[]{:S(2)}, u32[]{:S(2)}) collective-permute-start(bf16[4,48,1536]{2,1,0:T(8,128)(2,1)} %slice.179), channel_id=1, source_target_pairs={{0,1},{1,0},{2,3},{3,2},{4,5},{5,4},{6,7},{7,6},{8,9},{9,8},{10,11... | collective-permute-start | bytes 1769480 | tf_op jit(solution)/shard_map/ppermute | solution.py:65
  81.2 27.5 %collective-permute-start.14 = (bf16[4,48,1536]{2,1,0:T(8,128)(2,1)}, bf16[4,48,1536]{2,1,0:T(8,128)(2,1)S(1)}, u32[]{:S(2)}, u32[]{:S(2)}) collective-permute-start(bf16[4,48,1536]{2,1,0:T(8,128)(2,1)} %collective-permute-done.9.refs_10_), channel_id=1, source_target_pairs={{0,1},{1,0},{2,3},{3,2},{4,5},{5,4},{6,7},{7,6},{8,9},{9,8},{10,11... | collective-permute-start | bytes 1769480 | tf_op jit(solution)/shard_map/ppermute | solution.py:65
  109.5 76.2 %all-to-all-start.2 = ((bf16[16,128,768]{2,1,0:T(8,128)(2,1)}), bf16[16,128,768]{2,1,0:T(8,128)(2,1)}, u32[]{:S(2)}, u32[]{:S(2)}) async-start(bf16[16,128,768]{2,1,0:T(8,128)(2,1)} %bitcast.32), calls=%async_computation.2 | async-start | bytes 6291456 | tf_op jit(solution)/shard_map/all_to_all | solution.py:968
  115.1 14.8 %collective-permute-start.15 = (bf16[4,48,1920]{2,1,0:T(8,128)(2,1)}, bf16[4,48,1920]{2,1,0:T(8,128)(2,1)S(1)}, u32[]{:S(2)}, u32[]{:S(2)}) collective-permute-start(bf16[4,48,1920]{2,1,0:T(8,128)(2,1)} %collective-permute-done.8.refs_2_), channel_id=1, source_target_pairs={{0,16},{16,0},{1,17},{17,1},{2,18},{18,2},{3,19},{19,3},{4,20},{20... | collective-permute-start | bytes 2211848 | tf_op jit(solution)/shard_map/ppermute | solution.py:69
  115.1 14.8 %collective-permute-start.16 = (bf16[4,48,1920]{2,1,0:T(8,128)(2,1)}, bf16[4,48,1920]{2,1,0:T(8,128)(2,1)S(1)}, u32[]{:S(2)}, u32[]{:S(2)}) collective-permute-start(bf16[4,48,1920]{2,1,0:T(8,128)(2,1)} %collective-permute-done.11.refs_4_), channel_id=1, source_target_pairs={{0,16},{16,0},{1,17},{17,1},{2,18},{18,2},{3,19},{19,3},{4,20},{20... | collective-permute-start | bytes 2211848 | tf_op jit(solution)/shard_map/ppermute | solution.py:69
  115.6 14.3 %collective-permute-start.17 = (bf16[4,48,1920]{2,1,0:T(8,128)(2,1)S(1)}, bf16[4,48,1920]{2,1,0:T(8,128)(2,1)S(1)}, u32[]{:S(2)}, u32[]{:S(2)}) collective-permute-start(bf16[4,48,1920]{2,1,0:T(8,128)(2,1)S(1)} %collective-permute-done.12.refs_6_), channel_id=1, source_target_pairs={{0,16},{16,0},{1,17},{17,1},{2,18},{18,2},{3,19},{19,3},{4,20},{20... | collective-permute-start | bytes 2211848 | tf_op jit(solution)/shard_map/ppermute | solution.py:69
  185.6 87.6 %all-to-all-start.1 = ((bf16[16,128,768]{2,1,0:T(8,128)(2,1)}), bf16[16,128,768]{2,1,0:T(8,128)(2,1)S(1)}, u32[]{:S(2)}, u32[]{:S(2)}) async-start(bf16[16,128,768]{2,1,0:T(8,128)(2,1)} %bitcast.36), calls=%async_computation.1 | async-start | bytes 6291456 | tf_op jit(solution)/shard_map/all_to_all | solution.py:972
  291.5 55.8 %collective-permute-start.24 = (bf16[4,48,3456]{2,1,0:T(8,128)(2,1)}, bf16[4,48,3456]{2,1,0:T(8,128)(2,1)S(1)}, u32[]{:S(2)}, u32[]{:S(2)}) collective-permute-start(bf16[4,48,3456]{2,1,0:T(8,128)(2,1)} %get-tuple-element.165), channel_id=1, source_target_pairs={{0,1},{1,0},{2,3},{3,2},{4,5},{5,4},{6,7},{7,6},{8,9},{9,8},{10,11... | collective-permute-start | bytes 3981320 | tf_op jit(solution)/shard_map/ppermute | solution.py:65
  293.5 58.5 %collective-permute-start.25 = (bf16[4,48,3456]{2,1,0:T(8,128)(2,1)}, bf16[4,48,3456]{2,1,0:T(8,128)(2,1)S(1)}, u32[]{:S(2)}, u32[]{:S(2)}) collective-permute-start(bf16[4,48,3456]{2,1,0:T(8,128)(2,1)} %get-tuple-element.166), channel_id=1, source_target_pairs={{0,2},{1,3},{2,0},{3,1},{4,6},{5,7},{6,4},{7,5},{8,10},{9,11},{10,... | collective-permute-start | bytes 3981320 | tf_op jit(solution)/shard_map/ppermute | solution.py:65
  295.0 57.0 %collective-permute-start.26 = (bf16[4,48,3456]{2,1,0:T(8,128)(2,1)}, bf16[4,48,3456]{2,1,0:T(8,128)(2,1)}, u32[]{:S(2)}, u32[]{:S(2)}) collective-permute-start(bf16[4,48,3456]{2,1,0:T(8,128)(2,1)} %get-tuple-element.167), channel_id=1, source_target_pairs={{0,3},{1,2},{2,1},{3,0},{4,7},{5,6},{6,5},{7,4},{8,11},{9,10},{10,... | collective-permute-start | bytes 3981320 | tf_op jit(solution)/shard_map/ppermute | solution.py:65
  347.2 18.3 %collective-permute-start.27 = (bf16[768,1152]{1,0:T(8,128)(2,1)}, bf16[768,1152]{1,0:T(8,128)(2,1)}, u32[]{:S(2)}, u32[]{:S(2)}) collective-permute-start(bf16[768,1152]{1,0:T(8,128)(2,1)} %grad_qkv_other.1), channel_id=1, source_target_pairs={{0,16},{16,0},{1,17},{17,1},{2,18},{18,2},{3,19},{19,3},{4,20},{20... | collective-permute-start | bytes 5308424 | tf_op jit(solution)/shard_map/ppermute | solution.py:69
  357.5 54.5 %all-to-all-start.3 = ((bf16[4,48,3456]{2,1,0:T(8,128)(2,1)}), bf16[4,48,3456]{2,1,0:T(8,128)(2,1)}, u32[]{:S(2)}, u32[]{:S(2)}) async-start(bf16[4,48,3456]{2,1,0:T(8,128)(2,1)} %sum_parts.1), calls=%async_computation.3 | async-start | bytes 2654208 | tf_op jit(solution)/shard_map/all_to_all | solution.py:764
  376.9 34.0 %collective-permute-start.28 = (bf16[4,48,1152]{2,1,0:T(8,128)(2,1)}, bf16[4,48,1152]{2,1,0:T(8,128)(2,1)}, u32[]{:S(2)}, u32[]{:S(2)}) collective-permute-start(bf16[4,48,1152]{2,1,0:T(8,128)(2,1)} %get-tuple-element.181), channel_id=1, source_target_pairs={{0,1},{1,0},{2,3},{3,2},{4,5},{5,4},{6,7},{7,6},{8,9},{9,8},{10,11... | collective-permute-start | bytes 1327112 | tf_op jit(solution)/shard_map/ppermute | solution.py:65
  390.2 21.8 %collective-permute-start.29 = (bf16[4,48,1152]{2,1,0:T(8,128)(2,1)}, bf16[4,48,1152]{2,1,0:T(8,128)(2,1)}, u32[]{:S(2)}, u32[]{:S(2)}) collective-permute-start(bf16[4,48,1152]{2,1,0:T(8,128)(2,1)} %get-tuple-element.182), channel_id=1, source_target_pairs={{0,2},{1,3},{2,0},{3,1},{4,6},{5,7},{6,4},{7,5},{8,10},{9,11},{10,... | collective-permute-start | bytes 1327112 | tf_op jit(solution)/shard_map/ppermute | solution.py:65
  390.3 21.7 %collective-permute-start.30 = (bf16[4,48,1152]{2,1,0:T(8,128)(2,1)}, bf16[4,48,1152]{2,1,0:T(8,128)(2,1)}, u32[]{:S(2)}, u32[]{:S(2)}) collective-permute-start(bf16[4,48,1152]{2,1,0:T(8,128)(2,1)} %get-tuple-element.183), channel_id=1, source_target_pairs={{0,3},{1,2},{2,1},{3,0},{4,7},{5,6},{6,5},{7,4},{8,11},{9,10},{10,... | collective-permute-start | bytes 1327112 | tf_op jit(solution)/shard_map/ppermute | solution.py:65
  425.0 12.6 %collective-permute-start.35 = (bf16[48,1280]{1,0:T(8,128)(2,1)}, bf16[48,1280]{1,0:T(8,128)(2,1)S(1)}, u32[]{:S(2)}, u32[]{:S(2)}) collective-permute-start(bf16[48,1280]{1,0:T(8,128)(2,1)} %get-tuple-element.206), channel_id=1, source_target_pairs={{0,8},{1,9},{2,10},{3,11},{4,12},{5,13},{6,14},{7,15},{8,0},{9,1},... | collective-permute-start | bytes 368648 | tf_op jit(solution)/shard_map/ppermute | solution.py:65
  (43 other events, 329.5 us)
